TPU v7x, 32 devices: a whole 2x2x4 slice. The times are simulated.
32 devices in a mesh: dp: 8 (over y, x, core), own: 4 (over z).
Axes of the slice: x: 2, y: 2, z: 4, core: 2. Of those that a mesh axis runs over, the one named last changes fastest.
Arguments:
- hidden: bfloat16 [8192, 2560], P(('dp', 'own')), may hold values from -6 to 6
- cotangent: bfloat16 [8192, 2560], P(('dp', 'own')), may hold values from -6 to 6
- block_index: int32 [8, 1024], P('dp'), may hold values from 0 to 5, never falling along the last dimension, each value on 1 to 256 neighbouring positions
- owners: int32 [9], replicated, may hold values from 0 to 3
- query_down: float32 [4, 2560, 768], P('own', 'dp'), may hold values from -0.125 to 0.125
- query_down_first: float32 [4, 2560, 768], P('own', 'dp'), may hold values from -1792 to 1792
- query_down_second: float32 [4, 2560, 768], P('own', 'dp'), may hold values from 81920 to 327680
- query_up: float32 [4, 768, 3840], P('own', 'dp'), may hold values from -0.21875 to 0.21875
- query_up_first: float32 [4, 768, 3840], P('own', 'dp'), may hold values from -896 to 896
- query_up_second: float32 [4, 768, 3840], P('own', 'dp'), may hold values from 21299.2 to 81920
- latent_down: float32 [4, 2560, 288], P('own', 'dp'), may hold values from -0.125 to 0.125
- latent_down_first: float32 [4, 2560, 288], P('own', 'dp'), may hold values from -3584 to 3584
- latent_down_second: float32 [4, 2560, 288], P('own', 'dp'), may hold values from 327680 to 1310720
- latent_up: float32 [4, 256, 5120], P('own', 'dp'), may hold values from -0.375 to 0.375
- latent_up_first: float32 [4, 256, 5120], P('own', 'dp'), may hold values from -896 to 896
- latent_up_second: float32 [4, 256, 5120], P('own', 'dp'), may hold values from 21299.2 to 81920
- output_weight: float32 [4, 2560, 2560], P('own', 'dp'), may hold values from -15.094638 to 15.094638
- output_weight_first: float32 [4, 2560, 2560], P('own', 'dp'), may hold values from -7 to 7
- output_weight_second: float32 [4, 2560, 2560], P('own', 'dp'), may hold values from 1.28 to 5.12
- gate_weight: float32 [4, 2560, 6400], P('own', 'dp'), may hold values from -0.125 to 0.125
- gate_weight_first: float32 [4, 2560, 6400], P('own', 'dp'), may hold values from -512 to 512
- gate_weight_second: float32 [4, 2560, 6400], P('own', 'dp'), may hold values from 5734.4 to 22937.6
- up_weight: float32 [4, 2560, 6400], P('own', 'dp'), may hold values from -0.125 to 0.125
- up_weight_first: float32 [4, 2560, 6400], P('own', 'dp'), may hold values from -512 to 512
- up_weight_second: float32 [4, 2560, 6400], P('own', 'dp'), may hold values from 6553.6 to 26214.4
- down_weight: float32 [4, 6400, 2560], P('own', 'dp'), may hold values from -0.70243937 to 0.70243937
- down_weight_first: float32 [4, 6400, 2560], P('own', 'dp'), may hold values from -56 to 56
- down_weight_second: float32 [4, 6400, 2560], P('own', 'dp'), may hold values from 81.92 to 327.68
- norm_gains: float32 [4, 6144], P('own', 'dp'), may hold values from 0.5 to 1.5
- norm_gains_first: float32 [4, 6144], P('own', 'dp'), may hold values from -2048 to 2048
- norm_gains_second: float32 [4, 6144], P('own', 'dp'), may hold values from 131072 to 524288
Outputs:
- block_output: bfloat16 [8192, 2560], P(('dp', 'own'))
- input_grad: bfloat16 [8192, 2560], P(('dp', 'own'))
- new_query_down: float32 [4, 2560, 768], P('own', 'dp')
- new_query_down_first: float32 [4, 2560, 768], P('own', 'dp')
- new_query_down_second: float32 [4, 2560, 768], P('own', 'dp')
- new_query_up: float32 [4, 768, 3840], P('own', 'dp')
- new_query_up_first: float32 [4, 768, 3840], P('own', 'dp')
- new_query_up_second: float32 [4, 768, 3840], P('own', 'dp')
- new_latent_down: float32 [4, 2560, 288], P('own', 'dp')
- new_latent_down_first: float32 [4, 2560, 288], P('own', 'dp')
- new_latent_down_second: float32 [4, 2560, 288], P('own', 'dp')
- new_latent_up: float32 [4, 256, 5120], P('own', 'dp')
- new_latent_up_first: float32 [4, 256, 5120], P('own', 'dp')
- new_latent_up_second: float32 [4, 256, 5120], P('own', 'dp')
- new_output_weight: float32 [4, 2560, 2560], P('own', 'dp')
- new_output_weight_first: float32 [4, 2560, 2560], P('own', 'dp')
- new_output_weight_second: float32 [4, 2560, 2560], P('own', 'dp')
- new_gate_weight: float32 [4, 2560, 6400], P('own', 'dp')
- new_gate_weight_first: float32 [4, 2560, 6400], P('own', 'dp')
- new_gate_weight_second: float32 [4, 2560, 6400], P('own', 'dp')
- new_up_weight: float32 [4, 2560, 6400], P('own', 'dp')
- new_up_weight_first: float32 [4, 2560, 6400], P('own', 'dp')
- new_up_weight_second: float32 [4, 2560, 6400], P('own', 'dp')
- new_down_weight: float32 [4, 6400, 2560], P('own', 'dp')
- new_down_weight_first: float32 [4, 6400, 2560], P('own', 'dp')
- new_down_weight_second: float32 [4, 6400, 2560], P('own', 'dp')
- new_norm_gains: float32 [4, 6144], P('own', 'dp')
- new_norm_gains_first: float32 [4, 6144], P('own', 'dp')
- new_norm_gains_second: float32 [4, 6144], P('own', 'dp')
Inputs may be any that keep to these rules, and one draw needn't show every extreme that they name: `block_index`: along each sequence the block numbers never fall; each block holds 1 to 256 positions and one holds exactly 256.
All inputs are finite; a program needn't handle non-finite values.
Results may differ from a plain program's by a relative error of at most 0.022.
Values may be sent and summed in bfloat16 or wider, within the bound.
No kernel may reach another device: no remote copies, remote signals or barrier semaphores. Data moves between devices by JAX's collectives and lax.ppermute only.
A program may use at most 576 MiB of HBM per device.

v0:
```python
import math

import jax
import jax.numpy as jnp
from jax import lax
from jax.sharding import PartitionSpec as P

D = 2560
H = 40
NOPE = 64
ROPE = 32
VD = 64
QR = 768
KVR = 256
FF = 6400
HEAD_GROUP = 4
STEP = 7


EPSILON = 1e-05
RESIDUAL_SCALE = 1.4 / math.sqrt(62.0)
BETA_ONE = 0.5
BETA_TWO = 0.55
WEIGHT_DECAY = 0.1
ADAM_EPS = 1e-08
HIGHEST = lax.Precision.HIGHEST


def spread(value, axis, source):
    kept = jnp.where(lax.axis_index(axis) == source, value, 0).astype(value.dtype)
    return lax.psum(kept, axis)


def rms_forward(values, norm_gain):
    inverse = lax.rsqrt(jnp.mean(values * values, axis=-1, keepdims=True) + EPSILON)
    return (values * inverse * norm_gain, inverse)


def rms_backward(values, inverse, norm_gain, grad_normed):
    normed = values * inverse
    grad_gain = jnp.sum(grad_normed * normed, axis=0)
    scaled = grad_normed * norm_gain
    grad_values = inverse * (scaled - normed * jnp.mean(scaled * normed, axis=-1, keepdims=True))
    return (grad_values, grad_gain)


def rotary_tables(positions):
    half_width = ROPE // 2
    frequency = 10000.0 ** (-jnp.arange(half_width, dtype=jnp.float32) / half_width)
    angles = positions.astype(jnp.float32)[:, None] * frequency[None, :]
    return (jnp.cos(angles), jnp.sin(angles))


def rotate(values, cosine, sine_table):
    half_width = values.shape[-1] // 2
    former = values[..., :half_width]
    latter = values[..., half_width:]
    return jnp.concatenate(
        [former * cosine - latter * sine_table, latter * cosine + former * sine_table], axis=-1
    )


def unrotate(gradient, cosine, sine_table):
    half_width = gradient.shape[-1] // 2
    former = gradient[..., :half_width]
    latter = gradient[..., half_width:]
    return jnp.concatenate(
        [former * cosine + latter * sine_table, latter * cosine - former * sine_table], axis=-1
    )


def contract_rows(first_matrix, second_matrix):
    return lax.dot_general(
        first_matrix, second_matrix, (((0,), (0,)), ((), ())), preferred_element_type=jnp.float32
    )


def times_transpose(first_matrix, second_matrix):
    return lax.dot_general(
        first_matrix, second_matrix, (((1,), (1,)), ((), ())), preferred_element_type=jnp.float32
    )


def exact_rows(first_matrix, second_matrix):
    return lax.dot_general(
        first_matrix,
        second_matrix,
        (((0,), (0,)), ((), ())),
        precision=HIGHEST,
        preferred_element_type=jnp.float32,
    )


def exact_transpose(first_matrix, second_matrix):
    return lax.dot_general(
        first_matrix,
        second_matrix,
        (((1,), (1,)), ((), ())),
        precision=HIGHEST,
        preferred_element_type=jnp.float32,
    )


def reduce_term(gradient_term):
    wide_part = lax.psum_scatter(
        gradient_term.astype(jnp.bfloat16), "dp", scatter_dimension=0, tiled=True
    )
    reduced_rows = lax.psum(wide_part, "own").astype(jnp.float32)
    return reduced_rows


def adamw_update(master, first_moment, second_moment, gradient, learn_rate, weight_decay, is_owner):
    new_first = BETA_ONE * first_moment + (1.0 - BETA_ONE) * gradient
    new_second = BETA_TWO * second_moment + (1.0 - BETA_TWO) * gradient * gradient
    mean_hat = new_first / (1.0 - BETA_ONE**STEP)
    square_hat = new_second / (1.0 - BETA_TWO**STEP)
    new_master = master - learn_rate * (
        mean_hat / (jnp.sqrt(square_hat) + ADAM_EPS) + weight_decay * master
    )
    return (
        jnp.where(is_owner, new_master, master),
        jnp.where(is_owner, new_first, first_moment),
        jnp.where(is_owner, new_second, second_moment),
    )


def shards(
    hidden,
    cotangent,
    block_index,
    owners,
    query_down,
    query_down_first,
    query_down_second,
    query_up,
    query_up_first,
    query_up_second,
    latent_down,
    latent_down_first,
    latent_down_second,
    latent_up,
    latent_up_first,
    latent_up_second,
    output_weight,
    output_weight_first,
    output_weight_second,
    gate_weight,
    gate_weight_first,
    gate_weight_second,
    up_weight,
    up_weight_first,
    up_weight_second,
    down_weight,
    down_weight_first,
    down_weight_second,
    norm_gains,
    norm_gains_first,
    norm_gains_second,
):
    own_count = lax.axis_size("own")
    own_place = lax.axis_index("own")
    tokens_here = hidden.shape[0]
    sequence_length = tokens_here * own_count
    masters = (
        query_down,
        query_up,
        latent_down,
        latent_up,
        output_weight,
        gate_weight,
        up_weight,
        down_weight,
        norm_gains,
    )
    copies = []
    for tensor_slot in range(9):
        copies.append(
            spread(masters[tensor_slot][0].astype(jnp.bfloat16), "own", owners[tensor_slot])
        )
    (
        query_down_all,
        query_up_all,
        latent_down_all,
        latent_up_all,
        output_all,
        gate_all,
        up_all,
        down_all,
        gains_all,
    ) = (
        lax.all_gather(copies[0], "dp", axis=0, tiled=True),
        lax.all_gather(copies[1], "dp", axis=0, tiled=True),
        lax.all_gather(copies[2], "dp", axis=0, tiled=True),
        lax.all_gather(copies[3], "dp", axis=0, tiled=True),
        lax.all_gather(copies[4], "dp", axis=0, tiled=True),
        lax.all_gather(copies[5], "dp", axis=0, tiled=True),
        lax.all_gather(copies[6], "dp", axis=0, tiled=True),
        lax.all_gather(copies[7], "dp", axis=0, tiled=True),
        lax.all_gather(copies[8], "dp", axis=0, tiled=True),
    )
    gains_float = gains_all.astype(jnp.float32)
    gain_input = gains_float[:D]
    gain_query = gains_float[D : D + QR]
    gain_latent = gains_float[D + QR : D + QR + KVR]
    gain_ffn = gains_float[D + QR + KVR :]
    inputs = hidden.astype(jnp.float32)
    normed, inverse_input = rms_forward(inputs, gain_input)
    normed_low = normed.astype(jnp.bfloat16)
    query_latent = jnp.dot(normed_low, query_down_all, preferred_element_type=jnp.float32)
    query_normed, inverse_query = rms_forward(query_latent, gain_query)
    query_low = query_normed.astype(jnp.bfloat16)
    query_raw = jnp.dot(query_low, query_up_all, preferred_element_type=jnp.float32).reshape(
        tokens_here, H, NOPE + ROPE
    )
    positions = own_place * tokens_here + jnp.arange(tokens_here, dtype=jnp.int32)
    cosine, sine_table = rotary_tables(positions)
    queries = jnp.concatenate(
        [
            query_raw[..., :NOPE],
            rotate(query_raw[..., NOPE:], cosine[:, None], sine_table[:, None]),
        ],
        axis=-1,
    ).astype(jnp.bfloat16)
    key_latent = jnp.dot(normed_low, latent_down_all, preferred_element_type=jnp.float32)
    key_normed, inverse_key = rms_forward(key_latent[:, :KVR], gain_latent)
    key_low = key_normed.astype(jnp.bfloat16)
    rope_low = rotate(key_latent[:, KVR:], cosine, sine_table).astype(jnp.bfloat16)
    gathered_latent, rope_keys = (
        lax.all_gather(key_low, "own", axis=0, tiled=True),
        lax.all_gather(rope_low, "own", axis=0, tiled=True),
    )
    key_value = jnp.dot(gathered_latent, latent_up_all, preferred_element_type=jnp.float32).astype(
        jnp.bfloat16
    )
    key_value = key_value.reshape(sequence_length, H, NOPE + VD)
    sequence_blocks = block_index[0]
    query_blocks = lax.dynamic_slice_in_dim(
        sequence_blocks, own_place * tokens_here, tokens_here, 0
    )
    allowed = sequence_blocks[None, :] <= query_blocks[:, None]
    softmax_scale = (NOPE + ROPE) ** (-0.5)
    rounds = H // HEAD_GROUP

    def scores_for(head_start):
        query_part = lax.dynamic_slice_in_dim(queries, head_start, HEAD_GROUP, 1)
        key_part = lax.dynamic_slice_in_dim(key_value, head_start, HEAD_GROUP, 1)
        scores = jnp.einsum(
            "qhd,khd->hqk",
            query_part[..., :NOPE],
            key_part[..., :NOPE],
            preferred_element_type=jnp.float32,
        )
        scores = scores + jnp.einsum(
            "qhd,kd->hqk", query_part[..., NOPE:], rope_keys, preferred_element_type=jnp.float32
        )
        return (query_part, key_part, scores * softmax_scale)

    def forward_heads(head_round, loop_state):
        attended, logsum = loop_state
        head_start = head_round * HEAD_GROUP
        query_part, key_part, scores = scores_for(head_start)
        scores = jnp.where(allowed[None], scores, -1e30)
        row_peak = jnp.max(scores, axis=-1, keepdims=True)
        exponent = jnp.exp(scores - row_peak)
        totals = jnp.sum(exponent, axis=-1, keepdims=True)
        weights_low = (exponent / totals).astype(jnp.bfloat16)
        part_out = jnp.einsum(
            "hqk,khd->qhd", weights_low, key_part[..., NOPE:], preferred_element_type=jnp.float32
        )
        attended = lax.dynamic_update_slice_in_dim(attended, part_out, head_start, 1)
        logsum = lax.dynamic_update_slice_in_dim(
            logsum, (row_peak + jnp.log(totals))[..., 0], head_start, 0
        )
        return (attended, logsum)

    attended, logsum = lax.fori_loop(
        0,
        rounds,
        forward_heads,
        (jnp.zeros((tokens_here, H, VD), jnp.float32), jnp.zeros((H, tokens_here), jnp.float32)),
    )
    attended_low = attended.reshape(tokens_here, H * VD).astype(jnp.bfloat16)
    branch = jnp.dot(attended_low, output_all, preferred_element_type=jnp.float32)
    middle = inputs + RESIDUAL_SCALE * branch
    normed_ffn, inverse_ffn = rms_forward(middle, gain_ffn)
    normed_ffn_low = normed_ffn.astype(jnp.bfloat16)
    gate_pre = jnp.dot(normed_ffn_low, gate_all, preferred_element_type=jnp.float32)
    up_pre = jnp.dot(normed_ffn_low, up_all, preferred_element_type=jnp.float32)
    sigmoid_gate = jax.nn.sigmoid(gate_pre)
    silu_gate = gate_pre * sigmoid_gate
    activated_low = (silu_gate * up_pre).astype(jnp.bfloat16)
    ffn_branch = jnp.dot(activated_low, down_all, preferred_element_type=jnp.float32)
    block_output = (middle + RESIDUAL_SCALE * ffn_branch).astype(jnp.bfloat16)
    grad_output = cotangent.astype(jnp.float32)
    grad_ffn = (RESIDUAL_SCALE * grad_output).astype(jnp.bfloat16)
    reduced_down = reduce_term(contract_rows(activated_low, grad_ffn))
    grad_activated = times_transpose(grad_ffn, down_all)
    grad_gate_pre = (
        grad_activated * up_pre * sigmoid_gate * (1.0 + gate_pre * (1.0 - sigmoid_gate))
    ).astype(jnp.bfloat16)
    grad_up_pre = (grad_activated * silu_gate).astype(jnp.bfloat16)
    reduced_gate = reduce_term(contract_rows(normed_ffn_low, grad_gate_pre))
    reduced_up = reduce_term(contract_rows(normed_ffn_low, grad_up_pre))
    grad_normed_ffn = times_transpose(grad_gate_pre, gate_all) + times_transpose(
        grad_up_pre, up_all
    )
    grad_middle_part, grad_gain_ffn = rms_backward(middle, inverse_ffn, gain_ffn, grad_normed_ffn)
    grad_middle = grad_output + grad_middle_part
    grad_branch = (RESIDUAL_SCALE * grad_middle).astype(jnp.bfloat16)
    reduced_output = reduce_term(contract_rows(attended_low, grad_branch))
    grad_attended = (
        times_transpose(grad_branch, output_all).astype(jnp.bfloat16).reshape(tokens_here, H, VD)
    )

    def head_backward(head_start):
        query_part, key_part, scores = scores_for(head_start)
        heads_logsum = lax.dynamic_slice_in_dim(logsum, head_start, HEAD_GROUP, 0)
        weights_full = jnp.where(allowed[None], jnp.exp(scores - heads_logsum[..., None]), 0.0)
        grad_part = lax.dynamic_slice_in_dim(grad_attended, head_start, HEAD_GROUP, 1)
        grad_value = jnp.einsum(
            "hqk,qhd->khd",
            weights_full.astype(jnp.bfloat16),
            grad_part,
            preferred_element_type=jnp.float32,
        )
        grad_weights = jnp.einsum(
            "qhd,khd->hqk", grad_part, key_part[..., NOPE:], preferred_element_type=jnp.float32
        )
        row_inner = jnp.sum(weights_full * grad_weights, axis=-1, keepdims=True)
        grad_scores = (weights_full * (grad_weights - row_inner)).astype(jnp.bfloat16)
        query_nope = jnp.einsum(
            "hqk,khd->qhd", grad_scores, key_part[..., :NOPE], preferred_element_type=jnp.float32
        )
        query_rope = jnp.einsum(
            "hqk,kd->qhd", grad_scores, rope_keys, preferred_element_type=jnp.float32
        )
        key_nope = jnp.einsum(
            "hqk,qhd->khd", grad_scores, query_part[..., :NOPE], preferred_element_type=jnp.float32
        )
        key_rope = jnp.einsum(
            "hqk,qhd->kd", grad_scores, query_part[..., NOPE:], preferred_element_type=jnp.float32
        )
        partial_key = jnp.concatenate([key_nope * softmax_scale, grad_value], axis=-1).reshape(
            sequence_length, HEAD_GROUP * (NOPE + VD)
        )
        query_grad = jnp.concatenate([query_nope, query_rope], axis=-1) * softmax_scale
        return (query_grad, partial_key, key_rope * softmax_scale)

    up_float = latent_up_all.astype(jnp.float32)

    def backward_split(head_round, loop_state):
        grad_query, grad_key, grad_rope = loop_state
        head_start = head_round * HEAD_GROUP
        query_grad, partial_key, rope_part = head_backward(head_start)
        summed_key, summed_rope = (
            lax.psum_scatter(
                partial_key.astype(jnp.bfloat16), "own", scatter_dimension=0, tiled=True
            ).astype(jnp.float32),
            lax.psum_scatter(
                rope_part.astype(jnp.bfloat16), "own", scatter_dimension=0, tiled=True
            ).astype(jnp.float32),
        )
        grad_query = lax.dynamic_update_slice_in_dim(grad_query, query_grad, head_start, 1)
        grad_key = lax.dynamic_update_slice_in_dim(
            grad_key, summed_key, head_start * (NOPE + VD), 1
        )
        return (grad_query, grad_key, grad_rope + summed_rope)

    grad_query, grad_key, grad_rope = lax.fori_loop(
        0,
        rounds,
        backward_split,
        (
            jnp.zeros((tokens_here, H, NOPE + ROPE), jnp.float32),
            jnp.zeros((tokens_here, H * (NOPE + VD)), jnp.float32),
            jnp.zeros((tokens_here, ROPE), jnp.float32),
        ),
    )
    grad_latent_up = exact_rows(key_low.astype(jnp.float32), grad_key)
    grad_key_normed = exact_transpose(grad_key, up_float)
    reduced_latent_up = reduce_term(grad_latent_up)
    grad_key_latent, grad_gain_latent = rms_backward(
        key_latent[:, :KVR], inverse_key, gain_latent, grad_key_normed
    )
    grad_key_down = jnp.concatenate(
        [grad_key_latent, unrotate(grad_rope, cosine, sine_table)], axis=-1
    ).astype(jnp.bfloat16)
    reduced_latent_down = reduce_term(contract_rows(normed_low, grad_key_down))
    grad_normed = times_transpose(grad_key_down, latent_down_all)
    grad_query_raw = jnp.concatenate(
        [
            grad_query[..., :NOPE],
            unrotate(grad_query[..., NOPE:], cosine[:, None], sine_table[:, None]),
        ],
        axis=-1,
    )
    grad_query_raw = grad_query_raw.reshape(tokens_here, H * (NOPE + ROPE)).astype(jnp.bfloat16)
    reduced_query_up = reduce_term(contract_rows(query_low, grad_query_raw))
    grad_query_normed = times_transpose(grad_query_raw, query_up_all)
    grad_query_latent, grad_gain_query = rms_backward(
        query_latent, inverse_query, gain_query, grad_query_normed
    )
    grad_query_low = grad_query_latent.astype(jnp.bfloat16)
    reduced_query_down = reduce_term(contract_rows(normed_low, grad_query_low))
    grad_normed = grad_normed + times_transpose(grad_query_low, query_down_all)
    grad_inputs, grad_gain_input = rms_backward(inputs, inverse_input, gain_input, grad_normed)
    input_grad = (grad_middle + grad_inputs).astype(jnp.bfloat16)
    reduced_gains = reduce_term(
        jnp.concatenate([grad_gain_input, grad_gain_query, grad_gain_latent, grad_gain_ffn])
    )
    reduced = (
        reduced_query_down,
        reduced_query_up,
        reduced_latent_down,
        reduced_latent_up,
        reduced_output,
        reduced_gate,
        reduced_up,
        reduced_down,
        reduced_gains,
    )
    states = (
        (query_down, query_down_first, query_down_second),
        (query_up, query_up_first, query_up_second),
        (latent_down, latent_down_first, latent_down_second),
        (latent_up, latent_up_first, latent_up_second),
        (output_weight, output_weight_first, output_weight_second),
        (gate_weight, gate_weight_first, gate_weight_second),
        (up_weight, up_weight_first, up_weight_second),
        (down_weight, down_weight_first, down_weight_second),
        (norm_gains, norm_gains_first, norm_gains_second),
    )
    learn_rates = (
        D ** (-0.5),
        QR ** (-0.5),
        D ** (-0.5),
        KVR ** (-0.5),
        math.sqrt(sequence_length / (0.0632 * H * VD)),
        D ** (-0.5),
        D ** (-0.5),
        math.sqrt(1.0 / (0.0114 * FF)),
        0.6,
    )
    decays = (
        WEIGHT_DECAY,
        WEIGHT_DECAY,
        WEIGHT_DECAY,
        WEIGHT_DECAY,
        WEIGHT_DECAY,
        WEIGHT_DECAY,
        WEIGHT_DECAY,
        WEIGHT_DECAY,
        0.0,
    )
    results = [block_output, input_grad]
    for tensor_slot in range(9):
        master, first_moment, second_moment = states[tensor_slot]
        is_owner = own_place == owners[tensor_slot]
        updated = adamw_update(
            master[0],
            first_moment[0],
            second_moment[0],
            reduced[tensor_slot],
            learn_rates[tensor_slot],
            decays[tensor_slot],
            is_owner,
        )
        results.extend((member[None] for member in updated))
    return tuple(results)


def solution(mesh):
    return jax.shard_map(
        shards,
        mesh=mesh,
        in_specs=(
            P(("dp", "own"), None),
            P(("dp", "own"), None),
            P("dp", None),
            P(),
            P("own", "dp", None),
            P("own", "dp", None),
            P("own", "dp", None),
            P("own", "dp", None),
            P("own", "dp", None),
            P("own", "dp", None),
            P("own", "dp", None),
            P("own", "dp", None),
            P("own", "dp", None),
            P("own", "dp", None),
            P("own", "dp", None),
            P("own", "dp", None),
            P("own", "dp", None),
            P("own", "dp", None),
            P("own", "dp", None),
            P("own", "dp", None),
            P("own", "dp", None),
            P("own", "dp", None),
            P("own", "dp", None),
            P("own", "dp", None),
            P("own", "dp", None),
            P("own", "dp", None),
            P("own", "dp", None),
            P("own", "dp", None),
            P("own", "dp"),
            P("own", "dp"),
            P("own", "dp"),
        ),
        out_specs=(
            P(("dp", "own"), None),
            P(("dp", "own"), None),
            P("own", "dp", None),
            P("own", "dp", None),
            P("own", "dp", None),
            P("own", "dp", None),
            P("own", "dp", None),
            P("own", "dp", None),
            P("own", "dp", None),
            P("own", "dp", None),
            P("own", "dp", None),
            P("own", "dp", None),
            P("own", "dp", None),
            P("own", "dp", None),
            P("own", "dp", None),
            P("own", "dp", None),
            P("own", "dp", None),
            P("own", "dp", None),
            P("own", "dp", None),
            P("own", "dp", None),
            P("own", "dp", None),
            P("own", "dp", None),
            P("own", "dp", None),
            P("own", "dp", None),
            P("own", "dp", None),
            P("own", "dp", None),
            P("own", "dp"),
            P("own", "dp"),
            P("own", "dp"),
        ),
        check_vma=False,
    )
```

profile of v0, /device:TPU:0, one launch (start us, length us, event | category | flops | bytes accessed | tf_op | source)
XLA Modules:
  0.0 3479.9 jit_solution(2019100913301515250)
XLA Ops:
  35.0 534.5 %all-reduce.8.cloned.1.call-done = (bf16[320,288]{0,1:T(8,128)(2,1)}, bf16[32,5120]{1,0:T(8,128)(2,1)}, bf16[96,3840]{1,0:T(8,128)(2,1)}, bf16[320,768]{1,0:T(8,...) async-done(((bf16[320,288]{0,1:T(8,128)(2,1)}, bf16[32,5120]{1,0:T(8,128)(2,1)}, ...) | async-done | bytes 15667216 | tf_op jit(solution)/shard_map/psum | solution.py:31
  669.5 42.2 %all-gather.15.cloned.1.call-done = bf16[768,3840]{1,0:T(8,128)(2,1)} async-done(((bf16[96,3840]{1,0:T(8,128)(2,1)}), bf16[768,3840]{1,0:T(8,128)(2,1)}) %all-gather.15.cloned.1.call-update) | async-done | bytes 5898256 | tf_op jit(solution)/shard_map/all_gather | solution.py:192
  719.0 110.0 %while.36 = (s32[]{:T(128)}, bf16[256,40,64]{0,2,1:T(8,128)(2,1)S(1)}, f32[40,256]{1,0:T(8,128)S(1)}, bf16[1024,40,128]{0,2,1:T(8,128)(2,1)}, bf16[256,40,96]{0,...) while((s32[]{:T(128)}, ...), condition=%wide.region_11.12_spmd.clone, body=%wide.region_8.11_spmd.clone.sunk | while | flops 345242624 | bytes 23109316 | solution.py:276
  840.9 106.3 %all-gather.21.cloned.1.call-done = bf16[2560,6400]{1,0:T(8,128)(2,1)} async-done(((bf16[320,6400]{1,0:T(8,128)(2,1)}), bf16[2560,6400]{1,0:T(8,128)(2,1)}) %all-gather.21.cloned.1.call-update) | async-done | bytes 32768016 | tf_op jit(solution)/shard_map/all_gather | solution.py:197
  947.2 19.9 fusion.191
  967.1 139.5 %all-gather.19.cloned.1.call-done = bf16[2560,6400]{1,0:T(8,128)(2,1)} async-done(((bf16[320,6400]{1,0:T(8,128)(2,1)}), bf16[2560,6400]{1,0:T(8,128)(2,1)}) %all-gather.19.cloned.1.call-update) | async-done | bytes 32768016 | tf_op jit(solution)/shard_map/all_gather | solution.py:196
  1106.6 19.9 fusion.190
  1126.5 139.5 %all-gather.23.cloned.1.call-done = bf16[6400,2560]{1,0:T(8,128)(2,1)} async-done(((bf16[800,2560]{1,0:T(8,128)(2,1)}), bf16[6400,2560]{1,0:T(8,128)(2,1)}) %all-gather.23.cloned.1.call-update) | async-done | bytes 32768016 | tf_op jit(solution)/shard_map/all_gather | solution.py:198
  1266.0 21.4 multiply_convert_fusion.1
  1304.3 18.7 multiply_reduce_fusion.1
  1342.4 586.8 %while.37 = (s32[]{:T(128)}, f32[256,40,96]{0,2,1:T(8,128)}, f32[256,5120]{0,1:T(8,128)}, f32[256,32]{0,1:T(8,128)S(1)}, bf16[1024,40,128]{0,2,1:T(8,128)(2,1)},...) while((s32[]{:T(128)}, f32[256,40,96]{0,2,1:T(8,128)}, ...), condition=%wide.region_22.23_spmd.clone, body=%wide.region_18.22_spmd.clone.sunk | while | flops 886463488 | bytes 73166752 | solution.py:369
  1373.1 27.6 reduce-scatter.29.cloned.1.call-done
  1431.7 27.6 reduce-scatter.29.cloned.1.call-done
  1490.3 27.4 reduce-scatter.29.cloned.1.call-done
  1548.8 27.4 reduce-scatter.29.cloned.1.call-done
  1607.2 27.5 reduce-scatter.29.cloned.1.call-done
  1665.8 27.5 reduce-scatter.29.cloned.1.call-done
  1724.3 27.5 reduce-scatter.29.cloned.1.call-done
  1782.9 27.6 reduce-scatter.29.cloned.1.call-done
  1841.5 27.4 reduce-scatter.29.cloned.1.call-done
  1899.9 27.6 reduce-scatter.29.cloned.1.call-done
  2025.9 54.6 %reduce-scatter.13.cloned.1.call-done = bf16[320,768]{1,0:T(8,128)(2,1)} async-done(((bf16[2560,768]{1,0:T(8,128)(2,1)}), bf16[320,768]{1,0:T(8,128)(2,1)}) %reduce-scatter.13.cloned.1.call-update) | async-done | bytes 491536 | tf_op jit(solution)/shard_map/reduce_scatter | solution.py:105
  2080.5 63.6 %reduce-scatter.15.cloned.1.call-done = bf16[96,3840]{1,0:T(8,128)(2,1)} async-done(((bf16[768,3840]{1,0:T(8,128)(2,1)}), bf16[96,3840]{1,0:T(8,128)(2,1)}) %reduce-scatter.15.cloned.1.call-update) | async-done | bytes 737296 | tf_op jit(solution)/shard_map/reduce_scatter | solution.py:105
  2144.1 98.8 %reduce-scatter.19.cloned.1.call-done = bf16[320,2560]{1,0:T(8,128)(2,1)} async-done(((bf16[2560,2560]{1,0:T(8,128)(2,1)}), bf16[320,2560]{1,0:T(8,128)(2,1)}) %reduce-scatter.19.cloned.1.call-update) | async-done | bytes 1638416 | tf_op jit(solution)/shard_map/reduce_scatter | solution.py:105
  2242.9 205.5 %reduce-scatter.21.cloned.1.call-done = bf16[320,6400]{1,0:T(8,128)(2,1)} async-done(((bf16[2560,6400]{1,0:T(8,128)(2,1)}), bf16[320,6400]{1,0:T(8,128)(2,1)}) %reduce-scatter.21.cloned.1.call-update) | async-done | bytes 4096016 | tf_op jit(solution)/shard_map/reduce_scatter | solution.py:105
  2448.4 205.4 %reduce-scatter.23.cloned.1.call-done = bf16[320,6400]{1,0:T(8,128)(2,1)} async-done(((bf16[2560,6400]{1,0:T(8,128)(2,1)}), bf16[320,6400]{1,0:T(8,128)(2,1)}) %reduce-scatter.23.cloned.1.call-update) | async-done | bytes 4096016 | tf_op jit(solution)/shard_map/reduce_scatter | solution.py:105
  2653.8 205.3 %reduce-scatter.25.cloned.1.call-done = bf16[800,2560]{1,0:T(8,128)(2,1)} async-done(((bf16[6400,2560]{1,0:T(8,128)(2,1)}), bf16[800,2560]{1,0:T(8,128)(2,1)}) %reduce-scatter.25.cloned.1.call-update) | async-done | bytes 4096016 | tf_op jit(solution)/shard_map/reduce_scatter | solution.py:105
  2867.4 24.3 all-reduce
  2929.4 465.8 %all-reduce.6.cloned.1.call-done = (bf16[320,768]{1,0:T(8,128)(2,1)}, bf16[96,3840]{1,0:T(8,128)(2,1)}, bf16[320,288]{0,1:T(8,128)(2,1)}, bf16[32,5120]{1,0:T(8,...) async-done(((bf16[320,768]{1,0:T(8,128)(2,1)}, bf16[96,3840]{1,0:T(8,128)(2,1)}, ...) | async-done | bytes 15667216 | tf_op jit(solution)/shard_map/psum | solution.py:108
  3395.2 19.9 fusion.67
  3415.1 19.8 fusion.74
  3434.9 19.5 fusion.81
  (551 shorter events, 756.7 us)
Async XLA Ops:
  7.2 562.3 %all-reduce.8.cloned.1.call-start = ((), (), s32[]{:S(2)}) async-start(), calls=%async_computation.27 | async-start | bytes 31408128 | tf_op jit(solution)/shard_map/psum | solution.py:31
  34.9 561.7 %all-gather.25.cloned.1.call-start = ((), (), s32[]{:S(2)}) async-start(), calls=%async_computation.24 | async-start | bytes 1990656 | tf_op jit(solution)/shard_map/all_gather | solution.py:193
  569.5 63.8 %all-gather.11.cloned.1.call-start = ((), (), s32[]{:S(2)}) async-start(), calls=%async_computation.10 | async-start | bytes 2949120 | tf_op jit(solution)/shard_map/all_gather | solution.py:194
  570.3 95.7 %all-gather.13.cloned.1.call-start = ((), (), s32[]{:S(2)}) async-start(), calls=%async_computation.11 | async-start | bytes 4423680 | tf_op jit(solution)/shard_map/all_gather | solution.py:191
  570.9 140.8 %all-gather.15.cloned.1.call-start = ((), (), s32[]{:S(2)}) async-start(), calls=%async_computation.12 | async-start | bytes 6635520 | tf_op jit(solution)/shard_map/all_gather | solution.py:192
  571.4 257.5 %all-gather.17.cloned.1.call-start = ((), (), s32[]{:S(2)}) async-start(), calls=%async_computation.13 | async-start | bytes 14745600 | tf_op jit(solution)/shard_map/all_gather | solution.py:195
  572.0 375.2 %all-gather.21.cloned.1.call-start = ((), (), s32[]{:S(2)}) async-start(), calls=%async_computation.15 | async-start | bytes 36864000 | tf_op jit(solution)/shard_map/all_gather | solution.py:197
  572.8 533.8 %all-gather.19.cloned.1.call-start = ((), (), s32[]{:S(2)}) async-start(), calls=%async_computation.14 | async-start | bytes 36864000 | tf_op jit(solution)/shard_map/all_gather | solution.py:196
  573.5 692.4 %all-gather.23.cloned.1.call-start = ((), (), s32[]{:S(2)}) async-start(), calls=%async_computation.16 | async-start | bytes 36864000 | tf_op jit(solution)/shard_map/all_gather | solution.py:198
  1342.5 29.9 reduce-scatter.31.cloned.1.call-start
  1353.2 47.5 %reduce-scatter.29.cloned.1.call-start = ((), (), s32[]{:S(2)}) async-start(), calls=%async_computation.28 | async-start | bytes 1310720 | tf_op jit(solution)/shard_map/while/body/eval_jaxpr/reduce_scatter | solution.py:356
  1413.1 46.2 %reduce-scatter.29.cloned.1.call-start = ((), (), s32[]{:S(2)}) async-start(), calls=%async_computation.28 | async-start | bytes 1310720 | tf_op jit(solution)/shard_map/while/body/eval_jaxpr/reduce_scatter | solution.py:356
  1471.7 46.0 %reduce-scatter.29.cloned.1.call-start = ((), (), s32[]{:S(2)}) async-start(), calls=%async_computation.28 | async-start | bytes 1310720 | tf_op jit(solution)/shard_map/while/body/eval_jaxpr/reduce_scatter | solution.py:356
  1530.2 46.0 %reduce-scatter.29.cloned.1.call-start = ((), (), s32[]{:S(2)}) async-start(), calls=%async_computation.28 | async-start | bytes 1310720 | tf_op jit(solution)/shard_map/while/body/eval_jaxpr/reduce_scatter | solution.py:356
  1577.9 28.5 reduce-scatter.31.cloned.1.call-start
  1588.6 46.1 %reduce-scatter.29.cloned.1.call-start = ((), (), s32[]{:S(2)}) async-start(), calls=%async_computation.28 | async-start | bytes 1310720 | tf_op jit(solution)/shard_map/while/body/eval_jaxpr/reduce_scatter | solution.py:356
  1636.5 28.5 reduce-scatter.31.cloned.1.call-start
  1647.2 46.2 %reduce-scatter.29.cloned.1.call-start = ((), (), s32[]{:S(2)}) async-start(), calls=%async_computation.28 | async-start | bytes 1310720 | tf_op jit(solution)/shard_map/while/body/eval_jaxpr/reduce_scatter | solution.py:356
  1695.1 28.5 reduce-scatter.31.cloned.1.call-start
  1705.7 46.2 %reduce-scatter.29.cloned.1.call-start = ((), (), s32[]{:S(2)}) async-start(), calls=%async_computation.28 | async-start | bytes 1310720 | tf_op jit(solution)/shard_map/while/body/eval_jaxpr/reduce_scatter | solution.py:356
  1764.3 46.1 %reduce-scatter.29.cloned.1.call-start = ((), (), s32[]{:S(2)}) async-start(), calls=%async_computation.28 | async-start | bytes 1310720 | tf_op jit(solution)/shard_map/while/body/eval_jaxpr/reduce_scatter | solution.py:356
  1822.9 46.0 %reduce-scatter.29.cloned.1.call-start = ((), (), s32[]{:S(2)}) async-start(), calls=%async_computation.28 | async-start | bytes 1310720 | tf_op jit(solution)/shard_map/while/body/eval_jaxpr/reduce_scatter | solution.py:356
  1881.3 46.2 %reduce-scatter.29.cloned.1.call-start = ((), (), s32[]{:S(2)}) async-start(), calls=%async_computation.28 | async-start | bytes 1310720 | tf_op jit(solution)/shard_map/while/body/eval_jaxpr/reduce_scatter | solution.py:356
  1929.2 94.9 %reduce-scatter.27.cloned.1.call-start = ((), (), s32[]{:S(2)}) async-start(), calls=%async_computation.25 | async-start | bytes 2211840
  1938.9 87.1 %reduce-scatter.17.cloned.1.call-start = ((), (), s32[]{:S(2)}) async-start(), calls=%async_computation.19 | async-start | bytes 2949120 | tf_op jit(solution)/shard_map/reduce_scatter | solution.py:105
  1946.2 134.3 %reduce-scatter.13.cloned.1.call-start = ((), (), s32[]{:S(2)}) async-start(), calls=%async_computation.17 | async-start | bytes 4423680 | tf_op jit(solution)/shard_map/reduce_scatter | solution.py:105
  1959.1 185.0 %reduce-scatter.15.cloned.1.call-start = ((), (), s32[]{:S(2)}) async-start(), calls=%async_computation.18 | async-start | bytes 6635520 | tf_op jit(solution)/shard_map/reduce_scatter | solution.py:105
  1965.2 277.7 %reduce-scatter.19.cloned.1.call-start = ((), (), s32[]{:S(2)}) async-start(), calls=%async_computation.20 | async-start | bytes 14745600 | tf_op jit(solution)/shard_map/reduce_scatter | solution.py:105
  1974.9 473.5 %reduce-scatter.21.cloned.1.call-start = ((), (), s32[]{:S(2)}) async-start(), calls=%async_computation.21 | async-start | bytes 36864000 | tf_op jit(solution)/shard_map/reduce_scatter | solution.py:105
  1991.5 662.2 %reduce-scatter.23.cloned.1.call-start = ((), (), s32[]{:S(2)}) async-start(), calls=%async_computation.22 | async-start | bytes 36864000 | tf_op jit(solution)/shard_map/reduce_scatter | solution.py:105
  2008.0 851.1 %reduce-scatter.25.cloned.1.call-start = ((), (), s32[]{:S(2)}) async-start(), calls=%async_computation.23 | async-start | bytes 36864000 | tf_op jit(solution)/shard_map/reduce_scatter | solution.py:105
  2024.0 1371.2 %all-reduce.6.cloned.1.call-start = ((), (), s32[]{:S(2)}) async-start(), calls=%async_computation.26 | async-start | bytes 31408128 | tf_op jit(solution)/shard_map/psum | solution.py:108
  (84 other events, 3425.4 us)
Sparse Core Ops, SparseCore 0:
  35.1 534.4 all-reduce.7
  571.4 25.2 all-gather.24
  598.5 30.0 all-gather.10
  630.4 35.6 all-gather.12
  667.8 43.8 all-gather.14
  713.4 74.3 all-gather.16
  789.7 157.4 all-gather.20
  949.1 157.4 all-gather.18
  1108.5 157.4 all-gather.22
  1353.3 19.0 reduce-scatter.30
  1375.4 25.3 reduce-scatter.28
  1434.0 25.3 reduce-scatter.28
  1492.4 25.3 reduce-scatter.28
  1550.9 25.2 reduce-scatter.28
  1588.7 17.7 reduce-scatter.30
  1609.4 25.2 reduce-scatter.28
  1647.3 17.7 reduce-scatter.30
  1668.0 25.2 reduce-scatter.28
  1705.8 17.7 reduce-scatter.30
  1726.6 25.2 reduce-scatter.28
  1785.1 25.2 reduce-scatter.28
  1843.5 25.2 reduce-scatter.28
  1902.1 25.2 reduce-scatter.28
  1939.0 38.9 reduce-scatter.26
  1982.3 43.6 reduce-scatter.16
  2030.5 50.0 reduce-scatter.12
  2084.4 59.6 reduce-scatter.14
  2147.7 95.1 reduce-scatter.18
  2246.7 201.7 reduce-scatter.20
  2452.0 201.7 reduce-scatter.22
  2657.4 201.6 reduce-scatter.24
  2863.1 532.0 all-reduce.5
  (6 shorter events, 105.8 us)
where the time goes:
time: 3490 us; the launch traced here: 3480 us
  waiting for transfers between devices  2650 us (76%)
  matrix products  487 us (14%)
  other arithmetic  174 us (5%)
  blocking collectives  87.8 us (3%)
  local copies, waits for them, and re-layouts  57.5 us (2%)
    reduce_scatter x7, waiting for transfers between devices, reduce_term(): lax.psum_scatter(gradient_term.astype(jnp.bfloat16), 'dp', scatter_dimens...  833 us
    psum x1, waiting for transfers between devices, spread(): return lax.psum(kept, axis)  535 us
    psum x1, waiting for transfers between devices, reduce_term(): reduced_rows = lax.psum(wide_part, 'own').astype(jnp.float32)  466 us
    reduce_scatter x10, waiting for transfers between devices, backward_split(): lax.psum_scatter(partial_key.astype(jnp.bfloat16), 'own', scatter_dimensi...  275 us
    all_gather x1, waiting for transfers between devices, shards(): lax.all_gather(copies[7], 'dp', axis=0, tiled=True)  140 us
    all_gather x1, waiting for transfers between devices, shards(): lax.all_gather(copies[5], 'dp', axis=0, tiled=True)  139 us
    all_gather x1, waiting for transfers between devices, shards(): lax.all_gather(copies[6], 'dp', axis=0, tiled=True)  106 us
    reduce_scatter x10, waiting for transfers between devices, backward_split(): lax.psum_scatter(rope_part.astype(jnp.bfloat16), 'own', scatter_dimension...  93.9 us
  transfers between devices with their start and end apart: 38, of which 35 were waited for; matrix products, arithmetic and copies ran while one was open for 12% of the time, Pallas kernels for 0%

commit v1 on v0

v1 whole, which is shorter than its diff:
```python
import math

import jax
import jax.numpy as jnp
from jax import lax
from jax.experimental import pallas as pl
from jax.experimental.pallas import tpu as pltpu
from jax.sharding import PartitionSpec as P

D = 2560
H = 40
NOPE = 64
ROPE = 32
VD = 64
QR = 768
KVR = 256
FF = 6400
HEADS_STEP = 2
LANES = 128
STEP = 7


EPSILON = 1e-05
RESIDUAL_SCALE = 1.4 / math.sqrt(62.0)
BETA_ONE = 0.5
BETA_TWO = 0.55
WEIGHT_DECAY = 0.1
ADAM_EPS = 1e-08
MASKED = -1e30
SOFTMAX_SCALE = (NOPE + ROPE) ** (-0.5)


def tied(value, *earlier):
    return lax.optimization_barrier((value, *earlier))[0]


def pieces_of(rows, most):
    for parts in range(most, 1, -1):
        if rows.shape[0] % parts == 0 and (rows.shape[0] // parts) % 8 == 0:
            return [Piece(part) for part in jnp.split(rows, parts, axis=0)]
    return [Piece(rows)]


class Piece:
    def __init__(self, value):
        self.value = value
        self.leg = 0


class Line:
    def __init__(self):
        self.count, self.place = lax.axis_size("own"), lax.axis_index("own")
        self.active = []
        self.arrived = []

    def round(self, *new, after=()):
        last, half = self.count - 1, self.count // 2
        self.active.extend(new)
        values = [piece.value for piece in self.active]
        if self.arrived or after:
            values = lax.optimization_barrier((*values, *self.arrived, *after))
        self.arrived = []
        for piece, value in zip(self.active, values):
            if piece.leg < half - 1:
                hop = piece.leg
                landed = lax.ppermute(value, "own", [(hop, hop + 1), (last - hop, last - hop - 1)])
                piece.value = value + landed
            elif piece.leg == half - 1:
                landed = lax.ppermute(value, "own", [(half - 1, half), (half, half - 1)])
                piece.value = value + landed
            else:
                outer = 2 * half - 2 - piece.leg
                inner = outer + 1
                landed = lax.ppermute(
                    value, "own", [(inner, outer), (last - inner, last - outer)]
                )
                ended = (self.place == outer) | (self.place == last - outer)
                piece.value = jnp.where(ended, landed, value)
            piece.leg += 1
            self.arrived.append(landed)
        self.active = [piece for piece in self.active if piece.leg < self.count - 1]

    def then(self, value):
        return tied(value, *self.arrived)


def rows_of(pieces):
    return jnp.concatenate([piece.value for piece in pieces], axis=0)


def gather_rows(rows):
    return lax.all_gather(rows, "dp", axis=0, tiled=True)


def scatter_low(rows):
    return lax.psum_scatter(rows, "dp", scatter_dimension=0, tiled=True)


def scatter_rows(rows):
    return scatter_low(rows).astype(jnp.float32)


def rms_forward(values, norm_gain):
    inverse = lax.rsqrt(jnp.mean(values * values, axis=-1, keepdims=True) + EPSILON)
    return (values * inverse * norm_gain, inverse)


def rms_backward(values, inverse, norm_gain, grad_normed):
    normed = values * inverse
    grad_gain = jnp.sum(grad_normed * normed, axis=0)
    scaled = grad_normed * norm_gain
    grad_values = inverse * (scaled - normed * jnp.mean(scaled * normed, axis=-1, keepdims=True))
    return (grad_values, grad_gain)


def rotary_tables(positions):
    half_width = ROPE // 2
    frequency = 10000.0 ** (-jnp.arange(half_width, dtype=jnp.float32) / half_width)
    angles = positions.astype(jnp.float32)[:, None] * frequency[None, :]
    return (jnp.cos(angles), jnp.sin(angles))


def rotate(values, cosine, sine_table):
    half_width = values.shape[-1] // 2
    former = values[..., :half_width]
    latter = values[..., half_width:]
    return jnp.concatenate(
        [former * cosine - latter * sine_table, latter * cosine + former * sine_table], axis=-1
    )


def unrotate(gradient, cosine, sine_table):
    half_width = gradient.shape[-1] // 2
    former = gradient[..., :half_width]
    latter = gradient[..., half_width:]
    return jnp.concatenate(
        [former * cosine + latter * sine_table, latter * cosine - former * sine_table], axis=-1
    )


def contract_rows(first_matrix, second_matrix):
    return lax.dot_general(
        first_matrix, second_matrix, (((0,), (0,)), ((), ())), preferred_element_type=jnp.float32
    )


def times_transpose(first_matrix, second_matrix):
    return lax.dot_general(
        first_matrix, second_matrix, (((1,), (1,)), ((), ())), preferred_element_type=jnp.float32
    )


def wide_query(query):
    tokens=query.shape[1]
    zero=lambda rows: jnp.zeros((rows,tokens),query.dtype)
    return jnp.concatenate([query[:NOPE],zero(VD),query[NOPE:],zero(128-ROPE)],axis=0)

def attend_kernel(query_ref,kv_ref,rope_ref,bias_ref,out_ref,log_ref):
    rope=rope_ref[...]
    for head in range(HEADS_STEP):
        query=wide_query(query_ref[head*(NOPE+ROPE):(head+1)*(NOPE+ROPE),:])
        kv=kv_ref[:,head*(NOPE+VD):(head+1)*(NOPE+VD)]
        keys=jnp.concatenate([kv,rope],axis=1)
        scores=jnp.dot(keys,query,preferred_element_type=jnp.float32) * SOFTMAX_SCALE+bias_ref[...]
        peak=jnp.max(scores,axis=0,keepdims=True)
        exponent=jnp.exp(scores-peak)
        total=jnp.sum(exponent,axis=0,keepdims=True)
        weights=(exponent*(1.0/total)).astype(jnp.bfloat16)
        out=contract_rows(kv,weights)
        out_ref[head*VD:(head+1)*VD,:]=out[NOPE:].astype(out_ref.dtype)
        log_ref[head]=peak+jnp.log(total)

def attend(query,kv,rope,bias):
    tokens=query.shape[1]; length=kv.shape[0]
    return pl.pallas_call(
        attend_kernel,
        grid=(H//HEADS_STEP,),
        in_specs=[
            pl.BlockSpec((HEADS_STEP*(NOPE+ROPE),tokens),lambda i:(i,0)),
            pl.BlockSpec((length,HEADS_STEP*(NOPE+VD)),lambda i:(0,i)),
            pl.BlockSpec((length,128),lambda i:(0,0)),
            pl.BlockSpec((length,tokens),lambda i:(0,0)),
        ],
        out_specs=[
            pl.BlockSpec((HEADS_STEP*VD,tokens),lambda i:(i,0)),
            pl.BlockSpec((HEADS_STEP,1,tokens),lambda i:(i,0,0)),
        ],
        out_shape=[jax.ShapeDtypeStruct((H*VD,tokens),jnp.bfloat16),jax.ShapeDtypeStruct((H,1,tokens),jnp.float32)],
        compiler_params=pltpu.CompilerParams(vmem_limit_bytes=48*1024*1024),
    )(query,kv,rope,bias)

def attend_back_kernel(query_ref,kv_ref,rope_ref,bias_ref,log_ref,grad_ref,cos_ref,sin_ref,dq_ref,dkv_ref,dr_ref):
    rope=rope_ref[...]
    half=ROPE//2
    @pl.when(pl.program_id(0)==0)
    def _():
        dr_ref[...]=jnp.zeros_like(dr_ref)
    for head in range(HEADS_STEP):
        query=wide_query(query_ref[head*(NOPE+ROPE):(head+1)*(NOPE+ROPE),:])
        kv=kv_ref[:,head*(NOPE+VD):(head+1)*(NOPE+VD)]
        grad=grad_ref[head*VD:(head+1)*VD,:]
        grad=jnp.concatenate([jnp.zeros((NOPE,grad.shape[1]),grad.dtype),grad],axis=0)
        keys=jnp.concatenate([kv,rope],axis=1)
        scores=jnp.dot(keys,query,preferred_element_type=jnp.float32) * SOFTMAX_SCALE+bias_ref[...]
        weights=jnp.exp(scores-log_ref[head])
        grad_weights=jnp.dot(kv,grad,preferred_element_type=jnp.float32)
        inner=jnp.sum(weights*grad_weights,axis=0,keepdims=True)
        grad_scores=(weights*(grad_weights-inner)).astype(jnp.bfloat16)
        key_side=times_transpose(grad_scores,query) * SOFTMAX_SCALE
        dkv=key_side[:,:128]+times_transpose(weights.astype(jnp.bfloat16),grad)
        dkv_ref[:,head*(NOPE+VD):(head+1)*(NOPE+VD)]=dkv.astype(dkv_ref.dtype)
        dr_ref[...]+=key_side[:,128:]
        dq=contract_rows(keys,grad_scores) * SOFTMAX_SCALE
        former=dq[128:128+half]; latter=dq[128+half:128+ROPE]
        base=head*(NOPE+ROPE)
        dq_ref[base:base+NOPE,:]=dq[:NOPE].astype(dq_ref.dtype)
        dq_ref[base+NOPE:base+NOPE+half,:]=(former*cos_ref[...]+latter*sin_ref[...]).astype(dq_ref.dtype)
        dq_ref[base+NOPE+half:base+NOPE+ROPE,:]=(latter*cos_ref[...]-former*sin_ref[...]).astype(dq_ref.dtype)

def attend_back(query,kv,rope,bias,logs,grad,cos,sin):
    tokens=query.shape[1]; length=kv.shape[0]
    return pl.pallas_call(
        attend_back_kernel,
        grid=(H//HEADS_STEP,),
        in_specs=[
            pl.BlockSpec((HEADS_STEP*(NOPE+ROPE),tokens),lambda i:(i,0)),
            pl.BlockSpec((length,HEADS_STEP*(NOPE+VD)),lambda i:(0,i)),
            pl.BlockSpec((length,128),lambda i:(0,0)),
            pl.BlockSpec((length,tokens),lambda i:(0,0)),
            pl.BlockSpec((HEADS_STEP,1,tokens),lambda i:(i,0,0)),
            pl.BlockSpec((HEADS_STEP*VD,tokens),lambda i:(i,0)),
            pl.BlockSpec((ROPE//2,tokens),lambda i:(0,0)),
            pl.BlockSpec((ROPE//2,tokens),lambda i:(0,0)),
        ],
        out_specs=[
            pl.BlockSpec((HEADS_STEP*(NOPE+ROPE),tokens),lambda i:(i,0)),
            pl.BlockSpec((length,HEADS_STEP*(NOPE+VD)),lambda i:(0,i)),
            pl.BlockSpec((length,128),lambda i:(0,0)),
        ],
        out_shape=[jax.ShapeDtypeStruct((H*(NOPE+ROPE),tokens),jnp.bfloat16),
                   jax.ShapeDtypeStruct((length,H*(NOPE+VD)),jnp.bfloat16),
                   jax.ShapeDtypeStruct((length,128),jnp.float32)],
        compiler_params=pltpu.CompilerParams(vmem_limit_bytes=48*1024*1024),
    )(query,kv,rope,bias,logs,grad,cos,sin)


def adamw_update(master, first_moment, second_moment, gradient, learn_rate, weight_decay, is_owner):
    new_first = BETA_ONE * first_moment + (1.0 - BETA_ONE) * gradient
    new_second = BETA_TWO * second_moment + (1.0 - BETA_TWO) * gradient * gradient
    mean_hat = new_first / (1.0 - BETA_ONE**STEP)
    square_hat = new_second / (1.0 - BETA_TWO**STEP)
    new_master = master - learn_rate * (
        mean_hat / (jnp.sqrt(square_hat) + ADAM_EPS) + weight_decay * master
    )
    return (
        jnp.where(is_owner, new_master, master),
        jnp.where(is_owner, new_first, first_moment),
        jnp.where(is_owner, new_second, second_moment),
    )


def shards(
    hidden,
    cotangent,
    block_index,
    owners,
    query_down,
    query_down_first,
    query_down_second,
    query_up,
    query_up_first,
    query_up_second,
    latent_down,
    latent_down_first,
    latent_down_second,
    latent_up,
    latent_up_first,
    latent_up_second,
    output_weight,
    output_weight_first,
    output_weight_second,
    gate_weight,
    gate_weight_first,
    gate_weight_second,
    up_weight,
    up_weight_first,
    up_weight_second,
    down_weight,
    down_weight_first,
    down_weight_second,
    norm_gains,
    norm_gains_first,
    norm_gains_second,
):
    own_count = lax.axis_size("own")
    own_place = lax.axis_index("own")
    tokens_here = hidden.shape[0]
    sequence_length = tokens_here * own_count
    low = jnp.bfloat16
    inputs = hidden.astype(jnp.float32)
    is_owner = [own_place == owners[slot] for slot in range(9)]
    def owned(slot, tensor):
        return jnp.where(is_owner[slot], tensor[0], 0.0).astype(low)

    gain_count = norm_gains.shape[1]
    gain_columns = -(-gain_count // query_down.shape[1])
    gain_block = jnp.pad(
        owned(8, norm_gains), (0, gain_columns * query_down.shape[1] - gain_count)
    ).reshape(gain_columns, query_down.shape[1])
    width = QR + KVR + ROPE
    line = Line()
    down_latents = Piece(
        jnp.concatenate([owned(0, query_down), owned(2, latent_down), gain_block.T], axis=-1)
    )
    query_up_rows = Piece(owned(1, query_up))
    latent_up_rows = Piece(owned(3, latent_up))
    output_rows = Piece(owned(4, output_weight))
    gate_rows = pieces_of(owned(5, gate_weight), 2)
    up_rows = pieces_of(owned(6, up_weight), 2)
    down_rows = pieces_of(owned(7, down_weight), 2)
    grad_ffn_all = gather_rows(
        (RESIDUAL_SCALE * cotangent.astype(jnp.float32)).astype(low)
    )
    line.round(down_latents)
    line.round(query_up_rows, latent_up_rows)
    line.round()
    down_latents_all = gather_rows(down_latents.value)
    line.round(output_rows)
    query_up_all = gather_rows(query_up_rows.value)
    latent_up_all = gather_rows(latent_up_rows.value)
    down_latents_all = line.then(down_latents_all)
    line.round(gate_rows[0])
    gains_float = down_latents_all[:, width:].reshape(-1, query_down.shape[1], gain_columns)
    gains_float = gains_float.transpose(0, 2, 1).reshape(-1, gain_columns * query_down.shape[1])
    gains_float = gains_float[:, :gain_count].reshape(-1).astype(jnp.float32)
    down_latents_all = down_latents_all[:, :width]
    gain_input = gains_float[:D]
    gain_query = gains_float[D : D + QR]
    gain_latent = gains_float[D + QR : D + QR + KVR]
    gain_ffn = gains_float[D + QR + KVR :]

    grad_output = cotangent.astype(jnp.float32)

    normed, inverse_input = rms_forward(inputs, gain_input)
    normed_low = normed.astype(low)
    latents = jnp.dot(normed_low, down_latents_all, preferred_element_type=jnp.float32)
    query_latent = latents[:, :QR]
    key_latent = latents[:, QR:]
    query_normed, inverse_query = rms_forward(query_latent, gain_query)
    query_low = query_normed.astype(low)
    positions = own_place * tokens_here + jnp.arange(tokens_here, dtype=jnp.int32)
    cosine, sine_table = rotary_tables(positions)
    key_normed, inverse_key = rms_forward(key_latent[:, :KVR], gain_latent)
    key_low = key_normed.astype(low)
    rope_low = rotate(key_latent[:, KVR:], cosine, sine_table).astype(low)
    gathered_keys = lax.all_gather(
        jnp.concatenate([key_low, rope_low], axis=-1), "own", axis=0, tiled=True
    )
    line.round(*gate_rows[1:], after=[gathered_keys])
    output_all = gather_rows(output_rows.value)
    gathered_latent = gathered_keys[:, :KVR]
    rope_keys = jnp.pad(gathered_keys[:, KVR:], ((0, 0), (0, LANES - ROPE)))
    query_raw = lax.dot_general(
        query_up_all, query_low, (((0,), (1,)), ((), ())), preferred_element_type=jnp.float32
    ).reshape(H, NOPE + ROPE, tokens_here)
    cosine_rows, sine_rows = cosine.T, sine_table.T
    former, latter = jnp.split(query_raw[:, NOPE:], 2, axis=1)
    queries = jnp.concatenate(
        [
            query_raw[:, :NOPE],
            former * cosine_rows - latter * sine_rows,
            latter * cosine_rows + former * sine_rows,
        ],
        axis=1,
    )
    queries = queries.astype(low).reshape(H * (NOPE + ROPE), tokens_here)
    key_value = jnp.dot(gathered_latent, latent_up_all, preferred_element_type=jnp.float32).astype(
        low
    )
    key_value, queries = line.then(key_value), line.then(queries)
    line.round(up_rows[0], after=[key_value])
    sequence_blocks = block_index[0]
    query_blocks = lax.dynamic_slice_in_dim(
        sequence_blocks, own_place * tokens_here, tokens_here, 0
    )
    bias = jnp.where(sequence_blocks[:, None] <= query_blocks[None, :], 0.0, MASKED)
    bias = bias.astype(jnp.float32)
    attended_low, logsum = attend(queries, key_value, rope_keys, bias)
    line.round(*up_rows[1:], after=[attended_low])
    gate_columns = lax.all_to_all(rows_of(gate_rows), "dp", 1, 0, tiled=True)
    output_all = line.then(output_all)
    branch = contract_rows(attended_low, output_all)
    middle = inputs + RESIDUAL_SCALE * branch
    normed_ffn, inverse_ffn = rms_forward(middle, gain_ffn)

    normed_ffn_low = normed_ffn.astype(low)
    line.round(down_rows[0], after=[normed_ffn_low])
    normed_ffn_all = gather_rows(normed_ffn_low)
    line.round(*down_rows[1:])
    up_columns = lax.all_to_all(rows_of(up_rows), "dp", 1, 0, tiled=True)
    while line.active:
        line.round()
    down_rows = rows_of(down_rows)
    gate_pre = jnp.dot(normed_ffn_all, gate_columns, preferred_element_type=jnp.float32)
    up_pre = jnp.dot(normed_ffn_all, up_columns, preferred_element_type=jnp.float32)
    sigmoid_gate = jax.nn.sigmoid(gate_pre)
    silu_gate = gate_pre * sigmoid_gate
    activated_low = (silu_gate * up_pre).astype(low)
    down_part = contract_rows(activated_low, grad_ffn_all).astype(low)
    line = Line()
    down_sum = pieces_of(down_part, 4)
    line.round(down_sum[0])
    grad_activated = times_transpose(grad_ffn_all, down_rows)
    grad_gate_pre = (
        grad_activated * up_pre * sigmoid_gate * (1.0 + gate_pre * (1.0 - sigmoid_gate))
    ).astype(low)
    grad_up_pre = (grad_activated * silu_gate).astype(low)
    grad_normed_ffn = (
        times_transpose(grad_gate_pre, gate_columns) + times_transpose(grad_up_pre, up_columns)
    ).astype(low)
    grad_normed_ffn, grad_gate_pre, grad_up_pre = lax.optimization_barrier(
        (grad_normed_ffn, grad_gate_pre, grad_up_pre)
    )
    grad_normed_ffn = scatter_rows(grad_normed_ffn)
    line.round(*down_sum[1:2])
    gate_part = contract_rows(normed_ffn_all, grad_gate_pre).astype(low)
    gate_part, grad_up_pre = lax.optimization_barrier((gate_part, grad_up_pre))
    gate_part = lax.all_to_all(gate_part, "dp", 0, 1, tiled=True)
    line.round(*down_sum[2:3])
    grad_up_pre = line.then(grad_up_pre)
    up_part = contract_rows(normed_ffn_all, grad_up_pre).astype(low)
    line.round(*down_sum[3:4], after=[up_part])
    up_part = lax.all_to_all(tied(up_part, gate_part), "dp", 0, 1, tiled=True)
    gate_sum = pieces_of(gate_part, 2)
    line.round(gate_sum[0])
    grad_normed_ffn = line.then(grad_normed_ffn)

    grad_middle_part, grad_gain_ffn = rms_backward(middle, inverse_ffn, gain_ffn, grad_normed_ffn)
    grad_middle = grad_output + grad_middle_part
    grad_branch = (RESIDUAL_SCALE * grad_middle).astype(low)
    output_part = jnp.dot(attended_low, grad_branch, preferred_element_type=jnp.float32).astype(low)
    grad_attended = times_transpose(output_all, grad_branch).astype(low)
    grad_attended, output_part = lax.optimization_barrier((grad_attended, output_part))
    output_part = scatter_low(output_part)
    line.round(*gate_sum[1:], after=[grad_attended])
    grad_query_raw, grad_key, grad_rope = attend_back(
        queries, key_value, rope_keys, bias, logsum, grad_attended, cosine_rows, sine_rows
    )
    grad_key = line.then(grad_key)
    up_sum = pieces_of(up_part, 2)
    line.round(up_sum[0], after=[grad_query_raw])
    latent_up_part = scatter_low(contract_rows(gathered_latent, grad_key).astype(low))
    key_side = jnp.concatenate([times_transpose(grad_key, latent_up_all), grad_rope[:, :ROPE]], axis=-1)
    key_side = lax.psum_scatter(
        key_side.astype(low), "own", scatter_dimension=0, tiled=True
    ).astype(jnp.float32)
    query_up_part = scatter_low(
        lax.dot_general(
            query_low,
            grad_query_raw,
            (((0,), (1,)), ((), ())),
            preferred_element_type=jnp.float32,
        ).astype(low)
    )
    grad_query_normed = lax.dot_general(
        grad_query_raw, query_up_all, (((0,), (1,)), ((), ())), preferred_element_type=jnp.float32
    )
    grad_query_latent, grad_gain_query = rms_backward(
        query_latent, inverse_query, gain_query, grad_query_normed
    )
    grad_key_latent, grad_gain_latent = rms_backward(
        key_latent[:, :KVR], inverse_key, gain_latent, key_side[:, :KVR]
    )
    grad_latents = jnp.concatenate(
        [grad_query_latent, grad_key_latent, unrotate(key_side[:, KVR:], cosine, sine_table)],
        axis=-1,
    ).astype(low)
    grad_latents = line.then(grad_latents)
    grad_normed = times_transpose(grad_latents, down_latents_all)
    grad_inputs, grad_gain_input = rms_backward(inputs, inverse_input, gain_input, grad_normed)
    input_grad = (grad_middle + grad_inputs).astype(low)
    grad_gains = jnp.concatenate(
        [grad_gain_input, grad_gain_query, grad_gain_latent, grad_gain_ffn]
    ).reshape(-1, gain_count)
    grad_gains = jnp.pad(
        grad_gains, ((0, 0), (0, gain_columns * query_down.shape[1] - gain_count))
    ).reshape(-1, gain_columns, query_down.shape[1])
    latents_part = jnp.concatenate(
        [
            contract_rows(normed_low, grad_latents),
            grad_gains.transpose(0, 2, 1).reshape(-1, gain_columns),
        ],
        axis=-1,
    ).astype(low)
    line.round(*up_sum[1:], after=[latents_part])
    latents_part = scatter_low(latents_part)
    ffn_part = jnp.dot(activated_low, down_rows, preferred_element_type=jnp.float32).astype(low)
    ffn_branch = scatter_rows(tied(line.then(ffn_part), latents_part))
    block_output = (middle + RESIDUAL_SCALE * ffn_branch).astype(low)
    output_sum, latent_up_sum = Piece(output_part), Piece(latent_up_part)
    query_up_sum, latents_sum = Piece(query_up_part), Piece(latents_part)
    line.round(output_sum)
    line.round(latent_up_sum, query_up_sum)
    line.round(latents_sum)
    while line.active:
        line.round()
    reduced_output, reduced_latent_up = output_sum.value, latent_up_sum.value
    reduced_query_up, reduced_latents = query_up_sum.value, latents_sum.value
    reduced_down, reduced_gate, reduced_up = rows_of(down_sum), rows_of(gate_sum), rows_of(up_sum)
    reduced_latents = reduced_latents.astype(jnp.float32)
    reduced_gains = reduced_latents[:, width:].T.reshape(-1)[:gain_count]
    reduced = (
        reduced_latents[:, :QR],
        reduced_query_up.astype(jnp.float32),
        reduced_latents[:, QR:width],
        reduced_latent_up.astype(jnp.float32),
        reduced_output.astype(jnp.float32),
        reduced_gate.astype(jnp.float32),
        reduced_up.astype(jnp.float32),
        reduced_down.astype(jnp.float32),
        reduced_gains,
    )
    states = (
        (query_down, query_down_first, query_down_second),
        (query_up, query_up_first, query_up_second),
        (latent_down, latent_down_first, latent_down_second),
        (latent_up, latent_up_first, latent_up_second),
        (output_weight, output_weight_first, output_weight_second),
        (gate_weight, gate_weight_first, gate_weight_second),
        (up_weight, up_weight_first, up_weight_second),
        (down_weight, down_weight_first, down_weight_second),
        (norm_gains, norm_gains_first, norm_gains_second),
    )
    learn_rates = (
        D ** (-0.5),
        QR ** (-0.5),
        D ** (-0.5),
        KVR ** (-0.5),
        math.sqrt(sequence_length / (0.0632 * H * VD)),
        D ** (-0.5),
        D ** (-0.5),
        math.sqrt(1.0 / (0.0114 * FF)),
        0.6,
    )
    results = [block_output, input_grad]
    for slot in range(9):
        master, first_moment, second_moment = states[slot]
        updated = adamw_update(
            master[0],
            first_moment[0],
            second_moment[0],
            reduced[slot],
            learn_rates[slot],
            0.0 if slot == 8 else WEIGHT_DECAY,
            is_owner[slot],
        )
        results.extend((member[None] for member in updated))
    return tuple(results)


def solution(mesh):
    return jax.shard_map(
        shards,
        mesh=mesh,
        in_specs=(
            P(("dp", "own"), None),
            P(("dp", "own"), None),
            P("dp", None),
            P(),
            P("own", "dp", None),
            P("own", "dp", None),
            P("own", "dp", None),
            P("own", "dp", None),
            P("own", "dp", None),
            P("own", "dp", None),
            P("own", "dp", None),
            P("own", "dp", None),
            P("own", "dp", None),
            P("own", "dp", None),
            P("own", "dp", None),
            P("own", "dp", None),
            P("own", "dp", None),
            P("own", "dp", None),
            P("own", "dp", None),
            P("own", "dp", None),
            P("own", "dp", None),
            P("own", "dp", None),
            P("own", "dp", None),
            P("own", "dp", None),
            P("own", "dp", None),
            P("own", "dp", None),
            P("own", "dp", None),
            P("own", "dp", None),
            P("own", "dp"),
            P("own", "dp"),
            P("own", "dp"),
        ),
        out_specs=(
            P(("dp", "own"), None),
            P(("dp", "own"), None),
            P("own", "dp", None),
            P("own", "dp", None),
            P("own", "dp", None),
            P("own", "dp", None),
            P("own", "dp", None),
            P("own", "dp", None),
            P("own", "dp", None),
            P("own", "dp", None),
            P("own", "dp", None),
            P("own", "dp", None),
            P("own", "dp", None),
            P("own", "dp", None),
            P("own", "dp", None),
            P("own", "dp", None),
            P("own", "dp", None),
            P("own", "dp", None),
            P("own", "dp", None),
            P("own", "dp", None),
            P("own", "dp", None),
            P("own", "dp", None),
            P("own", "dp", None),
            P("own", "dp", None),
            P("own", "dp", None),
            P("own", "dp", None),
            P("own", "dp"),
            P("own", "dp"),
            P("own", "dp"),
        ),
        check_vma=False,
    )
```

time: 3490 us -> 1600 us (0.46)
  waiting for transfers between devices: 2650 us -> 580 us
  matrix products: 487 us -> 220 us
  starting transfers between devices: 1.78 us -> 230 us
  Pallas kernels: 0 us -> 86.2 us
  local copies, waits for them, and re-layouts: 57.5 us -> 124 us
  other arithmetic: 174 us -> 239 us
    reduce_scatter x27 -> x6, waiting for transfers between devices: 1200 us -> 7.36 us  [the longest x5 7.36 us: scatter_low(): return lax.psum_scatter(rows, 'dp', scatter_dimension=0, tiled=True)]
    psum x2 -> x0, waiting for transfers between devices: 1000 us -> none  [the longest x1 535 us: spread(): return lax.psum(kept, axis)]
    ppermute x0 -> x66, waiting for transfers between devices: none -> 495 us  [the longest x22 313 us: round(): lax.ppermute(value, 'own', [(hop, hop + 1), (last - hop, last - hop - 1)])]
    all_gather x8 -> x6, waiting for transfers between devices: 441 us -> 0.05 us  [gather_rows(): return lax.all_gather(rows, 'dp', axis=0, tiled=True)]
    dot_general x119 -> x8, matrix products: 336 us -> 71.3 us  [the longest x1 16.5 us: shards(): jnp.dot(activated_low, down_rows, preferred_element_type=jnp.float32)]
    ppermute x0 -> x66, starting transfers between devices: none -> 212 us  [the longest x22 154 us: round(): lax.ppermute(value, 'own', [(hop, hop + 1), (last - hop, last - hop - 1)])]
    pallas_call x0 -> x2, Pallas kernels: none -> 86.2 us  [the longest x1 49.4 us: attend_back(): pl.pallas_call(attend_back_kernel, grid=(H // HEADS_STEP,), in_specs=[pl....]
    add x10 -> x44, other arithmetic: 7.24 us -> 86.4 us  [the longest x43 84.5 us: round(): piece.value = value + landed]
  transfers between devices with their start and end apart: 38 -> 82, of which waited for: 35 -> 33; matrix products, arithmetic and copies ran while one was open for 12% -> 28% of each run, Pallas kernels for 0% -> 5%
where the time goes in v1:
time: 1600 us; the launch traced here: 1580 us
  waiting for transfers between devices  580 us (36%)
  other arithmetic  239 us (15%)
  starting transfers between devices  230 us (14%)
  matrix products  220 us (14%)
  local copies, waits for them, and re-layouts  124 us (8%)
  Pallas kernels  86.2 us (5%)
  blocking collectives  83.5 us (5%)
  between operations  22.3 us (1%)
    ppermute x22, waiting for transfers between devices, round(): lax.ppermute(value, 'own', [(hop, hop + 1), (last - hop, last - hop - 1)])  313 us
    ppermute x22, waiting for transfers between devices, round(): lax.ppermute(value, 'own', [(inner, outer), (last - inner, last - outer)])  182 us
    ppermute x22, starting transfers between devices, round(): lax.ppermute(value, 'own', [(hop, hop + 1), (last - hop, last - hop - 1)])  154 us
    add x43, other arithmetic, round(): piece.value = value + landed  84.5 us
    dot_general x6, matrix products, times_transpose(): lax.dot_general(first_matrix, second_matrix, (((1,), (1,)), ((), ())), pr...  82.3 us
    all_to_all x1, blocking collectives, shards(): up_part = lax.all_to_all(tied(up_part, gate_part), 'dp', 0, 1, tiled=True)  64.5 us
    dot_general x6, matrix products, contract_rows(): lax.dot_general(first_matrix, second_matrix, (((0,), (0,)), ((), ())), pr...  59 us
    select_n x4, other arithmetic, adamw_update(): jnp.where(is_owner, new_second, second_moment)  58.2 us
  transfers between devices with their start and end apart: 82, of which 33 were waited for; matrix products, arithmetic and copies ran while one was open for 28% of the time, Pallas kernels for 5%

profile of v1, /device:TPU:0, one launch (start us, length us, event | category | flops | bytes accessed | tf_op | source)
XLA Modules:
  0.0 1584.9 jit_solution(12700882220846238019)
XLA Ops:
  48.4 17.1 %collective-permute-done.3 = bf16[32,5120]{1,0:T(8,128)(2,1)S(1)} collective-permute-done((bf16[32,5120]{1,0:T(8,128)(2,1)S(1)}, bf16[32,5120]{1,0:T(8,128)(2,1)S(1)}, u32[]{:S(2)}, u32[]{:S(2)}) %collective-permute-start.3) | collective-permute-done | bytes 327712 | tf_op jit(solution)/shard_map/ppermute | solution.py:66
  69.7 17.5 %collective-permute-done.6 = bf16[320,1059]{1,0:T(8,128)(2,1)} collective-permute-done((bf16[320,1059]{1,0:T(8,128)(2,1)}, bf16[320,1059]{1,0:T(8,128)(2,1)}, u32[]{:S(2)}, u32[]{:S(2)}) %collective-permute-start.6) | collective-permute-done | bytes 677792 | tf_op jit(solution)/shard_map/ppermute | solution.py:74
  94.5 26.5 %collective-permute-done.8 = bf16[32,5120]{1,0:T(8,128)(2,1)S(1)} collective-permute-done((bf16[32,5120]{1,0:T(8,128)(2,1)S(1)}, bf16[32,5120]{1,0:T(8,128)(2,1)S(1)}, u32[]{:S(2)}, u32[]{:S(2)}) %collective-permute-start.8) | collective-permute-done | bytes 327712 | tf_op jit(solution)/shard_map/ppermute | solution.py:74
  142.6 28.9 %collective-permute-done.9 = bf16[320,2560]{1,0:T(8,128)(2,1)S(1)} collective-permute-done((bf16[320,2560]{1,0:T(8,128)(2,1)}, bf16[320,2560]{1,0:T(8,128)(2,1)S(1)}, u32[]{:S(2)}, u32[]{:S(2)}) %collective-permute-start.9) | collective-permute-done | bytes 1638432 | tf_op jit(solution)/shard_map/ppermute | solution.py:66
  185.8 31.1 %collective-permute-done.11 = bf16[160,6400]{1,0:T(8,128)(2,1)} collective-permute-done((bf16[160,6400]{1,0:T(8,128)(2,1)S(1)}, bf16[160,6400]{1,0:T(8,128)(2,1)}, u32[]{:S(2)}, u32[]{:S(2)}) %collective-permute-start.11) | collective-permute-done | bytes 2048032 | tf_op jit(solution)/shard_map/ppermute | solution.py:66
  230.6 19.0 %all_gather.23 = bf16[1024,288]{1,0:T(8,128)(2,1)S(1)} all-gather(bf16[256,288]{1,0:T(8,128)(2,1)S(1)} %pad_maximum_fusion.12), channel_id=1, replica_groups=mesh['dp'=8,'own'=4] {'own'}, dimensions={0}, use_global_device_ids=true | all-gather | bytes 737280 | tf_op jit(solution)/shard_map/all_gather | solution.py:356
  250.9 30.9 %collective-permute-done.12 = bf16[320,2560]{1,0:T(8,128)(2,1)S(1)} collective-permute-done((bf16[320,2560]{1,0:T(8,128)(2,1)}, bf16[320,2560]{1,0:T(8,128)(2,1)S(1)}, u32[]{:S(2)}, u32[]{:S(2)}) %collective-permute-start.12) | collective-permute-done | bytes 1638432 | tf_op jit(solution)/shard_map/ppermute | solution.py:74
  303.5 25.4 %collective-permute-done.14 = bf16[160,6400]{1,0:T(8,128)(2,1)} collective-permute-done((bf16[160,6400]{1,0:T(8,128)(2,1)}, bf16[160,6400]{1,0:T(8,128)(2,1)}, u32[]{:S(2)}, u32[]{:S(2)}) %collective-permute-start.14) | collective-permute-done | bytes 2048032 | tf_op jit(solution)/shard_map/ppermute | solution.py:66
  351.5 36.8 %shard_map.518 = (bf16[2560,256]{1,0:T(8,128)(2,1)S(1)}, f32[40,1,256]{2,1,0:T(1,128)S(1)}) custom-call(bf16[3840,256]{1,0:T(8,128)(2,1)S(1)} %bitcast.304, bf16[1024,5120]{1,0:T(8,128)(2,1)} %convolution_convert_fusion.3.kv_ref, bf16[1024,128]{1,0:T(8,128)(2,1)S(1)} %pad.14.rope_ref, f32[1024,256]{1,0:T(8,128)S(1)} %compare_select_fusion.bias_ref), custom_call_target="tpu_custom_call" | custom-call | tf_op jit(solution)/shard_map/pallas_call | solution.py:175
  407.4 28.7 %collective-permute-done.18 = bf16[160,6400]{1,0:T(8,128)(2,1)S(1)} collective-permute-done((bf16[160,6400]{1,0:T(8,128)(2,1)S(1)}, bf16[160,6400]{1,0:T(8,128)(2,1)S(1)}, u32[]{:S(2)}, u32[]{:S(2)}) %collective-permute-start.18) | collective-permute-done | bytes 2048032 | tf_op jit(solution)/shard_map/ppermute | solution.py:74
  470.6 31.4 %collective-permute-done.23 = bf16[400,2560]{1,0:T(8,128)(2,1)S(1)} collective-permute-done((bf16[400,2560]{1,0:T(8,128)(2,1)S(1)}, bf16[400,2560]{1,0:T(8,128)(2,1)S(1)}, u32[]{:S(2)}, u32[]{:S(2)}) %collective-permute-start.23) | collective-permute-done | bytes 2048032 | tf_op jit(solution)/shard_map/ppermute | solution.py:66
  526.5 19.7 %collective-permute-done.26 = bf16[400,2560]{1,0:T(8,128)(2,1)S(1)} collective-permute-done((bf16[400,2560]{1,0:T(8,128)(2,1)S(1)}, bf16[400,2560]{1,0:T(8,128)(2,1)S(1)}, u32[]{:S(2)}, u32[]{:S(2)}) %collective-permute-start.26) | collective-permute-done | bytes 2048032 | tf_op jit(solution)/shard_map/ppermute | solution.py:66
  615.9 19.6 %all-to-all-done = bf16[320,8,800]{2,0,1:T(8,128)(2,1)} async-done(((bf16[320,8,800]{2,0,1:T(8,128)(2,1)}), bf16[320,8,800]{2,0,1:T(8,128)(2,1)}, u32[]{:S(2)}, u32[]{:S(2)}) %all-to-all-start) | async-done | bytes 4096032 | tf_op jit(solution)/shard_map/all_to_all | solution.py:390
  660.9 32.6 %all-to-all-done.1 = bf16[320,8,800]{2,0,1:T(8,128)(2,1)} async-done(((bf16[320,8,800]{2,0,1:T(8,128)(2,1)}), bf16[320,8,800]{2,0,1:T(8,128)(2,1)}, u32[]{:S(2)}, u32[]{:S(2)}) %all-to-all-start.1) | async-done | bytes 4096032 | tf_op jit(solution)/shard_map/all_to_all | solution.py:400
  693.5 14.6 fusion.102
  708.1 19.4 %multiply_convert_fusion = (bf16[2048,800]{0,1:T(8,128)(2,1)}, bf16[2048,800]{0,1:T(8,128)(2,1)}, bf16[2048,800]{0,1:T(8,128)(2,1)}) fusion(f32[2048,800]{0,1:T(8,128)} %fusion.101, f32[2048,800]{0,1:T(8,128)} %fusion.102, bf16[2048,2560]{1,0:T(8,128)(2,1)} %all-gather.17.cloned.1.call-done, bf16[400,2560]{1,0:T(8,128)(2,1)} %broadcast_select_fusion, ...), kind=kOutput, calls=%fused_computation.27 | convolution fusion | flops 8421376000 | bytes 37519360 | tf_op jit(solution)/shard_map/dot_general | solution.py:148
  727.5 18.1 %fusion.103 = f32[2048,2560]{1,0:T(8,128)} fusion(bf16[2048,800]{0,1:T(8,128)(2,1)} %get-tuple-element.154, bf16[2560,800]{1,0:T(8,128)(2,1)} %bitcast.25), kind=kOutput, calls=%fused_computation.263 | convolution fusion | flops 8388608000 | bytes 28344320 | tf_op jit(solution)/shard_map/dot_general | solution.py:148
  745.6 19.6 %add_convert_fusion = bf16[2048,2560]{1,0:T(8,128)(2,1)} fusion(f32[2048,2560]{1,0:T(8,128)} %fusion.103, bf16[2048,800]{0,1:T(8,128)(2,1)} %get-tuple-element.157, bf16[2560,800]{1,0:T(8,128)(2,1)} %bitcast.30), kind=kOutput, calls=%fused_computation | convolution fusion | flops 8399093760 | bytes 38830080 | tf_op jit(solution)/shard_map/dot_general | solution.py:148
  783.6 18.8 %collective-permute-done.30 = bf16[200,2560]{1,0:T(8,128)(2,1)S(1)} collective-permute-done((bf16[200,2560]{1,0:T(8,128)(2,1)S(1)}, bf16[200,2560]{1,0:T(8,128)(2,1)S(1)}, u32[]{:S(2)}, u32[]{:S(2)}) %collective-permute-start.30) | collective-permute-done | bytes 1024032 | tf_op jit(solution)/shard_map/ppermute | solution.py:66
  812.0 17.5 %collective-permute-done.32 = bf16[200,2560]{1,0:T(8,128)(2,1)S(1)} collective-permute-done((bf16[200,2560]{1,0:T(8,128)(2,1)S(1)}, bf16[200,2560]{1,0:T(8,128)(2,1)S(1)}, u32[]{:S(2)}, u32[]{:S(2)}) %collective-permute-start.32) | collective-permute-done | bytes 1024032 | tf_op jit(solution)/shard_map/ppermute | solution.py:66
  897.5 24.4 %all-to-all-done.2 = bf16[8,320,800]{2,1,0:T(8,128)(2,1)} async-done(((bf16[8,320,800]{2,1,0:T(8,128)(2,1)}), bf16[8,320,800]{2,1,0:T(8,128)(2,1)}, u32[]{:S(2)}, u32[]{:S(2)}) %all-to-all-start.2) | async-done | bytes 4096032 | tf_op jit(solution)/shard_map/all_to_all | solution.py:428
  956.8 27.0 %collective-permute-done.40 = bf16[160,6400]{1,0:T(8,128)(2,1)} collective-permute-done((bf16[160,6400]{1,0:T(8,128)(2,1)S(1)}, bf16[160,6400]{1,0:T(8,128)(2,1)}, u32[]{:S(2)}, u32[]{:S(2)}) %collective-permute-start.40) | collective-permute-done | bytes 2048032 | tf_op jit(solution)/shard_map/ppermute | solution.py:66
  1016.7 49.4 %shard_map.519 = (bf16[3840,256]{1,0:T(8,128)(2,1)S(1)}, bf16[1024,5120]{1,0:T(8,128)(2,1)}, f32[1024,128]{1,0:T(8,128)S(1)}) custom-call(bf16[3840,256]{1,0:T(8,128)(2,1)} %bitcast.305, bf16[1024,5120]{1,0:T(8,128)(2,1)} %convolution_convert_fusion.3.kv_ref, bf16[1024,128]{1,0:T(8,128)(2,1)S(1)} %pad.14.rope_ref, ...), custom_call_target="tpu_custom_call" | custom-call | tf_op jit(solution)/shard_map/pallas_call | solution.py:222
  1084.5 64.5 %all_to_all.70 = bf16[8,320,800]{2,1,0:T(8,128)(2,1)S(1)} all-to-all(bf16[8,320,800]{2,1,0:T(8,128)(2,1)} %bitcast.310), channel_id=1, replica_groups=mesh['dp'=8,'own'=4] {'dp'}, dimensions={0} | all-to-all | bytes 8192000 | tf_op jit(solution)/shard_map/all_to_all | solution.py:433
  1190.1 21.2 %collective-permute-done.46 = bf16[160,6400]{1,0:T(8,128)(2,1)} collective-permute-done((bf16[160,6400]{1,0:T(8,128)(2,1)}, bf16[160,6400]{1,0:T(8,128)(2,1)}, u32[]{:S(2)}, u32[]{:S(2)}) %collective-permute-start.46) | collective-permute-done | bytes 2048032 | tf_op jit(solution)/shard_map/ppermute | solution.py:66
  1251.3 16.5 %convolution_convert_fusion.2 = bf16[2048,2560]{1,0:T(8,128)(2,1)} fusion(bf16[2048,800]{0,1:T(8,128)(2,1)} %get-tuple-element.391, bf16[400,2560]{1,0:T(8,128)(2,1)} %broadcast_select_fusion, bf16[400,2560]{1,0:T(8,128)(2,1)} %broadcast_select_fusion.1), kind=kOutput, calls=%fused_computation.9 | convolution fusion | flops 8402042880 | bytes 17858560 | tf_op jit(solution)/shard_map/dot_general | solution.py:497
  1305.0 17.5 %fusion.3 = (f32[1,800,2560]{2,1,0:T(8,128)}, f32[1,800,2560]{2,1,0:T(8,128)}, f32[1,800,2560]{2,1,0:T(8,128)}) fusion(f32[1,800,2560]{2,1,0:T(8,128)} %param.58, pred[]{:T(512)S(6)} %eq.32, bf16[1,200,2560]{2,1,0:T(8,128)(2,1)S(1)} %select_bitcast_fusion.4, bf16[1,200,2560]{2,1,0:T(8,128)(2,1)S(1)} %select_bitcast_fusion.5, ...), kind=kLoop, calls=%fused_computation.18 | loop fusion | flops 51200000 | bytes 53248000 | tf_op jit(solution)/shard_map/jit(_where)/select_n | solution.py:258
  1327.3 17.2 %collective-permute-done.50 = bf16[160,6400]{1,0:T(8,128)(2,1)S(1)} collective-permute-done((bf16[160,6400]{1,0:T(8,128)(2,1)}, bf16[160,6400]{1,0:T(8,128)(2,1)S(1)}, u32[]{:S(2)}, u32[]{:S(2)}) %collective-permute-start.50) | collective-permute-done | bytes 2048032 | tf_op jit(solution)/shard_map/ppermute | solution.py:66
  1367.7 26.1 %collective-permute-done.52 = bf16[320,2560]{1,0:T(8,128)(2,1)S(1)} collective-permute-done((bf16[320,2560]{1,0:T(8,128)(2,1)}, bf16[320,2560]{1,0:T(8,128)(2,1)S(1)}, u32[]{:S(2)}, u32[]{:S(2)}) %collective-permute-start.52) | collective-permute-done | bytes 1638432 | tf_op jit(solution)/shard_map/ppermute | solution.py:66
  1409.1 21.5 %fusion.5 = (f32[1,320,6400]{2,1,0:T(8,128)}, f32[1,320,6400]{2,1,0:T(8,128)}, f32[1,320,6400]{2,1,0:T(8,128)}) fusion(f32[1,320,6400]{2,1,0:T(8,128)} %param.52, pred[]{:T(512)S(6)} %eq.30, bf16[1,160,6400]{2,1,0:T(8,128)(2,1)} %select_bitcast_fusion.2, bf16[1,160,6400]{2,1,0:T(8,128)(2,1)} %select_bitcast_fusion.3, f32[1,320,6400]{2,1,0:T(8,128)} %param.50, ...), kind=kLoop, calls=%fused_computation.22 | loop fusion | flops 43008000 | bytes 53248000 | tf_op jit(solution)/shard_map/jit(_where)/select_n | solution.py:258
  1471.1 16.0 %collective-permute-start.60 = (bf16[320,1059]{1,0:T(8,128)(2,1)}, bf16[320,1059]{1,0:T(8,128)(2,1)S(1)}, u32[]{:S(2)}, u32[]{:S(2)}) collective-permute-start(bf16[320,1059]{1,0:T(8,128)(2,1)} %copy.204), channel_id=1, source_target_pairs={{0,1},{3,2},{4,5},{7,6},{8,9},{11,10},{12,13},{15,14},{16,17},{19,... | collective-permute-start | bytes 2033288 | tf_op jit(solution)/shard_map/ppermute | solution.py:66
  1492.0 19.2 %fusion.4 = (f32[1,320,6400]{2,1,0:T(8,128)}, f32[1,320,6400]{2,1,0:T(8,128)}, f32[1,320,6400]{2,1,0:T(8,128)}) fusion(f32[1,320,6400]{2,1,0:T(8,128)} %param.55, pred[]{:T(512)S(6)} %eq.31, bf16[1,160,6400]{2,1,0:T(8,128)(2,1)} %select_bitcast_fusion, bf16[1,160,6400]{2,1,0:T(8,128)(2,1)} %select_bitcast_fusion.1, f32[1,320,6400]{2,1,0:T(8,128)} %param.53, ...), kind=kLoop, calls=%fused_computation.20 | loop fusion | flops 43008000 | bytes 53248000 | tf_op jit(solution)/shard_map/jit(_where)/select_n | solution.py:258
  (597 shorter events, 768.9 us)
Async XLA Ops:
  7.2 212.3 %all-gather.9.cloned.1.call-start = ((), (), s32[]{:S(2)}) async-start(), calls=%async_computation.12 | async-start | bytes 6635520 | tf_op jit(solution)/shard_map/all_gather | solution.py:92
  89.2 207.1 %all-gather.11.cloned.1.call-start = ((), (), s32[]{:S(2)}) async-start(), calls=%async_computation.13 | async-start | bytes 2949120 | tf_op jit(solution)/shard_map/all_gather | solution.py:92
  121.8 224.5 %all-gather.7.cloned.1.call-start = ((), (), s32[]{:S(2)}) async-start(), calls=%async_computation.11 | async-start | bytes 6635520 | tf_op jit(solution)/shard_map/all_gather | solution.py:92
  138.9 301.2 %all-gather.13.cloned.1.call-start = ((), (), s32[]{:S(2)}) async-start(), calls=%async_computation.14 | async-start | bytes 14745600 | tf_op jit(solution)/shard_map/all_gather | solution.py:92
  283.2 363.2 %all-gather.15.cloned.1.call-start = ((), (), s32[]{:S(2)}) async-start(), calls=%async_computation.15 | async-start | bytes 11796480 | tf_op jit(solution)/shard_map/all_gather | solution.py:92
  336.3 52.0 %collective-permute-start.15 = (bf16[160,6400]{1,0:T(8,128)(2,1)}, bf16[160,6400]{1,0:T(8,128)(2,1)}, u32[]{:S(2)}, u32[]{:S(2)}) collective-permute-start(bf16[160,6400]{1,0:T(8,128)(2,1)} %add.401), channel_id=1, source_target_pairs={{1,2},{2,1},{5,6},{6,5},{9,10},{10,9},{13,14},{14,13},{17,18},{18,... | collective-permute-start | bytes 6144008 | tf_op jit(solution)/shard_map/ppermute | solution.py:69
  338.2 53.2 %collective-permute-start.16 = (bf16[160,6400]{1,0:T(8,128)(2,1)}, bf16[160,6400]{1,0:T(8,128)(2,1)}, u32[]{:S(2)}, u32[]{:S(2)}) collective-permute-start(bf16[160,6400]{1,0:T(8,128)(2,1)} %get-tuple-element.134), channel_id=1, source_target_pairs={{0,1},{3,2},{4,5},{7,6},{8,9},{11,10},{12,13},{15,14},{16,17},{19,... | collective-permute-start | bytes 6144008 | tf_op jit(solution)/shard_map/ppermute | solution.py:66
  344.3 50.7 %collective-permute-start.17 = (bf16[160,6400]{1,0:T(8,128)(2,1)}, bf16[160,6400]{1,0:T(8,128)(2,1)}, u32[]{:S(2)}, u32[]{:S(2)}) collective-permute-start(bf16[160,6400]{1,0:T(8,128)(2,1)} %add.400), channel_id=1, source_target_pairs={{1,0},{2,3},{5,4},{6,7},{9,8},{10,11},{13,12},{14,15},{17,16},{18,... | collective-permute-start | bytes 6144008 | tf_op jit(solution)/shard_map/ppermute | solution.py:74
  452.2 255.9 %all-gather.17.cloned.1.call-start = ((), (), s32[]{:S(2)}) async-start(), calls=%async_computation.16 | async-start | bytes 11796480 | tf_op jit(solution)/shard_map/all_gather | solution.py:92
  577.6 57.9 %all-to-all-start = ((bf16[320,8,800]{2,0,1:T(8,128)(2,1)}), bf16[320,8,800]{2,0,1:T(8,128)(2,1)}, u32[]{:S(2)}, u32[]{:S(2)}) async-start(bf16[320,8,800]{2,0,1:T(8,128)(2,1)} %copy.188), calls=%async_computation | async-start | bytes 9175040 | tf_op jit(solution)/shard_map/all_to_all | solution.py:390
  596.4 46.9 %collective-permute-start.29 = (bf16[400,2560]{1,0:T(8,128)(2,1)S(1)}, bf16[400,2560]{1,0:T(8,128)(2,1)}, u32[]{:S(2)}, u32[]{:S(2)}) collective-permute-start(bf16[400,2560]{1,0:T(8,128)(2,1)S(1)} %add.413), channel_id=1, source_target_pairs={{1,0},{2,3},{5,4},{6,7},{9,8},{10,11},{13,12},{14,15},{17,16},{18,... | collective-permute-start | bytes 6144008 | tf_op jit(solution)/shard_map/ppermute | solution.py:74
  635.5 57.9 %all-to-all-start.1 = ((bf16[320,8,800]{2,0,1:T(8,128)(2,1)}), bf16[320,8,800]{2,0,1:T(8,128)(2,1)}, u32[]{:S(2)}, u32[]{:S(2)}) async-start(bf16[320,8,800]{2,0,1:T(8,128)(2,1)} %copy.189), calls=%async_computation.1 | async-start | bytes 9175040 | tf_op jit(solution)/shard_map/all_to_all | solution.py:400
  640.1 347.0 %reduce-scatter.10.cloned.1.call-start = ((), (), s32[]{:S(2)}) async-start(), calls=%async_computation.17 | async-start | bytes 11796480 | tf_op jit(solution)/shard_map/reduce_scatter | solution.py:96
  860.2 61.8 %all-to-all-start.2 = ((bf16[8,320,800]{2,1,0:T(8,128)(2,1)}), bf16[8,320,800]{2,1,0:T(8,128)(2,1)}, u32[]{:S(2)}, u32[]{:S(2)}) async-start(bf16[8,320,800]{2,1,0:T(8,128)(2,1)} %bitcast.308), calls=%async_computation.2 | async-start | bytes 9175040 | tf_op jit(solution)/shard_map/all_to_all | solution.py:428
  868.5 309.3 %reduce-scatter.12.cloned.1.call-start = ((), (), s32[]{:S(2)}) async-start(), calls=%async_computation.18 | async-start | bytes 983040 | tf_op jit(solution)/shard_map/reduce_scatter | solution.py:454
  888.2 46.5 %collective-permute-start.37 = (bf16[200,2560]{1,0:T(8,128)(2,1)}, bf16[200,2560]{1,0:T(8,128)(2,1)}, u32[]{:S(2)}, u32[]{:S(2)}) collective-permute-start(bf16[200,2560]{1,0:T(8,128)(2,1)} %get-tuple-element.159), channel_id=1, source_target_pairs={{0,1},{3,2},{4,5},{7,6},{8,9},{11,10},{12,13},{15,14},{16,17},{19,... | collective-permute-start | bytes 3072008 | tf_op jit(solution)/shard_map/ppermute | solution.py:66
  937.4 46.3 %collective-permute-start.40 = (bf16[160,6400]{1,0:T(8,128)(2,1)S(1)}, bf16[160,6400]{1,0:T(8,128)(2,1)}, u32[]{:S(2)}, u32[]{:S(2)}) collective-permute-start(bf16[160,6400]{1,0:T(8,128)(2,1)S(1)} %split.87), channel_id=1, source_target_pairs={{0,1},{3,2},{4,5},{7,6},{8,9},{11,10},{12,13},{15,14},{16,17},{19,... | collective-permute-start | bytes 6144008 | tf_op jit(solution)/shard_map/ppermute | solution.py:66
  1007.5 58.7 %collective-permute-start.42 = (bf16[160,6400]{1,0:T(8,128)(2,1)}, bf16[160,6400]{1,0:T(8,128)(2,1)S(1)}, u32[]{:S(2)}, u32[]{:S(2)}) collective-permute-start(bf16[160,6400]{1,0:T(8,128)(2,1)} %add.424), channel_id=1, source_target_pairs={{1,2},{2,1},{5,6},{6,5},{9,10},{10,9},{13,14},{14,13},{17,18},{18,... | collective-permute-start | bytes 6144008 | tf_op jit(solution)/shard_map/ppermute | solution.py:69
  1008.2 57.9 %collective-permute-start.43 = (bf16[160,6400]{1,0:T(8,128)(2,1)}, bf16[160,6400]{1,0:T(8,128)(2,1)S(1)}, u32[]{:S(2)}, u32[]{:S(2)}) collective-permute-start(bf16[160,6400]{1,0:T(8,128)(2,1)} %split.89), channel_id=1, source_target_pairs={{0,1},{3,2},{4,5},{7,6},{8,9},{11,10},{12,13},{15,14},{16,17},{19,... | collective-permute-start | bytes 6144008 | tf_op jit(solution)/shard_map/ppermute | solution.py:66
  1015.3 50.8 %collective-permute-start.44 = (bf16[200,2560]{1,0:T(8,128)(2,1)}, bf16[200,2560]{1,0:T(8,128)(2,1)S(1)}, u32[]{:S(2)}, u32[]{:S(2)}) collective-permute-start(bf16[200,2560]{1,0:T(8,128)(2,1)} %add.423), channel_id=1, source_target_pairs={{1,0},{2,3},{5,4},{6,7},{9,8},{10,11},{13,12},{14,15},{17,16},{18,... | collective-permute-start | bytes 3072008 | tf_op jit(solution)/shard_map/ppermute | solution.py:74
  1076.5 271.4 %reduce-scatter.16.cloned.1.call-start = ((), (), s32[]{:S(2)}) async-start(), calls=%async_computation.20 | async-start | bytes 14745600 | tf_op jit(solution)/shard_map/reduce_scatter | solution.py:96
  1077.2 289.0 %reduce-scatter.22.cloned.1.call-start = ((), (), s32[]{:S(2)}) async-start(), calls=%async_computation.23 | async-start | bytes 6635520
  1162.3 49.0 %collective-permute-start.46 = (bf16[160,6400]{1,0:T(8,128)(2,1)}, bf16[160,6400]{1,0:T(8,128)(2,1)}, u32[]{:S(2)}, u32[]{:S(2)}) collective-permute-start(bf16[160,6400]{1,0:T(8,128)(2,1)} %split.91), channel_id=1, source_target_pairs={{0,1},{3,2},{4,5},{7,6},{8,9},{11,10},{12,13},{15,14},{16,17},{19,... | collective-permute-start | bytes 6144008 | tf_op jit(solution)/shard_map/ppermute | solution.py:66
  1170.1 46.7 %collective-permute-start.47 = (bf16[160,6400]{1,0:T(8,128)(2,1)}, bf16[160,6400]{1,0:T(8,128)(2,1)}, u32[]{:S(2)}, u32[]{:S(2)}) collective-permute-start(bf16[160,6400]{1,0:T(8,128)(2,1)} %add.426), channel_id=1, source_target_pairs={{1,0},{2,3},{5,4},{6,7},{9,8},{10,11},{13,12},{14,15},{17,16},{18,... | collective-permute-start | bytes 6144008 | tf_op jit(solution)/shard_map/ppermute | solution.py:74
  1237.8 162.4 %reduce-scatter.18.cloned.1.call-start = ((), (), s32[]{:S(2)}) async-start(), calls=%async_computation.21 | async-start | bytes 2949120 | tf_op jit(solution)/shard_map/reduce_scatter | solution.py:96
  1251.1 156.5 %reduce-scatter.20.cloned.1.call-start = ((), (), s32[]{:S(2)}) async-start(), calls=%async_computation.22 | async-start | bytes 6635520 | tf_op jit(solution)/shard_map/reduce_scatter | solution.py:96
  1276.8 298.7 %reduce-scatter.14.cloned.1.call-start = ((), (), s32[]{:S(2)}) async-start(), calls=%async_computation.19 | async-start | bytes 11796480 | tf_op jit(solution)/shard_map/reduce_scatter | solution.py:96
  1293.4 54.5 %collective-permute-start.48 = (bf16[160,6400]{1,0:T(8,128)(2,1)S(1)}, bf16[160,6400]{1,0:T(8,128)(2,1)}, u32[]{:S(2)}, u32[]{:S(2)}) collective-permute-start(bf16[160,6400]{1,0:T(8,128)(2,1)S(1)} %add.428), channel_id=1, source_target_pairs={{1,0},{2,3},{5,4},{6,7},{9,8},{10,11},{13,12},{14,15},{17,16},{18,... | collective-permute-start | bytes 6144008 | tf_op jit(solution)/shard_map/ppermute | solution.py:74
  1295.5 49.0 %collective-permute-start.50 = (bf16[160,6400]{1,0:T(8,128)(2,1)}, bf16[160,6400]{1,0:T(8,128)(2,1)S(1)}, u32[]{:S(2)}, u32[]{:S(2)}) collective-permute-start(bf16[160,6400]{1,0:T(8,128)(2,1)} %split.93), channel_id=1, source_target_pairs={{0,1},{3,2},{4,5},{7,6},{8,9},{11,10},{12,13},{15,14},{16,17},{19,... | collective-permute-start | bytes 6144008 | tf_op jit(solution)/shard_map/ppermute | solution.py:66
  1347.9 49.0 %collective-permute-start.51 = (bf16[160,6400]{1,0:T(8,128)(2,1)}, bf16[160,6400]{1,0:T(8,128)(2,1)}, u32[]{:S(2)}, u32[]{:S(2)}) collective-permute-start(bf16[160,6400]{1,0:T(8,128)(2,1)} %add.434), channel_id=1, source_target_pairs={{1,2},{2,1},{5,6},{6,5},{9,10},{10,9},{13,14},{14,13},{17,18},{18,... | collective-permute-start | bytes 6144008 | tf_op jit(solution)/shard_map/ppermute | solution.py:69
  1349.9 57.6 %collective-permute-start.53 = (bf16[160,6400]{1,0:T(8,128)(2,1)}, bf16[160,6400]{1,0:T(8,128)(2,1)}, u32[]{:S(2)}, u32[]{:S(2)}) collective-permute-start(bf16[160,6400]{1,0:T(8,128)(2,1)} %add.433), channel_id=1, source_target_pairs={{1,0},{2,3},{5,4},{6,7},{9,8},{10,11},{13,12},{14,15},{17,16},{18,... | collective-permute-start | bytes 6144008 | tf_op jit(solution)/shard_map/ppermute | solution.py:74
  1407.5 60.1 %collective-permute-start.57 = (bf16[160,6400]{1,0:T(8,128)(2,1)}, bf16[160,6400]{1,0:T(8,128)(2,1)}, u32[]{:S(2)}, u32[]{:S(2)}) collective-permute-start(bf16[160,6400]{1,0:T(8,128)(2,1)} %add.435), channel_id=1, source_target_pairs={{1,0},{2,3},{5,4},{6,7},{9,8},{10,11},{13,12},{14,15},{17,16},{18,... | collective-permute-start | bytes 6144008 | tf_op jit(solution)/shard_map/ppermute | solution.py:74
  (168 other events, 3798.6 us)
Sparse Core Ops, SparseCore 0:
  89.3 43.9 all-gather.8
  135.8 30.1 all-gather.10
  168.4 43.8 all-gather.6
  283.4 75.4 all-gather.12
  452.3 64.3 all-gather.14
  519.0 63.2 all-gather.16
  765.4 82.0 reduce-scatter.9
  1076.6 24.9 reduce-scatter.11
  1105.2 99.7 reduce-scatter.15
  1237.9 58.4 reduce-scatter.21
  1300.2 43.6 reduce-scatter.17
  1347.9 59.6 reduce-scatter.19
  1411.0 81.5 reduce-scatter.13

commit v2 on v1

--- a/solution.py
+++ b/solution.py
@@ -15,6 +15,7 @@
 QR = 768
 KVR = 256
 FF = 6400
+GAINS = 6144
 HEADS_STEP = 2
 LANES = 128
 STEP = 7
@@ -53,35 +54,54 @@
         self.active = []
         self.arrived = []
 
-    def round(self, *new, after=()):
-        last, half = self.count - 1, self.count // 2
+    def begin(self, *new):
         self.active.extend(new)
         values = [piece.value for piece in self.active]
-        if self.arrived or after:
-            values = lax.optimization_barrier((*values, *self.arrived, *after))
-        self.arrived = []
+        if self.arrived:
+            values = lax.optimization_barrier((*values, *self.arrived))
         for piece, value in zip(self.active, values):
-            if piece.leg < half - 1:
-                hop = piece.leg
-                landed = lax.ppermute(value, "own", [(hop, hop + 1), (last - hop, last - hop - 1)])
-                piece.value = value + landed
-            elif piece.leg == half - 1:
-                landed = lax.ppermute(value, "own", [(half - 1, half), (half, half - 1)])
-                piece.value = value + landed
+            piece.value = value
+        self.coming = [
+            lax.ppermute(piece.value, "own", self.pairs(piece.leg)) for piece in self.active
+        ]
+
+    def finish(self, *inside):
+        last, half = self.count - 1, self.count // 2
+        self.arrived = list(lax.optimization_barrier(tuple(self.coming)))
+        for piece, arrived in zip(self.active, self.arrived):
+            value = tied(piece.value, *inside) if inside else piece.value
+            if piece.leg < half:
+                piece.value = value + arrived
             else:
-                outer = 2 * half - 2 - piece.leg
-                inner = outer + 1
-                landed = lax.ppermute(
-                    value, "own", [(inner, outer), (last - inner, last - outer)]
-                )
+                outer = last - 1 - piece.leg
                 ended = (self.place == outer) | (self.place == last - outer)
-                piece.value = jnp.where(ended, landed, value)
+                piece.value = jnp.where(ended, arrived, value)
             piece.leg += 1
-            self.arrived.append(landed)
-        self.active = [piece for piece in self.active if piece.leg < self.count - 1]
+        self.active = [piece for piece in self.active if piece.leg < last]
+
+    def round(self, *new):
+        self.begin(*new)
+        self.finish()
+
+    def pairs(self, leg):
+        last, half = self.count - 1, self.count // 2
+        if leg == half - 1:
+            return [(half - 1, half), (half, half - 1)]
+        near, far = (leg, leg + 1) if leg < half else (last - leg, last - 1 - leg)
+        return [(near, far), (last - near, last - far)]
 
     def then(self, value):
         return tied(value, *self.arrived)
+
+
+def shuffled(columns):
+    shares = lax.axis_size("dp")
+    blocks = columns.reshape(shares, columns.shape[0] // shares, columns.shape[1])
+    return lax.all_to_all(blocks, "dp", 0, 0)
+
+
+def joined(blocks):
+    return blocks.transpose(1, 0, 2).reshape(blocks.shape[1], -1)
 
 
 def rows_of(pieces):
@@ -170,14 +190,14 @@
         out_ref[head*VD:(head+1)*VD,:]=out[NOPE:].astype(out_ref.dtype)
         log_ref[head]=peak+jnp.log(total)
 
-def attend(query,kv,rope,bias):
+def attend(query,kv,rope,bias,first,heads):
     tokens=query.shape[1]; length=kv.shape[0]
     return pl.pallas_call(
         attend_kernel,
-        grid=(H//HEADS_STEP,),
+        grid=(heads//HEADS_STEP,),
         in_specs=[
-            pl.BlockSpec((HEADS_STEP*(NOPE+ROPE),tokens),lambda i:(i,0)),
-            pl.BlockSpec((length,HEADS_STEP*(NOPE+VD)),lambda i:(0,i)),
+            pl.BlockSpec((HEADS_STEP*(NOPE+ROPE),tokens),lambda i:(i+first//HEADS_STEP,0)),
+            pl.BlockSpec((length,HEADS_STEP*(NOPE+VD)),lambda i:(0,i+first//HEADS_STEP)),
             pl.BlockSpec((length,128),lambda i:(0,0)),
             pl.BlockSpec((length,tokens),lambda i:(0,0)),
         ],
@@ -185,7 +205,7 @@
             pl.BlockSpec((HEADS_STEP*VD,tokens),lambda i:(i,0)),
             pl.BlockSpec((HEADS_STEP,1,tokens),lambda i:(i,0,0)),
         ],
-        out_shape=[jax.ShapeDtypeStruct((H*VD,tokens),jnp.bfloat16),jax.ShapeDtypeStruct((H,1,tokens),jnp.float32)],
+        out_shape=[jax.ShapeDtypeStruct((heads*VD,tokens),jnp.bfloat16),jax.ShapeDtypeStruct((heads,1,tokens),jnp.float32)],
         compiler_params=pltpu.CompilerParams(vmem_limit_bytes=48*1024*1024),
     )(query,kv,rope,bias)
 
@@ -323,13 +343,12 @@
     )
     line.round(down_latents)
     line.round(query_up_rows, latent_up_rows)
-    line.round()
-    down_latents_all = gather_rows(down_latents.value)
     line.round(output_rows)
+    down_latents_all = gather_rows(tied(down_latents.value, grad_ffn_all))
+    line.round(gate_rows[0])
     query_up_all = gather_rows(query_up_rows.value)
     latent_up_all = gather_rows(latent_up_rows.value)
     down_latents_all = line.then(down_latents_all)
-    line.round(gate_rows[0])
     gains_float = down_latents_all[:, width:].reshape(-1, query_down.shape[1], gain_columns)
     gains_float = gains_float.transpose(0, 2, 1).reshape(-1, gain_columns * query_down.shape[1])
     gains_float = gains_float[:, :gain_count].reshape(-1).astype(jnp.float32)
@@ -356,8 +375,8 @@
     gathered_keys = lax.all_gather(
         jnp.concatenate([key_low, rope_low], axis=-1), "own", axis=0, tiled=True
     )
-    line.round(*gate_rows[1:], after=[gathered_keys])
-    output_all = gather_rows(output_rows.value)
+    gate_rows[-1].value = tied(gate_rows[-1].value, gathered_keys)
+    line.begin(*gate_rows[1:])
     gathered_latent = gathered_keys[:, :KVR]
     rope_keys = jnp.pad(gathered_keys[:, KVR:], ((0, 0), (0, LANES - ROPE)))
     query_raw = lax.dot_general(
@@ -377,63 +396,80 @@
     key_value = jnp.dot(gathered_latent, latent_up_all, preferred_element_type=jnp.float32).astype(
         low
     )
-    key_value, queries = line.then(key_value), line.then(queries)
-    line.round(up_rows[0], after=[key_value])
+    line.finish(key_value)
+    output_all = gather_rows(output_rows.value)
     sequence_blocks = block_index[0]
     query_blocks = lax.dynamic_slice_in_dim(
         sequence_blocks, own_place * tokens_here, tokens_here, 0
     )
     bias = jnp.where(sequence_blocks[:, None] <= query_blocks[None, :], 0.0, MASKED)
     bias = bias.astype(jnp.float32)
-    attended_low, logsum = attend(queries, key_value, rope_keys, bias)
-    line.round(*up_rows[1:], after=[attended_low])
-    gate_columns = lax.all_to_all(rows_of(gate_rows), "dp", 1, 0, tiled=True)
-    output_all = line.then(output_all)
+    half_heads = H // 2
+    line.begin(up_rows[0])
+    attended_first, logsum_first = attend(
+        queries, line.then(key_value), rope_keys, bias, 0, half_heads
+    )
+    line.finish(attended_first)
+    queries_second = line.then(queries)
+    line.begin(*up_rows[1:])
+    attended_second, logsum_second = attend(
+        queries_second, key_value, rope_keys, bias, half_heads, H - half_heads
+    )
+    line.finish(attended_second)
+    attended_low = line.then(jnp.concatenate([attended_first, attended_second], axis=0))
+    logsum = jnp.concatenate([logsum_first, logsum_second], axis=0)
+    line.begin(down_rows[0])
     branch = contract_rows(attended_low, output_all)
     middle = inputs + RESIDUAL_SCALE * branch
     normed_ffn, inverse_ffn = rms_forward(middle, gain_ffn)
 
     normed_ffn_low = normed_ffn.astype(low)
-    line.round(down_rows[0], after=[normed_ffn_low])
+    line.finish(normed_ffn_low)
     normed_ffn_all = gather_rows(normed_ffn_low)
-    line.round(*down_rows[1:])
-    up_columns = lax.all_to_all(rows_of(up_rows), "dp", 1, 0, tiled=True)
-    while line.active:
-        line.round()
+    normed_columns = lax.all_to_all(line.then(normed_low), "dp", 1, 0, tiled=True)
+    gate_rows = line.then(rows_of(gate_rows))
+    line.begin(*down_rows[1:])
+    gate_columns = lax.all_to_all(gate_rows, "dp", 1, 0, tiled=True)
+    line.finish()
+    line.begin()
+    up_columns = lax.all_to_all(line.then(rows_of(up_rows)), "dp", 1, 0, tiled=True)
+    line.finish(normed_ffn_all, gate_columns)
+    line.begin()
+    gate_pre = jnp.dot(
+        line.then(normed_ffn_all), gate_columns, preferred_element_type=jnp.float32
+    )
+    line.finish(gate_pre, up_columns)
     down_rows = rows_of(down_rows)
-    gate_pre = jnp.dot(normed_ffn_all, gate_columns, preferred_element_type=jnp.float32)
     up_pre = jnp.dot(normed_ffn_all, up_columns, preferred_element_type=jnp.float32)
     sigmoid_gate = jax.nn.sigmoid(gate_pre)
     silu_gate = gate_pre * sigmoid_gate
     activated_low = (silu_gate * up_pre).astype(low)
     down_part = contract_rows(activated_low, grad_ffn_all).astype(low)
     line = Line()
-    down_sum = pieces_of(down_part, 4)
-    line.round(down_sum[0])
-    grad_activated = times_transpose(grad_ffn_all, down_rows)
+    down_sum = pieces_of(down_part, 2)
+    line.begin(down_sum[0])
+    grad_activated = times_transpose(tied(grad_ffn_all, down_part), down_rows)
     grad_gate_pre = (
         grad_activated * up_pre * sigmoid_gate * (1.0 + gate_pre * (1.0 - sigmoid_gate))
     ).astype(low)
     grad_up_pre = (grad_activated * silu_gate).astype(low)
+    line.finish(grad_gate_pre, grad_up_pre)
+    grad_gate_pre = line.then(grad_gate_pre)
+    line.begin(*down_sum[1:2])
     grad_normed_ffn = (
         times_transpose(grad_gate_pre, gate_columns) + times_transpose(grad_up_pre, up_columns)
     ).astype(low)
-    grad_normed_ffn, grad_gate_pre, grad_up_pre = lax.optimization_barrier(
-        (grad_normed_ffn, grad_gate_pre, grad_up_pre)
-    )
+    gate_part = contract_rows(normed_ffn_all, tied(grad_gate_pre, grad_normed_ffn)).astype(low)
+    line.finish(grad_normed_ffn, gate_part)
     grad_normed_ffn = scatter_rows(grad_normed_ffn)
-    line.round(*down_sum[1:2])
-    gate_part = contract_rows(normed_ffn_all, grad_gate_pre).astype(low)
-    gate_part, grad_up_pre = lax.optimization_barrier((gate_part, grad_up_pre))
-    gate_part = lax.all_to_all(gate_part, "dp", 0, 1, tiled=True)
-    line.round(*down_sum[2:3])
+    gate_sum = pieces_of(gate_part, 2)
     grad_up_pre = line.then(grad_up_pre)
+    line.begin(gate_sum[0])
     up_part = contract_rows(normed_ffn_all, grad_up_pre).astype(low)
-    line.round(*down_sum[3:4], after=[up_part])
-    up_part = lax.all_to_all(tied(up_part, gate_part), "dp", 0, 1, tiled=True)
-    gate_sum = pieces_of(gate_part, 2)
-    line.round(gate_sum[0])
+    line.finish(up_part)
+    up_sum = pieces_of(up_part, 2)
     grad_normed_ffn = line.then(grad_normed_ffn)
+    line.begin(*gate_sum[1:])
 
     grad_middle_part, grad_gain_ffn = rms_backward(middle, inverse_ffn, gain_ffn, grad_normed_ffn)
     grad_middle = grad_output + grad_middle_part
@@ -442,32 +478,72 @@
     grad_attended = times_transpose(output_all, grad_branch).astype(low)
     grad_attended, output_part = lax.optimization_barrier((grad_attended, output_part))
     output_part = scatter_low(output_part)
-    line.round(*gate_sum[1:], after=[grad_attended])
+    line.finish(grad_attended)
+    queries_again = line.then(queries)
+    line.begin(up_sum[0])
     grad_query_raw, grad_key, grad_rope = attend_back(
-        queries, key_value, rope_keys, bias, logsum, grad_attended, cosine_rows, sine_rows
-    )
-    grad_key = line.then(grad_key)
-    up_sum = pieces_of(up_part, 2)
-    line.round(up_sum[0], after=[grad_query_raw])
-    latent_up_part = scatter_low(contract_rows(gathered_latent, grad_key).astype(low))
+        queries_again, key_value, rope_keys, bias, logsum, grad_attended, cosine_rows, sine_rows
+    )
+    line.finish(grad_query_raw)
+    grad_key, grad_query_raw = line.then(grad_key), line.then(grad_query_raw)
+    line.begin(*up_sum[1:])
+    states = (
+        (query_down, query_down_first, query_down_second),
+        (query_up, query_up_first, query_up_second),
+        (latent_down, latent_down_first, latent_down_second),
+        (latent_up, latent_up_first, latent_up_second),
+        (output_weight, output_weight_first, output_weight_second),
+        (gate_weight, gate_weight_first, gate_weight_second),
+        (up_weight, up_weight_first, up_weight_second),
+        (down_weight, down_weight_first, down_weight_second),
+        (norm_gains, norm_gains_first, norm_gains_second),
+    )
+    learn_rates = (
+        D ** (-0.5),
+        QR ** (-0.5),
+        D ** (-0.5),
+        KVR ** (-0.5),
+        math.sqrt(sequence_length / (0.0632 * H * VD)),
+        D ** (-0.5),
+        D ** (-0.5),
+        math.sqrt(1.0 / (0.0114 * FF)),
+        0.6,
+    )
+
+    def update(slot, gradient):
+        master, first_moment, second_moment = states[slot]
+        return adamw_update(
+            master[0],
+            first_moment[0],
+            second_moment[0],
+            gradient.astype(jnp.float32),
+            learn_rates[slot],
+            0.0 if slot == 8 else WEIGHT_DECAY,
+            is_owner[slot],
+        )
+
+    new_down = update(7, line.then(rows_of(down_sum)))
     key_side = jnp.concatenate([times_transpose(grad_key, latent_up_all), grad_rope[:, :ROPE]], axis=-1)
     key_side = lax.psum_scatter(
-        key_side.astype(low), "own", scatter_dimension=0, tiled=True
+        tied(key_side.astype(low), output_part), "own", scatter_dimension=0, tiled=True
     ).astype(jnp.float32)
-    query_up_part = scatter_low(
-        lax.dot_general(
-            query_low,
-            grad_query_raw,
-            (((0,), (1,)), ((), ())),
-            preferred_element_type=jnp.float32,
-        ).astype(low)
-    )
+    latent_up_part = contract_rows(gathered_latent, grad_key).astype(low)
+    query_up_part = lax.dot_general(
+        query_low, grad_query_raw, (((0,), (1,)), ((), ())), preferred_element_type=jnp.float32
+    ).astype(low)
+    latent_up_part, query_up_part = scatter_low(latent_up_part), scatter_low(query_up_part)
     grad_query_normed = lax.dot_general(
         grad_query_raw, query_up_all, (((0,), (1,)), ((), ())), preferred_element_type=jnp.float32
     )
     grad_query_latent, grad_gain_query = rms_backward(
         query_latent, inverse_query, gain_query, grad_query_normed
     )
+    line.finish(grad_query_latent, *new_down)
+    output_sum = Piece(output_part)
+    line.begin(output_sum)
+    gate_blocks = shuffled(rows_of(gate_sum))
+    line.finish()
+    key_side = line.then(key_side)
     grad_key_latent, grad_gain_latent = rms_backward(
         key_latent[:, :KVR], inverse_key, gain_latent, key_side[:, :KVR]
     )
@@ -475,38 +551,49 @@
         [grad_query_latent, grad_key_latent, unrotate(key_side[:, KVR:], cosine, sine_table)],
         axis=-1,
     ).astype(low)
-    grad_latents = line.then(grad_latents)
     grad_normed = times_transpose(grad_latents, down_latents_all)
     grad_inputs, grad_gain_input = rms_backward(inputs, inverse_input, gain_input, grad_normed)
     input_grad = (grad_middle + grad_inputs).astype(low)
+    gain_width = -(-GAINS // tokens_here)
     grad_gains = jnp.concatenate(
         [grad_gain_input, grad_gain_query, grad_gain_latent, grad_gain_ffn]
-    ).reshape(-1, gain_count)
+    )
+    grad_gains = jnp.pad(grad_gains, (0, gain_width * tokens_here - GAINS))
+    grad_latents_all = gather_rows(
+        jnp.concatenate(
+            [grad_latents, grad_gains.reshape(tokens_here, gain_width).astype(low)], axis=-1
+        )
+    )
+    activated_late = line.then(activated_low)
+    latent_up_sum, query_up_sum = Piece(latent_up_part), Piece(query_up_part)
+    line.begin(latent_up_sum, query_up_sum)
+    ffn_part = jnp.dot(activated_late, down_rows, preferred_element_type=jnp.float32).astype(low)
+    line.finish(ffn_part, gate_blocks)
+    up_blocks = shuffled(rows_of(up_sum))
+    gate_gradient = joined(line.then(gate_blocks))
+    ffn_branch = scatter_rows(tied(line.then(ffn_part), grad_latents_all))
+    block_output = (middle + RESIDUAL_SCALE * ffn_branch).astype(low)
+    latents_part = contract_rows(normed_columns, grad_latents_all[:, :width])
+    grad_gains = grad_latents_all[:, width:].astype(jnp.float32)
+    grad_gains = jnp.sum(grad_gains.reshape(-1, tokens_here * gain_width), axis=0)
+    grad_gains = lax.dynamic_slice_in_dim(
+        grad_gains, lax.axis_index("dp") * gain_count, gain_count, 0
+    )
     grad_gains = jnp.pad(
-        grad_gains, ((0, 0), (0, gain_columns * query_down.shape[1] - gain_count))
-    ).reshape(-1, gain_columns, query_down.shape[1])
-    latents_part = jnp.concatenate(
-        [
-            contract_rows(normed_low, grad_latents),
-            grad_gains.transpose(0, 2, 1).reshape(-1, gain_columns),
-        ],
-        axis=-1,
-    ).astype(low)
-    line.round(*up_sum[1:], after=[latents_part])
-    latents_part = scatter_low(latents_part)
-    ffn_part = jnp.dot(activated_low, down_rows, preferred_element_type=jnp.float32).astype(low)
-    ffn_branch = scatter_rows(tied(line.then(ffn_part), latents_part))
-    block_output = (middle + RESIDUAL_SCALE * ffn_branch).astype(low)
-    output_sum, latent_up_sum = Piece(output_part), Piece(latent_up_part)
-    query_up_sum, latents_sum = Piece(query_up_part), Piece(latents_part)
-    line.round(output_sum)
-    line.round(latent_up_sum, query_up_sum)
-    line.round(latents_sum)
+        grad_gains, (0, gain_columns * query_down.shape[1] - gain_count)
+    ).reshape(gain_columns, query_down.shape[1])
+    latents_sum = Piece(jnp.concatenate([latents_part, grad_gains.T], axis=-1).astype(low))
+    line.begin(latents_sum)
+    line.finish(input_grad)
+    line.begin()
+    line.finish(up_blocks)
+    up_gradient = joined(line.then(up_blocks))
     while line.active:
         line.round()
-    reduced_output, reduced_latent_up = output_sum.value, latent_up_sum.value
-    reduced_query_up, reduced_latents = query_up_sum.value, latents_sum.value
-    reduced_down, reduced_gate, reduced_up = rows_of(down_sum), rows_of(gate_sum), rows_of(up_sum)
+    reduced_output, reduced_latents = output_sum.value, latents_sum.value
+
+    reduced_latent_up, reduced_query_up = latent_up_sum.value, query_up_sum.value
+    reduced_gate, reduced_up = gate_gradient, up_gradient
     reduced_latents = reduced_latents.astype(jnp.float32)
     reduced_gains = reduced_latents[:, width:].T.reshape(-1)[:gain_count]
     reduced = (
@@ -517,43 +604,12 @@
         reduced_output.astype(jnp.float32),
         reduced_gate.astype(jnp.float32),
         reduced_up.astype(jnp.float32),
-        reduced_down.astype(jnp.float32),
+        None,
         reduced_gains,
-    )
-    states = (
-        (query_down, query_down_first, query_down_second),
-        (query_up, query_up_first, query_up_second),
-        (latent_down, latent_down_first, latent_down_second),
-        (latent_up, latent_up_first, latent_up_second),
-        (output_weight, output_weight_first, output_weight_second),
-        (gate_weight, gate_weight_first, gate_weight_second),
-        (up_weight, up_weight_first, up_weight_second),
-        (down_weight, down_weight_first, down_weight_second),
-        (norm_gains, norm_gains_first, norm_gains_second),
-    )
-    learn_rates = (
-        D ** (-0.5),
-        QR ** (-0.5),
-        D ** (-0.5),
-        KVR ** (-0.5),
-        math.sqrt(sequence_length / (0.0632 * H * VD)),
-        D ** (-0.5),
-        D ** (-0.5),
-        math.sqrt(1.0 / (0.0114 * FF)),
-        0.6,
     )
     results = [block_output, input_grad]
     for slot in range(9):
-        master, first_moment, second_moment = states[slot]
-        updated = adamw_update(
-            master[0],
-            first_moment[0],
-            second_moment[0],
-            reduced[slot],
-            learn_rates[slot],
-            0.0 if slot == 8 else WEIGHT_DECAY,
-            is_owner[slot],
-        )
+        updated = new_down if slot == 7 else update(slot, reduced[slot])
         results.extend((member[None] for member in updated))
     return tuple(results)
 

time: 1600 us -> 1390 us (0.87)
  waiting for transfers between devices: 580 us -> 425 us
  blocking collectives: 83.5 us -> 17.5 us
  other arithmetic: 239 us -> 260 us
    ppermute x66 -> x60, waiting for transfers between devices: 495 us -> 348 us  [begin(): lax.ppermute(piece.value, 'own', self.pairs(piece.leg))]
    all_to_all x1 -> x0, blocking collectives: 64.5 us -> none  [shards(): up_part = lax.all_to_all(tied(up_part, gate_part), 'dp', 0, 1, tiled=True)]
    convert_element_type x0 -> x6, local copies, waits for them, and re-layouts: none -> 38.2 us  [the longest x2 19.2 us: shards(): reduced_up.astype(jnp.float32)]
    ppermute x66 -> x60, starting transfers between devices: 212 us -> 183 us  [begin(): lax.ppermute(piece.value, 'own', self.pairs(piece.leg))]
    split x14 -> x6, local copies, waits for them, and re-layouts: 33.2 us -> 10.1 us  [pieces_of(): return [Piece(part) for part in jnp.split(rows, parts, axis=0)]]
    all_to_all x4 -> x5, local copies, waits for them, and re-layouts: 31.5 us -> 32.7 us  [the longest x2 15.8 us: shards(): gate_columns = lax.all_to_all(gate_rows, 'dp', 1, 0, tiled=True)]
    pallas_call x1 -> x2, Pallas kernels: 36.8 us -> 37.9 us  [attend(): pl.pallas_call(attend_kernel, grid=(heads // HEADS_STEP,), in_specs=[pl.B...]
    add x44 -> x40, other arithmetic: 86.4 us -> 85.4 us  [finish(): piece.value = value + arrived]
  transfers between devices with their start and end apart: 82 -> 78, of which waited for: 33 -> 30; matrix products, arithmetic and copies ran while one was open for 28% -> 38% of each run, Pallas kernels for 5% -> 6%
where the time goes in v2:
time: 1390 us; the launch traced here: 1380 us
  waiting for transfers between devices  425 us (31%)
  other arithmetic  260 us (19%)
  matrix products  217 us (16%)
  starting transfers between devices  216 us (16%)
  local copies, waits for them, and re-layouts  134 us (10%)
  Pallas kernels  87.1 us (6%)
  between operations  22.2 us (2%)
  blocking collectives  17.5 us (1%)
    ppermute x60, waiting for transfers between devices, begin(): lax.ppermute(piece.value, 'own', self.pairs(piece.leg))  348 us
    ppermute x60, starting transfers between devices, begin(): lax.ppermute(piece.value, 'own', self.pairs(piece.leg))  183 us
    add x40, other arithmetic, finish(): piece.value = value + arrived  85.4 us
    dot_general x6, matrix products, times_transpose(): lax.dot_general(first_matrix, second_matrix, (((1,), (1,)), ((), ())), pr...  80.8 us
    select_n x4, other arithmetic, adamw_update(): jnp.where(is_owner, new_second, second_moment)  65.7 us
    dot_general x6, matrix products, contract_rows(): lax.dot_general(first_matrix, second_matrix, (((0,), (0,)), ((), ())), pr...  58 us
    pallas_call x1, Pallas kernels, attend_back(): pl.pallas_call(attend_back_kernel, grid=(H // HEADS_STEP,), in_specs=[pl....  49.2 us
    pallas_call x2, Pallas kernels, attend(): pl.pallas_call(attend_kernel, grid=(heads // HEADS_STEP,), in_specs=[pl.B...  37.9 us
  transfers between devices with their start and end apart: 78, of which 30 were waited for; matrix products, arithmetic and copies ran while one was open for 38% of the time, Pallas kernels for 6%

profile of v2, /device:TPU:0, one launch (start us, length us, event | category | flops | bytes accessed | tf_op | source)
XLA Modules:
  0.0 1377.3 jit_solution(9622247626655908548)
XLA Ops:
  45.8 20.1 %collective-permute-done.3 = bf16[32,5120]{1,0:T(8,128)(2,1)S(1)} collective-permute-done((bf16[32,5120]{1,0:T(8,128)(2,1)S(1)}, bf16[32,5120]{1,0:T(8,128)(2,1)S(1)}, u32[]{:S(2)}, u32[]{:S(2)}) %collective-permute-start.3) | collective-permute-done | bytes 327712 | tf_op jit(solution)/shard_map/ppermute | solution.py:65
  76.2 15.4 %collective-permute-done.4 = bf16[320,1059]{1,0:T(8,128)(2,1)} collective-permute-done((bf16[320,1059]{1,0:T(8,128)(2,1)S(1)}, bf16[320,1059]{1,0:T(8,128)(2,1)}, u32[]{:S(2)}, u32[]{:S(2)}) %collective-permute-start.4) | collective-permute-done | bytes 677792 | tf_op jit(solution)/shard_map/ppermute | solution.py:65
  122.4 21.9 %collective-permute-done.9 = bf16[32,5120]{1,0:T(8,128)(2,1)S(1)} collective-permute-done((bf16[32,5120]{1,0:T(8,128)(2,1)S(1)}, bf16[32,5120]{1,0:T(8,128)(2,1)S(1)}, u32[]{:S(2)}, u32[]{:S(2)}) %collective-permute-start.9) | collective-permute-done | bytes 327712 | tf_op jit(solution)/shard_map/ppermute | solution.py:65
  144.3 16.0 %collective-permute-done.11 = bf16[160,6400]{1,0:T(8,128)(2,1)S(1)} collective-permute-done((bf16[160,6400]{1,0:T(8,128)(2,1)S(1)}, bf16[160,6400]{1,0:T(8,128)(2,1)S(1)}, u32[]{:S(2)}, u32[]{:S(2)}) %collective-permute-start.11) | collective-permute-done | bytes 2048032 | tf_op jit(solution)/shard_map/ppermute | solution.py:65
  179.0 17.5 %all_gather.27 = bf16[1024,288]{1,0:T(8,128)(2,1)S(1)} all-gather(bf16[256,288]{1,0:T(8,128)(2,1)S(1)} %pad_maximum_fusion.12), channel_id=1, replica_groups=mesh['dp'=8,'own'=4] {'own'}, dimensions={0}, use_global_device_ids=true | all-gather | bytes 737280 | tf_op jit(solution)/shard_map/all_gather | solution.py:375
  211.8 25.6 %collective-permute-done.12 = bf16[320,2560]{1,0:T(8,128)(2,1)} collective-permute-done((bf16[320,2560]{1,0:T(8,128)(2,1)}, bf16[320,2560]{1,0:T(8,128)(2,1)}, u32[]{:S(2)}, u32[]{:S(2)}) %collective-permute-start.12) | collective-permute-done | bytes 1638432 | tf_op jit(solution)/shard_map/ppermute | solution.py:65
  273.9 19.1 %shard_map.518 = (bf16[1280,256]{1,0:T(8,128)(2,1)S(1)}, f32[20,1,256]{2,1,0:T(1,128)S(1)}) custom-call(bf16[3840,256]{1,0:T(8,128)(2,1)S(1)} %bitcast.326, bf16[1024,5120]{1,0:T(8,128)(2,1)} %convolution_convert_fusion.2.kv_ref, bf16[1024,128]{1,0:T(8,128)(2,1)S(1)} %pad.14.rope_ref, f32[1024,256]{1,0:T(8,128)S(1)} %compare_select_fusion.bias_ref), custom_call_target="tpu_custom_call" | custom-call | tf_op jit(solution)/shard_map/pallas_call | solution.py:195
  319.1 18.7 %shard_map.519 = (bf16[1280,256]{1,0:T(8,128)(2,1)S(1)}, f32[20,1,256]{2,1,0:T(1,128)S(1)}) custom-call(bf16[3840,256]{1,0:T(8,128)(2,1)S(1)} %bitcast.327, bf16[1024,5120]{1,0:T(8,128)(2,1)} %convolution_convert_fusion.2.kv_ref, bf16[1024,128]{1,0:T(8,128)(2,1)S(1)} %pad.14.rope_ref, f32[1024,256]{1,0:T(8,128)S(1)} %compare_select_fusion.bias_ref), custom_call_target="tpu_custom_call" | custom-call | tf_op jit(solution)/shard_map/pallas_call | solution.py:195
  387.7 27.6 %collective-permute-done.21 = bf16[160,6400]{1,0:T(8,128)(2,1)S(1)} collective-permute-done((bf16[160,6400]{1,0:T(8,128)(2,1)S(1)}, bf16[160,6400]{1,0:T(8,128)(2,1)S(1)}, u32[]{:S(2)}, u32[]{:S(2)}) %collective-permute-start.21) | collective-permute-done | bytes 2048032 | tf_op jit(solution)/shard_map/ppermute | solution.py:65
  495.3 15.2 %all-to-all-done = bf16[320,8,800]{2,0,1:T(8,128)(2,1)} async-done(((bf16[320,8,800]{2,0,1:T(8,128)(2,1)}), bf16[320,8,800]{2,0,1:T(8,128)(2,1)}, u32[]{:S(2)}, u32[]{:S(2)}) %all-to-all-start) | async-done | bytes 4096032 | tf_op jit(solution)/shard_map/all_to_all | solution.py:432
  520.5 14.5 %fusion.120 = f32[2048,800]{0,1:T(8,128)} fusion(bf16[2048,2560]{1,0:T(8,128)(2,1)} %all-gather.18.cloned.1.call-done, bf16[2560,800]{1,0:T(8,128)(2,1)} %bitcast.27), kind=kOutput, calls=%fused_computation.284 | convolution fusion | flops 8388608000 | bytes 21135360 | tf_op jit(solution)/shard_map/dot_general | solution.py:438
  535.0 33.5 %all-to-all-done.1 = bf16[320,8,800]{2,0,1:T(8,128)(2,1)} async-done(((bf16[320,8,800]{2,0,1:T(8,128)(2,1)}), bf16[320,8,800]{2,0,1:T(8,128)(2,1)}, u32[]{:S(2)}, u32[]{:S(2)}) %all-to-all-start.1) | async-done | bytes 4096032 | tf_op jit(solution)/shard_map/all_to_all | solution.py:435
  568.5 16.7 %multiply_convert_fusion.2 = (bf16[2048,800]{0,1:T(8,128)(2,1)}, f32[2048,800]{0,1:T(8,128)}) fusion(f32[2048,800]{0,1:T(8,128)} %fusion.120, bf16[2048,2560]{1,0:T(8,128)(2,1)} %all-gather.18.cloned.1.call-done, bf16[2560,800]{1,0:T(8,128)(2,1)} %bitcast.29), kind=kOutput, calls=%fused_computation.34 | convolution fusion | flops 8398438400 | bytes 30965760 | tf_op jit(solution)/shard_map/dot_general | solution.py:443
  585.2 12.5 convolution_convert_fusion.7
  606.2 18.5 %multiply_convert_fusion = (bf16[2048,800]{0,1:T(8,128)(2,1)}, bf16[2048,800]{0,1:T(8,128)(2,1)}) fusion(f32[2048,800]{0,1:T(8,128)} %fusion.120, f32[2048,800]{0,1:T(8,128)} %get-tuple-element.603, bf16[2048,2560]{1,0:T(8,128)(2,1)} %all-gather.10.cloned.1.call-done, bf16[400,2560]{1,0:T(8,128)(2,1)S(1)} %broadcast_select_fusion.6, ...), kind=kOutput, calls=%fused_computation.32 | convolution fusion | flops 8418099200 | bytes 34242560 | tf_op jit(solution)/shard_map/dot_general | solution.py:168
  624.8 18.0 %fusion.121 = f32[2048,2560]{1,0:T(8,128)} fusion(bf16[2048,800]{0,1:T(8,128)(2,1)} %get-tuple-element.313, bf16[2560,800]{1,0:T(8,128)(2,1)} %bitcast.29), kind=kOutput, calls=%fused_computation.285 | convolution fusion | flops 8388608000 | bytes 28344320 | tf_op jit(solution)/shard_map/dot_general | solution.py:168
  642.8 19.9 %add_convert_fusion = bf16[2048,2560]{1,0:T(8,128)(2,1)} fusion(f32[2048,2560]{1,0:T(8,128)} %fusion.121, bf16[2048,800]{0,1:T(8,128)(2,1)} %get-tuple-element.306, bf16[2560,800]{1,0:T(8,128)(2,1)} %bitcast.27), kind=kOutput, calls=%fused_computation | convolution fusion | flops 8399093760 | bytes 38830080 | tf_op jit(solution)/shard_map/dot_general | solution.py:168
  672.0 12.6 convolution_convert_fusion.6
  686.2 25.6 %collective-permute-done.32 = bf16[400,2560]{1,0:T(8,128)(2,1)S(1)} collective-permute-done((bf16[400,2560]{1,0:T(8,128)(2,1)S(1)}, bf16[400,2560]{1,0:T(8,128)(2,1)S(1)}, u32[]{:S(2)}, u32[]{:S(2)}) %collective-permute-start.32) | collective-permute-done | bytes 2048032 | tf_op jit(solution)/shard_map/ppermute | solution.py:65
  724.0 33.3 %collective-permute-done.33 = bf16[400,2560]{1,0:T(8,128)(2,1)S(1)} collective-permute-done((bf16[400,2560]{1,0:T(8,128)(2,1)S(1)}, bf16[400,2560]{1,0:T(8,128)(2,1)S(1)}, u32[]{:S(2)}, u32[]{:S(2)}) %collective-permute-start.33) | collective-permute-done | bytes 2048032 | tf_op jit(solution)/shard_map/ppermute | solution.py:65
  783.8 12.5 convolution_convert_fusion.5
  812.1 31.1 %collective-permute-done.36 = bf16[400,2560]{1,0:T(8,128)(2,1)S(1)} collective-permute-done((bf16[400,2560]{1,0:T(8,128)(2,1)S(1)}, bf16[400,2560]{1,0:T(8,128)(2,1)S(1)}, u32[]{:S(2)}, u32[]{:S(2)}) %collective-permute-start.36) | collective-permute-done | bytes 2048032 | tf_op jit(solution)/shard_map/ppermute | solution.py:65
  859.4 49.2 %shard_map.520 = (bf16[3840,256]{1,0:T(8,128)(2,1)S(1)}, bf16[1024,5120]{1,0:T(8,128)(2,1)}, f32[1024,128]{1,0:T(8,128)S(1)}) custom-call(bf16[3840,256]{1,0:T(8,128)(2,1)} %bitcast.328, bf16[1024,5120]{1,0:T(8,128)(2,1)} %convolution_convert_fusion.2.kv_ref, bf16[1024,128]{1,0:T(8,128)(2,1)S(1)} %copy-done.2, f32[1024,256]{1,0:T(8,128)S(1)} %compare_select_fusion.bias_ref, ...), custom_call_target="tpu_custom_call" | custom-call | tf_op jit(solution)/shard_map/pallas_call | solution.py:242
  960.1 20.7 %bitcast_select_fusion = (f32[800,2560]{1,0:T(8,128)}, f32[800,2560]{1,0:T(8,128)}, f32[800,2560]{1,0:T(8,128)}) fusion(f32[1,800,2560]{2,1,0:T(8,128)} %param.58, bf16[800,2560]{1,0:T(8,128)(2,1)} %pad_maximum_fusion.3, pred[]{:T(512)S(6)} %eq.32, f32[1,800,2560]{2,1,0:T(8,128)} %param.57, f32[1,800,2560]{2,1,0:T(8,128)} %param.56), kind=kLoop, calls=%fused_computation.16 | loop fusion | flops 36864000 | bytes 53248000 | tf_op jit(solution)/shard_map/jit(_where)/select_n | solution.py:278
  980.7 13.2 collective-permute-done.42
  1013.6 30.7 %collective-permute-done.47 = bf16[320,2560]{1,0:T(8,128)(2,1)} collective-permute-done((bf16[320,2560]{1,0:T(8,128)(2,1)}, bf16[320,2560]{1,0:T(8,128)(2,1)}, u32[]{:S(2)}, u32[]{:S(2)}) %collective-permute-start.47) | collective-permute-done | bytes 1638432 | tf_op jit(solution)/shard_map/ppermute | solution.py:65
  1064.6 12.6 all-to-all-start.3
  1122.3 16.3 %convolution_convert_fusion.1 = bf16[2048,2560]{1,0:T(8,128)(2,1)} fusion(bf16[2048,800]{0,1:T(8,128)(2,1)} %get-tuple-element.362, bf16[400,2560]{1,0:T(8,128)(2,1)} %copy-done.74, bf16[400,2560]{1,0:T(8,128)(2,1)} %copy-done.73), kind=kOutput, calls=%fused_computation.8 | convolution fusion | flops 8402042880 | bytes 17858560 | tf_op jit(solution)/shard_map/dot_general | solution.py:570
  1154.6 16.4 %all-to-all-done.2 = bf16[8,320,800]{2,1,0:T(8,128)(2,1)} async-done(((bf16[8,320,800]{2,1,0:T(8,128)(2,1)}), bf16[8,320,800]{2,1,0:T(8,128)(2,1)}, u32[]{:S(2)}, u32[]{:S(2)}) %all-to-all-start.2) | async-done | bytes 4096032 | tf_op jit(solution)/shard_map/all_to_all | solution.py:100
  1240.1 23.0 %fusion.11 = (f32[1,320,6400]{2,1,0:T(8,128)}, f32[1,320,6400]{2,1,0:T(8,128)}, f32[1,320,6400]{2,1,0:T(8,128)}) fusion(f32[1,320,6400]{2,1,0:T(8,128)} %param.52, f32[1,320,6400]{2,1,0:T(8,128)} %reshape.298, pred[]{:T(512)S(6)} %eq.30, f32[1,320,6400]{2,1,0:T(8,128)} %param.50, f32[1,320,6400]{2,1,0:T(8,128)} %param.51), kind=kLoop, calls=%fused_computation.39 | loop fusion | flops 34816000 | bytes 57344000 | tf_op jit(solution)/shard_map/jit(_where)/select_n | solution.py:278
  1284.0 14.4 %collective-permute-done.57 = bf16[96,3840]{1,0:T(8,128)(2,1)} collective-permute-done((bf16[96,3840]{1,0:T(8,128)(2,1)S(1)}, bf16[96,3840]{1,0:T(8,128)(2,1)}, u32[]{:S(2)}, u32[]{:S(2)}) %collective-permute-start.57) | collective-permute-done | bytes 737312 | tf_op jit(solution)/shard_map/ppermute | solution.py:65
  1329.7 22.0 %fusion.10 = (f32[1,320,6400]{2,1,0:T(8,128)}, f32[1,320,6400]{2,1,0:T(8,128)}, f32[1,320,6400]{2,1,0:T(8,128)}) fusion(f32[1,320,6400]{2,1,0:T(8,128)} %param.55, f32[1,320,6400]{2,1,0:T(8,128)} %reshape.299, pred[]{:T(512)S(6)} %eq.31, f32[1,320,6400]{2,1,0:T(8,128)} %param.53, f32[1,320,6400]{2,1,0:T(8,128)} %param.54), kind=kLoop, calls=%fused_computation.38 | loop fusion | flops 34816000 | bytes 57344000 | tf_op jit(solution)/shard_map/jit(_where)/select_n | solution.py:278
  (607 shorter events, 691.0 us)
Async XLA Ops:
  7.2 98.8 %all-gather.10.cloned.1.call-start = ((), (), s32[]{:S(2)}) async-start(), calls=%async_computation.12 | async-start | bytes 11796480 | tf_op jit(solution)/shard_map/all_gather | solution.py:112
  10.0 159.3 %all-gather.12.cloned.1.call-start = ((), (), s32[]{:S(2)}) async-start(), calls=%async_computation.13 | async-start | bytes 6635520 | tf_op jit(solution)/shard_map/all_gather | solution.py:112
  106.0 98.3 %all-gather.14.cloned.1.call-start = ((), (), s32[]{:S(2)}) async-start(), calls=%async_computation.14 | async-start | bytes 2949120 | tf_op jit(solution)/shard_map/all_gather | solution.py:112
  162.4 105.5 %all-gather.8.cloned.1.call-start = ((), (), s32[]{:S(2)}) async-start(), calls=%async_computation.11 | async-start | bytes 6635520 | tf_op jit(solution)/shard_map/all_gather | solution.py:112
  163.4 190.1 %all-gather.16.cloned.1.call-start = ((), (), s32[]{:S(2)}) async-start(), calls=%async_computation.15 | async-start | bytes 14745600 | tf_op jit(solution)/shard_map/all_gather | solution.py:112
  243.6 271.7 %all-gather.18.cloned.1.call-start = ((), (), s32[]{:S(2)}) async-start(), calls=%async_computation.16 | async-start | bytes 11796480 | tf_op jit(solution)/shard_map/all_gather | solution.py:112
  257.6 45.6 %collective-permute-start.17 = (bf16[160,6400]{1,0:T(8,128)(2,1)}, bf16[160,6400]{1,0:T(8,128)(2,1)}, u32[]{:S(2)}, u32[]{:S(2)}) collective-permute-start(bf16[160,6400]{1,0:T(8,128)(2,1)} %get-tuple-element.263), channel_id=1, source_target_pairs={{0,1},{3,2},{4,5},{7,6},{8,9},{11,10},{12,13},{15,14},{16,17},{19,... | collective-permute-start | bytes 6144008 | tf_op jit(solution)/shard_map/ppermute | solution.py:65
  452.1 58.4 %all-to-all-start = ((bf16[320,8,800]{2,0,1:T(8,128)(2,1)}), bf16[320,8,800]{2,0,1:T(8,128)(2,1)}, u32[]{:S(2)}, u32[]{:S(2)}) async-start(bf16[320,8,800]{2,0,1:T(8,128)(2,1)} %copy.149), calls=%async_computation | async-start | bytes 9175040 | tf_op jit(solution)/shard_map/all_to_all | solution.py:432
  510.5 58.0 %all-to-all-start.1 = ((bf16[320,8,800]{2,0,1:T(8,128)(2,1)}), bf16[320,8,800]{2,0,1:T(8,128)(2,1)}, u32[]{:S(2)}, u32[]{:S(2)}) async-start(bf16[320,8,800]{2,0,1:T(8,128)(2,1)} %copy.150), calls=%async_computation.1 | async-start | bytes 9175040 | tf_op jit(solution)/shard_map/all_to_all | solution.py:435
  515.1 246.1 %reduce-scatter.7.cloned.1.call-start = ((), (), s32[]{:S(2)}) async-start(), calls=%async_computation.17 | async-start | bytes 11796480 | tf_op jit(solution)/shard_map/reduce_scatter | solution.py:116
  519.2 84.5 %collective-permute-start.29 = (bf16[400,2560]{1,0:T(8,128)(2,1)}, bf16[400,2560]{1,0:T(8,128)(2,1)}, u32[]{:S(2)}, u32[]{:S(2)}) collective-permute-start(bf16[400,2560]{1,0:T(8,128)(2,1)} %add.396), channel_id=1, source_target_pairs={{1,0},{2,3},{5,4},{6,7},{9,8},{10,11},{13,12},{14,15},{17,16},{18,... | collective-permute-start | bytes 6144008 | tf_op jit(solution)/shard_map/ppermute | solution.py:65
  662.7 254.6 %reduce-scatter.9.cloned.1.call-start = ((), (), s32[]{:S(2)}) async-start(), calls=%async_computation.18 | async-start | bytes 14745600 | tf_op jit(solution)/shard_map/reduce_scatter | solution.py:116
  666.4 45.4 %collective-permute-start.32 = (bf16[400,2560]{1,0:T(8,128)(2,1)S(1)}, bf16[400,2560]{1,0:T(8,128)(2,1)S(1)}, u32[]{:S(2)}, u32[]{:S(2)}) collective-permute-start(bf16[400,2560]{1,0:T(8,128)(2,1)S(1)} %copy-done.42), channel_id=1, source_target_pairs={{0,1},{3,2},{4,5},{7,6},{8,9},{11,10},{12,13},{15,14},{16,17},{19,... | collective-permute-start | bytes 6144008 | tf_op jit(solution)/shard_map/ppermute | solution.py:65
  715.7 45.5 %collective-permute-start.35 = (bf16[1280,800]{0,1:T(8,128)(2,1)S(1)}, bf16[1280,800]{0,1:T(8,128)(2,1)}, u32[]{:S(2)}, u32[]{:S(2)}) collective-permute-start(bf16[1280,800]{0,1:T(8,128)(2,1)S(1)} %get-tuple-element.318), channel_id=1, source_target_pairs={{0,1},{3,2},{4,5},{7,6},{8,9},{11,10},{12,13},{15,14},{16,17},{19,... | collective-permute-start | bytes 6144008 | tf_op jit(solution)/shard_map/ppermute | solution.py:65
  783.7 228.8 %reduce-scatter.15.cloned.1.call-start = ((), (), s32[]{:S(2)}) async-start(), calls=%async_computation.21 | async-start | bytes 983040 | tf_op jit(solution)/shard_map/reduce_scatter | solution.py:527
  849.0 59.6 %collective-permute-start.39 = (bf16[1280,800]{0,1:T(8,128)(2,1)S(1)}, bf16[1280,800]{0,1:T(8,128)(2,1)S(1)}, u32[]{:S(2)}, u32[]{:S(2)}) collective-permute-start(bf16[1280,800]{0,1:T(8,128)(2,1)S(1)} %add.405), channel_id=1, source_target_pairs={{1,0},{2,3},{5,4},{6,7},{9,8},{10,11},{13,12},{14,15},{17,16},{18,... | collective-permute-start | bytes 6144008 | tf_op jit(solution)/shard_map/ppermute | solution.py:65
  850.4 58.2 %collective-permute-start.40 = (bf16[1280,800]{0,1:T(8,128)(2,1)S(1)}, bf16[1280,800]{0,1:T(8,128)(2,1)}, u32[]{:S(2)}, u32[]{:S(2)}) collective-permute-start(bf16[1280,800]{0,1:T(8,128)(2,1)S(1)} %add.406), channel_id=1, source_target_pairs={{1,2},{2,1},{5,6},{6,5},{9,10},{10,9},{13,14},{14,13},{17,18},{18,... | collective-permute-start | bytes 6144008 | tf_op jit(solution)/shard_map/ppermute | solution.py:65
  852.4 56.3 %collective-permute-start.41 = (bf16[1280,800]{0,1:T(8,128)(2,1)S(1)}, bf16[1280,800]{0,1:T(8,128)(2,1)}, u32[]{:S(2)}, u32[]{:S(2)}) collective-permute-start(bf16[1280,800]{0,1:T(8,128)(2,1)S(1)} %get-tuple-element.340), channel_id=1, source_target_pairs={{0,1},{3,2},{4,5},{7,6},{8,9},{11,10},{12,13},{15,14},{16,17},{19,... | collective-permute-start | bytes 6144008 | tf_op jit(solution)/shard_map/ppermute | solution.py:65
  917.3 201.2 %reduce-scatter.11.cloned.1.call-start = ((), (), s32[]{:S(2)}) async-start(), calls=%async_computation.19 | async-start | bytes 2949120 | tf_op jit(solution)/shard_map/reduce_scatter | solution.py:116
  926.0 192.6 %reduce-scatter.13.cloned.1.call-start = ((), (), s32[]{:S(2)}) async-start(), calls=%async_computation.20 | async-start | bytes 6635520 | tf_op jit(solution)/shard_map/reduce_scatter | solution.py:116
  933.6 281.7 %all-gather.20.cloned.1.call-start = ((), (), s32[]{:S(2)}) async-start(), calls=%async_computation.22 | async-start | bytes 4976640 | tf_op jit(solution)/shard_map/all_gather | solution.py:112
  945.9 48.0 %collective-permute-start.42 = (bf16[1280,800]{0,1:T(8,128)(2,1)}, bf16[1280,800]{0,1:T(8,128)(2,1)}, u32[]{:S(2)}, u32[]{:S(2)}) collective-permute-start(bf16[1280,800]{0,1:T(8,128)(2,1)} %add.407), channel_id=1, source_target_pairs={{1,0},{2,3},{5,4},{6,7},{9,8},{10,11},{13,12},{14,15},{17,16},{18,... | collective-permute-start | bytes 6144008 | tf_op jit(solution)/shard_map/ppermute | solution.py:65
  947.2 46.7 %collective-permute-start.43 = (bf16[1280,800]{0,1:T(8,128)(2,1)}, bf16[1280,800]{0,1:T(8,128)(2,1)}, u32[]{:S(2)}, u32[]{:S(2)}) collective-permute-start(bf16[1280,800]{0,1:T(8,128)(2,1)} %add.408), channel_id=1, source_target_pairs={{1,2},{2,1},{5,6},{6,5},{9,10},{10,9},{13,14},{14,13},{17,18},{18,... | collective-permute-start | bytes 6144008 | tf_op jit(solution)/shard_map/ppermute | solution.py:65
  949.3 44.7 %collective-permute-start.44 = (bf16[1280,800]{0,1:T(8,128)(2,1)}, bf16[1280,800]{0,1:T(8,128)(2,1)}, u32[]{:S(2)}, u32[]{:S(2)}) collective-permute-start(bf16[1280,800]{0,1:T(8,128)(2,1)} %get-tuple-element.352), channel_id=1, source_target_pairs={{0,1},{3,2},{4,5},{7,6},{8,9},{11,10},{12,13},{15,14},{16,17},{19,... | collective-permute-start | bytes 6144008 | tf_op jit(solution)/shard_map/ppermute | solution.py:65
  1000.8 46.9 %collective-permute-start.45 = (bf16[1280,800]{0,1:T(8,128)(2,1)}, bf16[1280,800]{0,1:T(8,128)(2,1)}, u32[]{:S(2)}, u32[]{:S(2)}) collective-permute-start(bf16[1280,800]{0,1:T(8,128)(2,1)} %add.414), channel_id=1, source_target_pairs={{1,0},{2,3},{5,4},{6,7},{9,8},{10,11},{13,12},{14,15},{17,16},{18,... | collective-permute-start | bytes 6144008 | tf_op jit(solution)/shard_map/ppermute | solution.py:65
  1002.1 45.6 %collective-permute-start.46 = (bf16[1280,800]{0,1:T(8,128)(2,1)S(1)}, bf16[1280,800]{0,1:T(8,128)(2,1)}, u32[]{:S(2)}, u32[]{:S(2)}) collective-permute-start(bf16[1280,800]{0,1:T(8,128)(2,1)S(1)} %add.415), channel_id=1, source_target_pairs={{1,2},{2,1},{5,6},{6,5},{9,10},{10,9},{13,14},{14,13},{17,18},{18,... | collective-permute-start | bytes 6144008 | tf_op jit(solution)/shard_map/ppermute | solution.py:65
  1101.3 69.6 %all-to-all-start.2 = ((bf16[8,320,800]{2,1,0:T(8,128)(2,1)}), bf16[8,320,800]{2,1,0:T(8,128)(2,1)}, u32[]{:S(2)}, u32[]{:S(2)}) async-start(bf16[8,320,800]{2,1,0:T(8,128)(2,1)} %bitcast.330), calls=%async_computation.8 | async-start | bytes 9175040 | tf_op jit(solution)/shard_map/all_to_all | solution.py:100
  1118.6 52.4 %collective-permute-start.48 = (bf16[1280,800]{0,1:T(8,128)(2,1)}, bf16[1280,800]{0,1:T(8,128)(2,1)}, u32[]{:S(2)}, u32[]{:S(2)}) collective-permute-start(bf16[1280,800]{0,1:T(8,128)(2,1)} %add.416), channel_id=1, source_target_pairs={{1,0},{2,3},{5,4},{6,7},{9,8},{10,11},{13,12},{14,15},{17,16},{18,... | collective-permute-start | bytes 6144008 | tf_op jit(solution)/shard_map/ppermute | solution.py:65
  1120.1 50.8 %collective-permute-start.49 = (bf16[320,2560]{1,0:T(8,128)(2,1)}, bf16[320,2560]{1,0:T(8,128)(2,1)}, u32[]{:S(2)}, u32[]{:S(2)}) collective-permute-start(bf16[320,2560]{1,0:T(8,128)(2,1)} %add.417), channel_id=1, source_target_pairs={{1,2},{2,1},{5,6},{6,5},{9,10},{10,9},{13,14},{14,13},{17,18},{18,... | collective-permute-start | bytes 4915208 | tf_op jit(solution)/shard_map/ppermute | solution.py:65
  1188.7 95.2 %all-to-all-start.4 = ((bf16[8,320,800]{2,1,0:T(8,128)(2,1)}), bf16[8,320,800]{2,1,0:T(8,128)(2,1)}, u32[]{:S(2)}, u32[]{:S(2)}) async-start(bf16[8,320,800]{2,1,0:T(8,128)(2,1)} %bitcast.329), calls=%async_computation.10 | async-start | bytes 9175040 | tf_op jit(solution)/shard_map/all_to_all | solution.py:100
  1193.3 174.6 %reduce-scatter.17.cloned.1.call-start = ((), (), s32[]{:S(2)}) async-start(), calls=%async_computation.23 | async-start | bytes 11796480 | tf_op jit(solution)/shard_map/reduce_scatter | solution.py:116
  1300.5 55.6 %collective-permute-start.59 = (bf16[320,1059]{1,0:T(8,128)(2,1)}, bf16[320,1059]{1,0:T(8,128)(2,1)}, u32[]{:S(2)}, u32[]{:S(2)}) collective-permute-start(bf16[320,1059]{1,0:T(8,128)(2,1)} %add.428), channel_id=1, source_target_pairs={{1,0},{2,3},{5,4},{6,7},{9,8},{10,11},{13,12},{14,15},{17,16},{18,... | collective-permute-start | bytes 2033288 | tf_op jit(solution)/shard_map/ppermute | solution.py:65
  (171 other events, 3829.1 us)
Sparse Core Ops, SparseCore 0:
  10.5 65.9 all-gather.9
  106.2 42.9 all-gather.11
  162.5 30.2 all-gather.13
  195.2 43.8 all-gather.7
  243.7 73.3 all-gather.15
  363.8 64.4 all-gather.17
  662.8 82.3 reduce-scatter.6
  783.9 103.7 reduce-scatter.8
  917.5 36.2 reduce-scatter.14
  957.5 41.5 reduce-scatter.10
  1003.2 59.6 reduce-scatter.12
  1065.2 69.8 all-gather.19
  1215.5 81.9 reduce-scatter.16

commit v3 on v2

--- a/solution.py
+++ b/solution.py
@@ -1,3 +1,4 @@
+import functools
 import math
 
 import jax
@@ -100,8 +101,68 @@
     return lax.all_to_all(blocks, "dp", 0, 0)
 
 
-def joined(blocks):
-    return blocks.transpose(1, 0, 2).reshape(blocks.shape[1], -1)
+def update_kernel(
+    learn_rate,
+    weight_decay,
+    owner_ref,
+    blocks_ref,
+    master_ref,
+    first_ref,
+    second_ref,
+    new_master_ref,
+    new_first_ref,
+    new_second_ref,
+    gradient_ref,
+):
+    @pl.when(owner_ref[0] == 1)
+    def _():
+        width = blocks_ref.shape[2]
+        for number in range(blocks_ref.shape[0]):
+            gradient_ref[:, number * width : (number + 1) * width] = blocks_ref[number].astype(
+                jnp.float32
+            )
+        gradient, master = gradient_ref[...], master_ref[...]
+        new_first = BETA_ONE * first_ref[...] + (1.0 - BETA_ONE) * gradient
+        new_second = BETA_TWO * second_ref[...] + (1.0 - BETA_TWO) * gradient * gradient
+        mean_hat = new_first / (1.0 - BETA_ONE**STEP)
+        square_hat = new_second / (1.0 - BETA_TWO**STEP)
+        new_master_ref[...] = master - learn_rate * (
+            mean_hat / (jnp.sqrt(square_hat) + ADAM_EPS) + weight_decay * master
+        )
+        new_first_ref[...] = new_first
+        new_second_ref[...] = new_second
+
+    @pl.when(owner_ref[0] != 1)
+    def _():
+        new_master_ref[...] = master_ref[...]
+        new_first_ref[...] = first_ref[...]
+        new_second_ref[...] = second_ref[...]
+
+
+def update_joined(is_owner, blocks, master, first_moment, second_moment, learn_rate):
+    rows, columns = master.shape
+    step_rows = next(size for size in (64, 32, 16, rows) if rows % size == 0)
+    state = pl.BlockSpec((step_rows, columns), lambda i, _: (i, 0))
+    return pl.pallas_call(
+        functools.partial(update_kernel, learn_rate, WEIGHT_DECAY),
+        grid_spec=pltpu.PrefetchScalarGridSpec(
+            num_scalar_prefetch=1,
+            grid=(rows // step_rows,),
+            in_specs=[
+                pl.BlockSpec((blocks.shape[0], step_rows, blocks.shape[2]), lambda i, _: (0, i, 0)),
+                state,
+                state,
+                state,
+            ],
+            out_specs=[state, state, state],
+            scratch_shapes=[pltpu.VMEM((step_rows, columns), jnp.float32)],
+        ),
+        out_shape=[jax.ShapeDtypeStruct(master.shape, jnp.float32)] * 3,
+        cost_estimate=pl.CostEstimate(
+            flops=20 * rows * columns, bytes_accessed=26 * rows * columns, transcendentals=0
+        ),
+        compiler_params=pltpu.CompilerParams(vmem_limit_bytes=48 * 1024 * 1024),
+    )(is_owner.astype(jnp.int32).reshape(1), blocks, master, first_moment, second_moment)
 
 
 def rows_of(pieces):
@@ -342,8 +403,10 @@
         (RESIDUAL_SCALE * cotangent.astype(jnp.float32)).astype(low)
     )
     line.round(down_latents)
-    line.round(query_up_rows, latent_up_rows)
-    line.round(output_rows)
+    line.begin(query_up_rows, latent_up_rows)
+    line.finish(output_rows.value, *[piece.value for piece in gate_rows])
+    line.begin(output_rows)
+    line.finish(*[piece.value for piece in up_rows + down_rows])
     down_latents_all = gather_rows(tied(down_latents.value, grad_ffn_all))
     line.round(gate_rows[0])
     query_up_all = gather_rows(query_up_rows.value)
@@ -433,7 +496,7 @@
     line.finish()
     line.begin()
     up_columns = lax.all_to_all(line.then(rows_of(up_rows)), "dp", 1, 0, tiled=True)
-    line.finish(normed_ffn_all, gate_columns)
+    line.finish(normed_ffn_all, gate_columns, normed_columns)
     line.begin()
     gate_pre = jnp.dot(
         line.then(normed_ffn_all), gate_columns, preferred_element_type=jnp.float32
@@ -460,13 +523,14 @@
         times_transpose(grad_gate_pre, gate_columns) + times_transpose(grad_up_pre, up_columns)
     ).astype(low)
     gate_part = contract_rows(normed_ffn_all, tied(grad_gate_pre, grad_normed_ffn)).astype(low)
-    line.finish(grad_normed_ffn, gate_part)
+    up_part = contract_rows(normed_ffn_all, tied(grad_up_pre, gate_part)).astype(low)
+    line.finish(grad_normed_ffn, gate_part, up_part)
     grad_normed_ffn = scatter_rows(grad_normed_ffn)
     gate_sum = pieces_of(gate_part, 2)
-    grad_up_pre = line.then(grad_up_pre)
+    activated_late = line.then(activated_low)
     line.begin(gate_sum[0])
-    up_part = contract_rows(normed_ffn_all, grad_up_pre).astype(low)
-    line.finish(up_part)
+    ffn_part = jnp.dot(activated_late, down_rows, preferred_element_type=jnp.float32).astype(low)
+    line.finish(ffn_part)
     up_sum = pieces_of(up_part, 2)
     grad_normed_ffn = line.then(grad_normed_ffn)
     line.begin(*gate_sum[1:])
@@ -564,13 +628,11 @@
             [grad_latents, grad_gains.reshape(tokens_here, gain_width).astype(low)], axis=-1
         )
     )
-    activated_late = line.then(activated_low)
     latent_up_sum, query_up_sum = Piece(latent_up_part), Piece(query_up_part)
     line.begin(latent_up_sum, query_up_sum)
-    ffn_part = jnp.dot(activated_late, down_rows, preferred_element_type=jnp.float32).astype(low)
-    line.finish(ffn_part, gate_blocks)
+    line.finish(gate_blocks)
     up_blocks = shuffled(rows_of(up_sum))
-    gate_gradient = joined(line.then(gate_blocks))
+    gate_blocks = line.then(gate_blocks)
     ffn_branch = scatter_rows(tied(line.then(ffn_part), grad_latents_all))
     block_output = (middle + RESIDUAL_SCALE * ffn_branch).astype(low)
     latents_part = contract_rows(normed_columns, grad_latents_all[:, :width])
@@ -587,13 +649,11 @@
     line.finish(input_grad)
     line.begin()
     line.finish(up_blocks)
-    up_gradient = joined(line.then(up_blocks))
     while line.active:
         line.round()
     reduced_output, reduced_latents = output_sum.value, latents_sum.value
 
     reduced_latent_up, reduced_query_up = latent_up_sum.value, query_up_sum.value
-    reduced_gate, reduced_up = gate_gradient, up_gradient
     reduced_latents = reduced_latents.astype(jnp.float32)
     reduced_gains = reduced_latents[:, width:].T.reshape(-1)[:gain_count]
     reduced = (
@@ -602,14 +662,19 @@
         reduced_latents[:, QR:width],
         reduced_latent_up.astype(jnp.float32),
         reduced_output.astype(jnp.float32),
-        reduced_gate.astype(jnp.float32),
-        reduced_up.astype(jnp.float32),
+        None,
+        None,
         None,
         reduced_gains,
     )
     results = [block_output, input_grad]
     for slot in range(9):
-        updated = new_down if slot == 7 else update(slot, reduced[slot])
+        if slot in (5, 6):
+            blocks = gate_blocks if slot == 5 else up_blocks
+            members = (member[0] for member in states[slot])
+            updated = update_joined(is_owner[slot], blocks, *members, learn_rates[slot])
+        else:
+            updated = new_down if slot == 7 else update(slot, reduced[slot])
         results.extend((member[None] for member in updated))
     return tuple(results)
 

time: 1390 us -> 1350 us (0.971)
  other arithmetic: 260 us -> 214 us
  Pallas kernels: 87.1 us -> 133 us
  local copies, waits for them, and re-layouts: 134 us -> 99.7 us
    pallas_call x0 -> x2, Pallas kernels: none -> 45.5 us  [update_joined(): pl.pallas_call(functools.partial(update_kernel, learn_rate, WEIGHT_DECAY)...]
    select_n x4 -> x2, other arithmetic: 65.7 us -> 20.6 us  [adamw_update(): jnp.where(is_owner, new_second, second_moment)]
    convert_element_type x4 -> x0, local copies, waits for them, and re-layouts: 38 us -> none  [the longest x2 19.2 us: shards(): reduced_up.astype(jnp.float32)]
    all_to_all x2, waiting for transfers between devices: 16.4 us -> 38.5 us  [shuffled(): return lax.all_to_all(blocks, 'dp', 0, 0)]
    all_to_all x1, waiting for transfers between devices: 33.5 us -> 18 us  [shards(): lax.all_to_all(line.then(rows_of(up_rows)), 'dp', 1, 0, tiled=True)]
    unnamed x260 -> x298, local copies, waits for them, and re-layouts: 24.6 us -> 28.2 us
  transfers between devices with their start and end apart: 78 -> 78, of which waited for: 30 -> 33; matrix products, arithmetic and copies ran while one was open for 38% -> 32% of each run, Pallas kernels for 6% -> 10%
where the time goes in v3:
time: 1350 us; the launch traced here: 1340 us
  waiting for transfers between devices  417 us (31%)
  starting transfers between devices  219 us (16%)
  other arithmetic  214 us (16%)
  matrix products  214 us (16%)
  Pallas kernels  133 us (10%)
  local copies, waits for them, and re-layouts  99.7 us (7%)
  between operations  22.3 us (2%)
  blocking collectives  17.7 us (1%)
    ppermute x60, waiting for transfers between devices, begin(): lax.ppermute(piece.value, 'own', self.pairs(piece.leg))  356 us
    ppermute x60, starting transfers between devices, begin(): lax.ppermute(piece.value, 'own', self.pairs(piece.leg))  187 us
    add x40, other arithmetic, finish(): piece.value = value + arrived  92.9 us
    dot_general x6, matrix products, times_transpose(): lax.dot_general(first_matrix, second_matrix, (((1,), (1,)), ((), ())), pr...  80.9 us
    dot_general x6, matrix products, contract_rows(): lax.dot_general(first_matrix, second_matrix, (((0,), (0,)), ((), ())), pr...  55 us
    pallas_call x1, Pallas kernels, attend_back(): pl.pallas_call(attend_back_kernel, grid=(H // HEADS_STEP,), in_specs=[pl....  49.3 us
    pallas_call x2, Pallas kernels, update_joined(): pl.pallas_call(functools.partial(update_kernel, learn_rate, WEIGHT_DECAY)...  45.5 us
    all_to_all x2, waiting for transfers between devices, shuffled(): return lax.all_to_all(blocks, 'dp', 0, 0)  38.5 us
  transfers between devices with their start and end apart: 78, of which 33 were waited for; matrix products, arithmetic and copies ran while one was open for 32% of the time, Pallas kernels for 10%

profile of v3, /device:TPU:0, one launch (start us, length us, event | category | flops | bytes accessed | tf_op | source)
XLA Modules:
  0.0 1336.4 jit_solution(5755669260234624561)
XLA Ops:
  47.8 17.8 %collective-permute-done.3 = bf16[32,5120]{1,0:T(8,128)(2,1)} collective-permute-done((bf16[32,5120]{1,0:T(8,128)(2,1)S(1)}, bf16[32,5120]{1,0:T(8,128)(2,1)}, u32[]{:S(2)}, u32[]{:S(2)}) %collective-permute-start.3) | collective-permute-done | bytes 327712 | tf_op jit(solution)/shard_map/ppermute | solution.py:66
  86.1 12.2 collective-permute-done.4
  122.9 21.2 %collective-permute-done.9 = bf16[32,5120]{1,0:T(8,128)(2,1)S(1)} collective-permute-done((bf16[32,5120]{1,0:T(8,128)(2,1)S(1)}, bf16[32,5120]{1,0:T(8,128)(2,1)S(1)}, u32[]{:S(2)}, u32[]{:S(2)}) %collective-permute-start.9) | collective-permute-done | bytes 327712 | tf_op jit(solution)/shard_map/ppermute | solution.py:66
  145.3 13.7 %collective-permute-done.11 = bf16[160,6400]{1,0:T(8,128)(2,1)} collective-permute-done((bf16[160,6400]{1,0:T(8,128)(2,1)S(1)}, bf16[160,6400]{1,0:T(8,128)(2,1)}, u32[]{:S(2)}, u32[]{:S(2)}) %collective-permute-start.11) | collective-permute-done | bytes 2048032 | tf_op jit(solution)/shard_map/ppermute | solution.py:66
  178.1 17.7 %all_gather.27 = bf16[1024,288]{1,0:T(8,128)(2,1)S(1)} all-gather(bf16[256,288]{1,0:T(8,128)(2,1)S(1)} %pad_maximum_fusion.12), channel_id=1, replica_groups=mesh['dp'=8,'own'=4] {'own'}, dimensions={0}, use_global_device_ids=true | all-gather | bytes 737280 | tf_op jit(solution)/shard_map/all_gather | solution.py:438
  210.9 24.1 %collective-permute-done.12 = bf16[320,2560]{1,0:T(8,128)(2,1)} collective-permute-done((bf16[320,2560]{1,0:T(8,128)(2,1)}, bf16[320,2560]{1,0:T(8,128)(2,1)}, u32[]{:S(2)}, u32[]{:S(2)}) %collective-permute-start.12) | collective-permute-done | bytes 1638432 | tf_op jit(solution)/shard_map/ppermute | solution.py:66
  267.1 19.1 %shard_map.518 = (bf16[1280,256]{1,0:T(8,128)(2,1)S(1)}, f32[20,1,256]{2,1,0:T(1,128)S(1)}) custom-call(bf16[3840,256]{1,0:T(8,128)(2,1)S(1)} %bitcast.330, bf16[1024,5120]{1,0:T(8,128)(2,1)} %convolution_convert_fusion.2.kv_ref, bf16[1024,128]{1,0:T(8,128)(2,1)S(1)} %pad.14.rope_ref, f32[1024,256]{1,0:T(8,128)S(1)} %compare_select_fusion.bias_ref), custom_call_target="tpu_custom_call" | custom-call | tf_op jit(solution)/shard_map/pallas_call | solution.py:256
  311.4 18.7 %shard_map.519 = (bf16[1280,256]{1,0:T(8,128)(2,1)S(1)}, f32[20,1,256]{2,1,0:T(1,128)S(1)}) custom-call(bf16[3840,256]{1,0:T(8,128)(2,1)S(1)} %bitcast.331, bf16[1024,5120]{1,0:T(8,128)(2,1)} %convolution_convert_fusion.2.kv_ref, bf16[1024,128]{1,0:T(8,128)(2,1)S(1)} %pad.14.rope_ref, f32[1024,256]{1,0:T(8,128)S(1)} %compare_select_fusion.bias_ref), custom_call_target="tpu_custom_call" | custom-call | tf_op jit(solution)/shard_map/pallas_call | solution.py:256
  374.8 24.5 %collective-permute-done.21 = bf16[160,6400]{1,0:T(8,128)(2,1)S(1)} collective-permute-done((bf16[160,6400]{1,0:T(8,128)(2,1)S(1)}, bf16[160,6400]{1,0:T(8,128)(2,1)S(1)}, u32[]{:S(2)}, u32[]{:S(2)}) %collective-permute-start.21) | collective-permute-done | bytes 2048032 | tf_op jit(solution)/shard_map/ppermute | solution.py:66
  454.7 13.2 collective-permute-done.24
  513.4 12.8 collective-permute-done.27
  531.6 14.5 %fusion.118 = f32[2048,800]{0,1:T(8,128)} fusion(bf16[2048,2560]{1,0:T(8,128)(2,1)} %all-gather.18.cloned.1.call-done, bf16[2560,800]{1,0:T(8,128)(2,1)} %bitcast.25), kind=kOutput, calls=%fused_computation.270 | convolution fusion | flops 8388608000 | bytes 21135360 | tf_op jit(solution)/shard_map/dot_general | solution.py:501
  546.1 18.0 %all-to-all-done.1 = bf16[320,8,800]{2,0,1:T(8,128)(2,1)} async-done(((bf16[320,8,800]{2,0,1:T(8,128)(2,1)}), bf16[320,8,800]{2,0,1:T(8,128)(2,1)}, u32[]{:S(2)}, u32[]{:S(2)}) %all-to-all-start.1) | async-done | bytes 4096032 | tf_op jit(solution)/shard_map/all_to_all | solution.py:498
  564.1 16.7 %multiply_convert_fusion.2 = (bf16[2048,800]{0,1:T(8,128)(2,1)}, f32[2048,800]{0,1:T(8,128)}) fusion(f32[2048,800]{0,1:T(8,128)} %fusion.118, bf16[2048,2560]{1,0:T(8,128)(2,1)} %all-gather.18.cloned.1.call-done, bf16[2560,800]{1,0:T(8,128)(2,1)} %bitcast.27), kind=kOutput, calls=%fused_computation.24 | convolution fusion | flops 8398438400 | bytes 30965760 | tf_op jit(solution)/shard_map/dot_general | solution.py:506
  580.8 12.5 convolution_convert_fusion.7
  604.0 18.5 %multiply_convert_fusion = (bf16[2048,800]{0,1:T(8,128)(2,1)}, bf16[2048,800]{0,1:T(8,128)(2,1)}) fusion(f32[2048,800]{0,1:T(8,128)} %fusion.118, f32[2048,800]{0,1:T(8,128)} %get-tuple-element.592, bf16[2048,2560]{1,0:T(8,128)(2,1)} %all-gather.10.cloned.1.call-done, bf16[400,2560]{1,0:T(8,128)(2,1)S(1)} %broadcast_select_fusion.6, ...), kind=kOutput, calls=%fused_computation.22 | convolution fusion | flops 8418099200 | bytes 34242560 | tf_op jit(solution)/shard_map/dot_general | solution.py:229
  622.6 18.0 %fusion.119 = f32[2048,2560]{1,0:T(8,128)} fusion(bf16[2048,800]{0,1:T(8,128)(2,1)} %get-tuple-element.331, bf16[2560,800]{1,0:T(8,128)(2,1)} %bitcast.27), kind=kOutput, calls=%fused_computation.271 | convolution fusion | flops 8388608000 | bytes 28344320 | tf_op jit(solution)/shard_map/dot_general | solution.py:229
  640.6 19.8 %add_convert_fusion = bf16[2048,2560]{1,0:T(8,128)(2,1)} fusion(f32[2048,2560]{1,0:T(8,128)} %fusion.119, bf16[2048,800]{0,1:T(8,128)(2,1)} %get-tuple-element.330, bf16[2560,800]{1,0:T(8,128)(2,1)} %bitcast.25), kind=kOutput, calls=%fused_computation | convolution fusion | flops 8399093760 | bytes 38830080 | tf_op jit(solution)/shard_map/dot_general | solution.py:229
  669.6 12.7 convolution_convert_fusion.6
  694.1 15.0 %collective-permute-done.32 = bf16[400,2560]{1,0:T(8,128)(2,1)S(1)} collective-permute-done((bf16[400,2560]{1,0:T(8,128)(2,1)S(1)}, bf16[400,2560]{1,0:T(8,128)(2,1)S(1)}, u32[]{:S(2)}, u32[]{:S(2)}) %collective-permute-start.32) | collective-permute-done | bytes 2048032 | tf_op jit(solution)/shard_map/ppermute | solution.py:66
  721.5 32.7 %collective-permute-done.33 = bf16[400,2560]{1,0:T(8,128)(2,1)S(1)} collective-permute-done((bf16[400,2560]{1,0:T(8,128)(2,1)S(1)}, bf16[400,2560]{1,0:T(8,128)(2,1)S(1)}, u32[]{:S(2)}, u32[]{:S(2)}) %collective-permute-start.33) | collective-permute-done | bytes 2048032 | tf_op jit(solution)/shard_map/ppermute | solution.py:66
  781.4 16.5 %convolution_convert_fusion.1 = bf16[2048,2560]{1,0:T(8,128)(2,1)} fusion(bf16[2048,800]{0,1:T(8,128)(2,1)} %get-tuple-element.328, bf16[400,2560]{1,0:T(8,128)(2,1)} %copy-done.84, bf16[400,2560]{1,0:T(8,128)(2,1)} %copy-done.82), kind=kOutput, calls=%fused_computation.4 | convolution fusion | flops 8402042880 | bytes 17858560 | tf_op jit(solution)/shard_map/dot_general | solution.py:532
  815.3 30.6 %collective-permute-done.36 = bf16[400,2560]{1,0:T(8,128)(2,1)S(1)} collective-permute-done((bf16[400,2560]{1,0:T(8,128)(2,1)S(1)}, bf16[400,2560]{1,0:T(8,128)(2,1)S(1)}, u32[]{:S(2)}, u32[]{:S(2)}) %collective-permute-start.36) | collective-permute-done | bytes 2048032 | tf_op jit(solution)/shard_map/ppermute | solution.py:66
  862.6 49.3 %shard_map.520 = (bf16[3840,256]{1,0:T(8,128)(2,1)S(1)}, bf16[1024,5120]{1,0:T(8,128)(2,1)}, f32[1024,128]{1,0:T(8,128)S(1)}) custom-call(bf16[3840,256]{1,0:T(8,128)(2,1)} %bitcast.332, bf16[1024,5120]{1,0:T(8,128)(2,1)} %convolution_convert_fusion.2.kv_ref, bf16[1024,128]{1,0:T(8,128)(2,1)S(1)} %copy-done.2, f32[1024,256]{1,0:T(8,128)S(1)} %compare_select_fusion.bias_ref, ...), custom_call_target="tpu_custom_call" | custom-call | tf_op jit(solution)/shard_map/pallas_call | solution.py:303
  962.5 20.6 %bitcast_select_fusion = (f32[800,2560]{1,0:T(8,128)}, f32[800,2560]{1,0:T(8,128)}, f32[800,2560]{1,0:T(8,128)}) fusion(f32[1,800,2560]{2,1,0:T(8,128)} %param.58, bf16[800,2560]{1,0:T(8,128)(2,1)} %pad_maximum_fusion.3, pred[]{:T(512)S(6)} %eq.32, f32[1,800,2560]{2,1,0:T(8,128)} %param.57, f32[1,800,2560]{2,1,0:T(8,128)} %param.56), kind=kLoop, calls=%fused_computation.8 | loop fusion | flops 36864000 | bytes 53248000 | tf_op jit(solution)/shard_map/jit(_where)/select_n | solution.py:339
  983.1 14.1 %collective-permute-done.42 = bf16[1280,800]{0,1:T(8,128)(2,1)} collective-permute-done((bf16[1280,800]{0,1:T(8,128)(2,1)}, bf16[1280,800]{0,1:T(8,128)(2,1)}, u32[]{:S(2)}, u32[]{:S(2)}) %collective-permute-start.42) | collective-permute-done | bytes 2048032 | tf_op jit(solution)/shard_map/ppermute | solution.py:66
  1016.9 30.5 %collective-permute-done.47 = bf16[320,2560]{1,0:T(8,128)(2,1)} collective-permute-done((bf16[320,2560]{1,0:T(8,128)(2,1)}, bf16[320,2560]{1,0:T(8,128)(2,1)}, u32[]{:S(2)}, u32[]{:S(2)}) %collective-permute-start.47) | collective-permute-done | bytes 1638432 | tf_op jit(solution)/shard_map/ppermute | solution.py:66
  1090.1 12.3 all-to-all-start.3
  1113.1 22.0 %collective-permute-done.50 = bf16[32,5120]{1,0:T(8,128)(2,1)S(1)} collective-permute-done((bf16[32,5120]{1,0:T(8,128)(2,1)S(1)}, bf16[32,5120]{1,0:T(8,128)(2,1)S(1)}, u32[]{:S(2)}, u32[]{:S(2)}) %collective-permute-start.50) | collective-permute-done | bytes 327712 | tf_op jit(solution)/shard_map/ppermute | solution.py:66
  1136.0 27.5 %all-to-all-done.3.blocks_ref = bf16[8,320,800]{2,1,0:T(8,128)(2,1)} async-done(((bf16[8,320,800]{2,1,0:T(8,128)(2,1)}), bf16[8,320,800]{2,1,0:T(8,128)(2,1)}, u32[]{:S(2)}, u32[]{:S(2)}) %all-to-all-start.3) | async-done | bytes 4096032 | tf_op jit(solution)/shard_map/all_to_all | solution.py:101
  1215.3 22.7 %shard_map.521 = (f32[320,6400]{1,0:T(8,128)}, f32[320,6400]{1,0:T(8,128)}, f32[320,6400]{1,0:T(8,128)}) custom-call(s32[1]{0:T(128)} %bitcast.62.owner_ref, bf16[8,320,800]{2,1,0:T(8,128)(2,1)} %all-to-all-done.3.blocks_ref, f32[320,6400]{1,0:T(8,128)} %bitcast.333, f32[320,6400]{1,0:T(8,128)} %bitcast.339, f32[320,6400]{1,0:T(8,128)} %bitcast.340), custom_call_target="tpu_custom_call" | custom-call | flops 40960000 | bytes 53248000 | tf_op jit(solution)/shard_map/pallas_call | solution.py:146
  1249.0 22.8 %shard_map.522 = (f32[320,6400]{1,0:T(8,128)}, f32[320,6400]{1,0:T(8,128)}, f32[320,6400]{1,0:T(8,128)}) custom-call(s32[1]{0:T(128)} %bitcast.68.owner_ref, bf16[8,320,800]{2,1,0:T(8,128)(2,1)} %all-to-all-done.4.blocks_ref, f32[320,6400]{1,0:T(8,128)} %bitcast.334, f32[320,6400]{1,0:T(8,128)} %bitcast.341, f32[320,6400]{1,0:T(8,128)} %bitcast.342), custom_call_target="tpu_custom_call" | custom-call | flops 40960000 | bytes 53248000 | tf_op jit(solution)/shard_map/pallas_call | solution.py:146
  (641 shorter events, 671.7 us)
Async XLA Ops:
  7.2 102.6 %all-gather.10.cloned.1.call-start = ((), (), s32[]{:S(2)}) async-start(), calls=%async_computation.12 | async-start | bytes 11796480 | tf_op jit(solution)/shard_map/all_gather | solution.py:173
  10.0 158.5 %all-gather.12.cloned.1.call-start = ((), (), s32[]{:S(2)}) async-start(), calls=%async_computation.13 | async-start | bytes 6635520 | tf_op jit(solution)/shard_map/all_gather | solution.py:173
  109.9 93.6 %all-gather.14.cloned.1.call-start = ((), (), s32[]{:S(2)}) async-start(), calls=%async_computation.14 | async-start | bytes 2949120 | tf_op jit(solution)/shard_map/all_gather | solution.py:173
  159.8 101.2 %all-gather.8.cloned.1.call-start = ((), (), s32[]{:S(2)}) async-start(), calls=%async_computation.11 | async-start | bytes 6635520 | tf_op jit(solution)/shard_map/all_gather | solution.py:173
  160.8 183.9 %all-gather.16.cloned.1.call-start = ((), (), s32[]{:S(2)}) async-start(), calls=%async_computation.15 | async-start | bytes 14745600 | tf_op jit(solution)/shard_map/all_gather | solution.py:173
  241.2 285.0 %all-gather.18.cloned.1.call-start = ((), (), s32[]{:S(2)}) async-start(), calls=%async_computation.16 | async-start | bytes 11796480 | tf_op jit(solution)/shard_map/all_gather | solution.py:173
  419.4 48.5 %collective-permute-start.24 = (bf16[160,6400]{1,0:T(8,128)(2,1)}, bf16[160,6400]{1,0:T(8,128)(2,1)}, u32[]{:S(2)}, u32[]{:S(2)}) collective-permute-start(bf16[160,6400]{1,0:T(8,128)(2,1)} %add.353), channel_id=1, source_target_pairs={{1,0},{2,3},{5,4},{6,7},{9,8},{10,11},{13,12},{14,15},{17,16},{18,... | collective-permute-start | bytes 6144008 | tf_op jit(solution)/shard_map/ppermute | solution.py:66
  420.7 47.2 %collective-permute-start.25 = (bf16[400,2560]{1,0:T(8,128)(2,1)}, bf16[400,2560]{1,0:T(8,128)(2,1)}, u32[]{:S(2)}, u32[]{:S(2)}) collective-permute-start(bf16[400,2560]{1,0:T(8,128)(2,1)} %add.354), channel_id=1, source_target_pairs={{1,2},{2,1},{5,6},{6,5},{9,10},{10,9},{13,14},{14,13},{17,18},{18,... | collective-permute-start | bytes 6144008 | tf_op jit(solution)/shard_map/ppermute | solution.py:66
  422.6 49.8 %collective-permute-start.26 = (bf16[400,2560]{1,0:T(8,128)(2,1)}, bf16[400,2560]{1,0:T(8,128)(2,1)}, u32[]{:S(2)}, u32[]{:S(2)}) collective-permute-start(bf16[400,2560]{1,0:T(8,128)(2,1)} %get-tuple-element.303), channel_id=1, source_target_pairs={{0,1},{3,2},{4,5},{7,6},{8,9},{11,10},{12,13},{15,14},{16,17},{19,... | collective-permute-start | bytes 6144008 | tf_op jit(solution)/shard_map/ppermute | solution.py:66
  448.1 58.1 %all-to-all-start = ((bf16[320,8,800]{2,0,1:T(8,128)(2,1)}), bf16[320,8,800]{2,0,1:T(8,128)(2,1)}, u32[]{:S(2)}, u32[]{:S(2)}) async-start(bf16[320,8,800]{2,0,1:T(8,128)(2,1)} %copy.117), calls=%async_computation | async-start | bytes 9175040 | tf_op jit(solution)/shard_map/all_to_all | solution.py:495
  479.1 47.1 %collective-permute-start.27 = (bf16[400,2560]{1,0:T(8,128)(2,1)S(1)}, bf16[400,2560]{1,0:T(8,128)(2,1)}, u32[]{:S(2)}, u32[]{:S(2)}) collective-permute-start(bf16[400,2560]{1,0:T(8,128)(2,1)S(1)} %add.355), channel_id=1, source_target_pairs={{1,0},{2,3},{5,4},{6,7},{9,8},{10,11},{13,12},{14,15},{17,16},{18,... | collective-permute-start | bytes 6144008 | tf_op jit(solution)/shard_map/ppermute | solution.py:66
  506.2 57.9 %all-to-all-start.1 = ((bf16[320,8,800]{2,0,1:T(8,128)(2,1)}), bf16[320,8,800]{2,0,1:T(8,128)(2,1)}, u32[]{:S(2)}, u32[]{:S(2)}) async-start(bf16[320,8,800]{2,0,1:T(8,128)(2,1)} %copy.118), calls=%async_computation.1 | async-start | bytes 9175040 | tf_op jit(solution)/shard_map/all_to_all | solution.py:498
  510.8 247.8 %reduce-scatter.7.cloned.1.call-start = ((), (), s32[]{:S(2)}) async-start(), calls=%async_computation.17 | async-start | bytes 11796480 | tf_op jit(solution)/shard_map/reduce_scatter | solution.py:177
  530.2 71.3 %collective-permute-start.29 = (bf16[400,2560]{1,0:T(8,128)(2,1)}, bf16[400,2560]{1,0:T(8,128)(2,1)}, u32[]{:S(2)}, u32[]{:S(2)}) collective-permute-start(bf16[400,2560]{1,0:T(8,128)(2,1)} %add.358), channel_id=1, source_target_pairs={{1,0},{2,3},{5,4},{6,7},{9,8},{10,11},{13,12},{14,15},{17,16},{18,... | collective-permute-start | bytes 6144008 | tf_op jit(solution)/shard_map/ppermute | solution.py:66
  660.5 260.2 %reduce-scatter.9.cloned.1.call-start = ((), (), s32[]{:S(2)}) async-start(), calls=%async_computation.18 | async-start | bytes 14745600 | tf_op jit(solution)/shard_map/reduce_scatter | solution.py:177
  781.4 234.5 %reduce-scatter.15.cloned.1.call-start = ((), (), s32[]{:S(2)}) async-start(), calls=%async_computation.21 | async-start | bytes 983040 | tf_op jit(solution)/shard_map/reduce_scatter | solution.py:591
  851.8 60.2 %collective-permute-start.39 = (bf16[1280,800]{0,1:T(8,128)(2,1)S(1)}, bf16[1280,800]{0,1:T(8,128)(2,1)S(1)}, u32[]{:S(2)}, u32[]{:S(2)}) collective-permute-start(bf16[1280,800]{0,1:T(8,128)(2,1)S(1)} %add.367), channel_id=1, source_target_pairs={{1,0},{2,3},{5,4},{6,7},{9,8},{10,11},{13,12},{14,15},{17,16},{18,... | collective-permute-start | bytes 6144008 | tf_op jit(solution)/shard_map/ppermute | solution.py:66
  853.2 58.8 %collective-permute-start.40 = (bf16[1280,800]{0,1:T(8,128)(2,1)S(1)}, bf16[1280,800]{0,1:T(8,128)(2,1)}, u32[]{:S(2)}, u32[]{:S(2)}) collective-permute-start(bf16[1280,800]{0,1:T(8,128)(2,1)S(1)} %add.368), channel_id=1, source_target_pairs={{1,2},{2,1},{5,6},{6,5},{9,10},{10,9},{13,14},{14,13},{17,18},{18,... | collective-permute-start | bytes 6144008 | tf_op jit(solution)/shard_map/ppermute | solution.py:66
  855.2 56.9 %collective-permute-start.41 = (bf16[1280,800]{0,1:T(8,128)(2,1)S(1)}, bf16[1280,800]{0,1:T(8,128)(2,1)}, u32[]{:S(2)}, u32[]{:S(2)}) collective-permute-start(bf16[1280,800]{0,1:T(8,128)(2,1)S(1)} %get-tuple-element.361), channel_id=1, source_target_pairs={{0,1},{3,2},{4,5},{7,6},{8,9},{11,10},{12,13},{15,14},{16,17},{19,... | collective-permute-start | bytes 6144008 | tf_op jit(solution)/shard_map/ppermute | solution.py:66
  920.7 154.7 %reduce-scatter.11.cloned.1.call-start = ((), (), s32[]{:S(2)}) async-start(), calls=%async_computation.19 | async-start | bytes 2949120 | tf_op jit(solution)/shard_map/reduce_scatter | solution.py:177
  929.3 146.0 %reduce-scatter.13.cloned.1.call-start = ((), (), s32[]{:S(2)}) async-start(), calls=%async_computation.20 | async-start | bytes 6635520 | tf_op jit(solution)/shard_map/reduce_scatter | solution.py:177
  937.0 199.0 %all-gather.20.cloned.1.call-start = ((), (), s32[]{:S(2)}) async-start(), calls=%async_computation.22 | async-start | bytes 4976640 | tf_op jit(solution)/shard_map/all_gather | solution.py:173
  949.0 48.1 %collective-permute-start.42 = (bf16[1280,800]{0,1:T(8,128)(2,1)}, bf16[1280,800]{0,1:T(8,128)(2,1)}, u32[]{:S(2)}, u32[]{:S(2)}) collective-permute-start(bf16[1280,800]{0,1:T(8,128)(2,1)} %add.369), channel_id=1, source_target_pairs={{1,0},{2,3},{5,4},{6,7},{9,8},{10,11},{13,12},{14,15},{17,16},{18,... | collective-permute-start | bytes 6144008 | tf_op jit(solution)/shard_map/ppermute | solution.py:66
  1075.4 60.5 %collective-permute-start.48 = (bf16[1280,800]{0,1:T(8,128)(2,1)}, bf16[1280,800]{0,1:T(8,128)(2,1)}, u32[]{:S(2)}, u32[]{:S(2)}) collective-permute-start(bf16[1280,800]{0,1:T(8,128)(2,1)} %add.378), channel_id=1, source_target_pairs={{1,0},{2,3},{5,4},{6,7},{9,8},{10,11},{13,12},{14,15},{17,16},{18,... | collective-permute-start | bytes 6144008 | tf_op jit(solution)/shard_map/ppermute | solution.py:66
  1078.6 57.3 %collective-permute-start.49 = (bf16[320,2560]{1,0:T(8,128)(2,1)}, bf16[320,2560]{1,0:T(8,128)(2,1)}, u32[]{:S(2)}, u32[]{:S(2)}) collective-permute-start(bf16[320,2560]{1,0:T(8,128)(2,1)} %add.379), channel_id=1, source_target_pairs={{1,2},{2,1},{5,6},{6,5},{9,10},{10,9},{13,14},{14,13},{17,18},{18,... | collective-permute-start | bytes 4915208 | tf_op jit(solution)/shard_map/ppermute | solution.py:66
  1090.1 73.4 %all-to-all-start.3 = ((bf16[8,320,800]{2,1,0:T(8,128)(2,1)}), bf16[8,320,800]{2,1,0:T(8,128)(2,1)}, u32[]{:S(2)}, u32[]{:S(2)}) async-start(bf16[8,320,800]{2,1,0:T(8,128)(2,1)} %bitcast.338), calls=%async_computation.9 | async-start | bytes 9175040 | tf_op jit(solution)/shard_map/all_to_all | solution.py:101
  1102.4 224.6 %reduce-scatter.17.cloned.1.call-start = ((), (), s32[]{:S(2)}) async-start(), calls=%async_computation.23 | async-start | bytes 11796480 | tf_op jit(solution)/shard_map/reduce_scatter | solution.py:177
  1175.6 73.4 %all-to-all-start.4 = ((bf16[8,320,800]{2,1,0:T(8,128)(2,1)}), bf16[8,320,800]{2,1,0:T(8,128)(2,1)}, u32[]{:S(2)}, u32[]{:S(2)}) async-start(bf16[8,320,800]{2,1,0:T(8,128)(2,1)} %bitcast.337), calls=%async_computation.10 | async-start | bytes 9175040 | tf_op jit(solution)/shard_map/all_to_all | solution.py:101
  1192.6 79.3 %collective-permute-start.52 = (bf16[320,2560]{1,0:T(8,128)(2,1)}, bf16[320,2560]{1,0:T(8,128)(2,1)}, u32[]{:S(2)}, u32[]{:S(2)}) collective-permute-start(bf16[320,2560]{1,0:T(8,128)(2,1)} %add.383), channel_id=1, source_target_pairs={{1,0},{2,3},{5,4},{6,7},{9,8},{10,11},{13,12},{14,15},{17,16},{18,... | collective-permute-start | bytes 4915208 | tf_op jit(solution)/shard_map/ppermute | solution.py:66
  1198.1 73.8 %collective-permute-start.53 = (bf16[32,5120]{1,0:T(8,128)(2,1)}, bf16[32,5120]{1,0:T(8,128)(2,1)}, u32[]{:S(2)}, u32[]{:S(2)}) collective-permute-start(bf16[32,5120]{1,0:T(8,128)(2,1)} %add.384), channel_id=1, source_target_pairs={{1,2},{2,1},{5,6},{6,5},{9,10},{10,9},{13,14},{14,13},{17,18},{18,... | collective-permute-start | bytes 983048 | tf_op jit(solution)/shard_map/ppermute | solution.py:66
  1199.5 72.4 %collective-permute-start.54 = (bf16[96,3840]{1,0:T(8,128)(2,1)S(1)}, bf16[96,3840]{1,0:T(8,128)(2,1)}, u32[]{:S(2)}, u32[]{:S(2)}) collective-permute-start(bf16[96,3840]{1,0:T(8,128)(2,1)S(1)} %add.385), channel_id=1, source_target_pairs={{1,2},{2,1},{5,6},{6,5},{9,10},{10,9},{13,14},{14,13},{17,18},{18,... | collective-permute-start | bytes 2211848 | tf_op jit(solution)/shard_map/ppermute | solution.py:66
  1201.0 70.9 %collective-permute-start.55 = (bf16[320,1059]{1,0:T(8,128)(2,1)}, bf16[320,1059]{1,0:T(8,128)(2,1)}, u32[]{:S(2)}, u32[]{:S(2)}) collective-permute-start(bf16[320,1059]{1,0:T(8,128)(2,1)} %pad_maximum_fusion.11), channel_id=1, source_target_pairs={{0,1},{3,2},{4,5},{7,6},{8,9},{11,10},{12,13},{15,14},{16,17},{19,... | collective-permute-start | bytes 2033288 | tf_op jit(solution)/shard_map/ppermute | solution.py:66
  (190 other events, 3999.7 us)
Sparse Core Ops, SparseCore 0:
  10.5 65.9 all-gather.9
  110.0 42.9 all-gather.11
  159.9 30.2 all-gather.13
  192.5 43.8 all-gather.7
  241.3 73.8 all-gather.15
  355.2 66.9 all-gather.17
  660.6 81.5 reduce-scatter.6
  781.5 103.3 reduce-scatter.8
  920.8 36.5 reduce-scatter.14
  961.1 41.3 reduce-scatter.10
  1006.6 59.6 reduce-scatter.12
  1068.6 54.8 all-gather.19
  1136.1 126.2 reduce-scatter.16

commit v4 on v3

--- a/solution.py
+++ b/solution.py
@@ -17,7 +17,7 @@
 KVR = 256
 FF = 6400
 GAINS = 6144
-HEADS_STEP = 2
+HEADS_STEP = 4
 LANES = 128
 STEP = 7
 
@@ -648,6 +648,8 @@
     line.begin(latents_sum)
     line.finish(input_grad)
     line.begin()
+    line.finish()
+    line.begin()
     line.finish(up_blocks)
     while line.active:
         line.round()

time: 1350 us -> 1350 us (level)
  no operation moved by 1% of the time
where the time goes in v4:
time: 1350 us; the launch traced here: 1330 us
  waiting for transfers between devices  421 us (31%)
  starting transfers between devices  219 us (16%)
  other arithmetic  214 us (16%)
  matrix products  214 us (16%)
  Pallas kernels  127 us (9%)
  local copies, waits for them, and re-layouts  99.7 us (7%)
  between operations  22.3 us (2%)
  blocking collectives  17.7 us (1%)
    ppermute x60, waiting for transfers between devices, begin(): lax.ppermute(piece.value, 'own', self.pairs(piece.leg))  358 us
    ppermute x60, starting transfers between devices, begin(): lax.ppermute(piece.value, 'own', self.pairs(piece.leg))  187 us
    add x40, other arithmetic, finish(): piece.value = value + arrived  92.9 us
    dot_general x6, matrix products, times_transpose(): lax.dot_general(first_matrix, second_matrix, (((1,), (1,)), ((), ())), pr...  80.9 us
    dot_general x6, matrix products, contract_rows(): lax.dot_general(first_matrix, second_matrix, (((0,), (0,)), ((), ())), pr...  55 us
    pallas_call x1, Pallas kernels, attend_back(): pl.pallas_call(attend_back_kernel, grid=(H // HEADS_STEP,), in_specs=[pl....  48 us
    all_to_all x2, waiting for transfers between devices, shuffled(): return lax.all_to_all(blocks, 'dp', 0, 0)  42.1 us
    pallas_call x2, Pallas kernels, update_joined(): pl.pallas_call(functools.partial(update_kernel, learn_rate, WEIGHT_DECAY)...  41.9 us
  transfers between devices with their start and end apart: 78, of which 33 were waited for; matrix products, arithmetic and copies ran while one was open for 32% of the time, Pallas kernels for 10%

profile of v4, /device:TPU:0, one launch (start us, length us, event | category | flops | bytes accessed | tf_op | source)
XLA Modules:
  0.0 1334.7 jit_solution(17577125151902084068)
XLA Ops:
  47.8 17.8 %collective-permute-done.3 = bf16[32,5120]{1,0:T(8,128)(2,1)} collective-permute-done((bf16[32,5120]{1,0:T(8,128)(2,1)S(1)}, bf16[32,5120]{1,0:T(8,128)(2,1)}, u32[]{:S(2)}, u32[]{:S(2)}) %collective-permute-start.3) | collective-permute-done | bytes 327712 | tf_op jit(solution)/shard_map/ppermute | solution.py:66
  122.9 21.2 %collective-permute-done.9 = bf16[32,5120]{1,0:T(8,128)(2,1)S(1)} collective-permute-done((bf16[32,5120]{1,0:T(8,128)(2,1)S(1)}, bf16[32,5120]{1,0:T(8,128)(2,1)S(1)}, u32[]{:S(2)}, u32[]{:S(2)}) %collective-permute-start.9) | collective-permute-done | bytes 327712 | tf_op jit(solution)/shard_map/ppermute | solution.py:66
  145.3 13.7 %collective-permute-done.11 = bf16[160,6400]{1,0:T(8,128)(2,1)} collective-permute-done((bf16[160,6400]{1,0:T(8,128)(2,1)S(1)}, bf16[160,6400]{1,0:T(8,128)(2,1)}, u32[]{:S(2)}, u32[]{:S(2)}) %collective-permute-start.11) | collective-permute-done | bytes 2048032 | tf_op jit(solution)/shard_map/ppermute | solution.py:66
  178.1 17.7 %all_gather.27 = bf16[1024,288]{1,0:T(8,128)(2,1)S(1)} all-gather(bf16[256,288]{1,0:T(8,128)(2,1)S(1)} %pad_maximum_fusion.12), channel_id=1, replica_groups=mesh['dp'=8,'own'=4] {'own'}, dimensions={0}, use_global_device_ids=true | all-gather | bytes 737280 | tf_op jit(solution)/shard_map/all_gather | solution.py:438
  210.9 24.1 %collective-permute-done.12 = bf16[320,2560]{1,0:T(8,128)(2,1)} collective-permute-done((bf16[320,2560]{1,0:T(8,128)(2,1)}, bf16[320,2560]{1,0:T(8,128)(2,1)}, u32[]{:S(2)}, u32[]{:S(2)}) %collective-permute-start.12) | collective-permute-done | bytes 1638432 | tf_op jit(solution)/shard_map/ppermute | solution.py:66
  267.1 18.9 %shard_map.518 = (bf16[1280,256]{1,0:T(8,128)(2,1)S(1)}, f32[20,1,256]{2,1,0:T(1,128)S(1)}) custom-call(bf16[3840,256]{1,0:T(8,128)(2,1)S(1)} %bitcast.330, bf16[1024,5120]{1,0:T(8,128)(2,1)} %convolution_convert_fusion.2.kv_ref, bf16[1024,128]{1,0:T(8,128)(2,1)S(1)} %pad.14.rope_ref, f32[1024,256]{1,0:T(8,128)S(1)} %compare_select_fusion.bias_ref), custom_call_target="tpu_custom_call" | custom-call | tf_op jit(solution)/shard_map/pallas_call | solution.py:256
  311.8 18.2 %shard_map.519 = (bf16[1280,256]{1,0:T(8,128)(2,1)S(1)}, f32[20,1,256]{2,1,0:T(1,128)S(1)}) custom-call(bf16[3840,256]{1,0:T(8,128)(2,1)S(1)} %bitcast.331, bf16[1024,5120]{1,0:T(8,128)(2,1)} %convolution_convert_fusion.2.kv_ref, bf16[1024,128]{1,0:T(8,128)(2,1)S(1)} %pad.14.rope_ref, f32[1024,256]{1,0:T(8,128)S(1)} %compare_select_fusion.bias_ref), custom_call_target="tpu_custom_call" | custom-call | tf_op jit(solution)/shard_map/pallas_call | solution.py:256
  374.8 24.4 %collective-permute-done.21 = bf16[160,6400]{1,0:T(8,128)(2,1)S(1)} collective-permute-done((bf16[160,6400]{1,0:T(8,128)(2,1)S(1)}, bf16[160,6400]{1,0:T(8,128)(2,1)S(1)}, u32[]{:S(2)}, u32[]{:S(2)}) %collective-permute-start.21) | collective-permute-done | bytes 2048032 | tf_op jit(solution)/shard_map/ppermute | solution.py:66
  454.2 13.6 %collective-permute-done.24 = bf16[160,6400]{1,0:T(8,128)(2,1)} collective-permute-done((bf16[160,6400]{1,0:T(8,128)(2,1)}, bf16[160,6400]{1,0:T(8,128)(2,1)}, u32[]{:S(2)}, u32[]{:S(2)}) %collective-permute-start.24) | collective-permute-done | bytes 2048032 | tf_op jit(solution)/shard_map/ppermute | solution.py:66
  512.9 13.8 %collective-permute-done.27 = bf16[400,2560]{1,0:T(8,128)(2,1)} collective-permute-done((bf16[400,2560]{1,0:T(8,128)(2,1)S(1)}, bf16[400,2560]{1,0:T(8,128)(2,1)}, u32[]{:S(2)}, u32[]{:S(2)}) %collective-permute-start.27) | collective-permute-done | bytes 2048032 | tf_op jit(solution)/shard_map/ppermute | solution.py:66
  532.0 14.5 %fusion.118 = f32[2048,800]{0,1:T(8,128)} fusion(bf16[2048,2560]{1,0:T(8,128)(2,1)} %all-gather.18.cloned.1.call-done, bf16[2560,800]{1,0:T(8,128)(2,1)} %bitcast.25), kind=kOutput, calls=%fused_computation.270 | convolution fusion | flops 8388608000 | bytes 21135360 | tf_op jit(solution)/shard_map/dot_general | solution.py:501
  546.5 17.1 %all-to-all-done.1 = bf16[320,8,800]{2,0,1:T(8,128)(2,1)} async-done(((bf16[320,8,800]{2,0,1:T(8,128)(2,1)}), bf16[320,8,800]{2,0,1:T(8,128)(2,1)}, u32[]{:S(2)}, u32[]{:S(2)}) %all-to-all-start.1) | async-done | bytes 4096032 | tf_op jit(solution)/shard_map/all_to_all | solution.py:498
  563.7 16.7 %multiply_convert_fusion.2 = (bf16[2048,800]{0,1:T(8,128)(2,1)}, f32[2048,800]{0,1:T(8,128)}) fusion(f32[2048,800]{0,1:T(8,128)} %fusion.118, bf16[2048,2560]{1,0:T(8,128)(2,1)} %all-gather.18.cloned.1.call-done, bf16[2560,800]{1,0:T(8,128)(2,1)} %bitcast.27), kind=kOutput, calls=%fused_computation.24 | convolution fusion | flops 8398438400 | bytes 30965760 | tf_op jit(solution)/shard_map/dot_general | solution.py:506
  580.4 12.5 convolution_convert_fusion.7
  604.0 18.5 %multiply_convert_fusion = (bf16[2048,800]{0,1:T(8,128)(2,1)}, bf16[2048,800]{0,1:T(8,128)(2,1)}) fusion(f32[2048,800]{0,1:T(8,128)} %fusion.118, f32[2048,800]{0,1:T(8,128)} %get-tuple-element.588, bf16[2048,2560]{1,0:T(8,128)(2,1)} %all-gather.10.cloned.1.call-done, bf16[400,2560]{1,0:T(8,128)(2,1)S(1)} %broadcast_select_fusion.6, ...), kind=kOutput, calls=%fused_computation.22 | convolution fusion | flops 8418099200 | bytes 34242560 | tf_op jit(solution)/shard_map/dot_general | solution.py:229
  622.6 18.0 %fusion.119 = f32[2048,2560]{1,0:T(8,128)} fusion(bf16[2048,800]{0,1:T(8,128)(2,1)} %get-tuple-element.329, bf16[2560,800]{1,0:T(8,128)(2,1)} %bitcast.27), kind=kOutput, calls=%fused_computation.271 | convolution fusion | flops 8388608000 | bytes 28344320 | tf_op jit(solution)/shard_map/dot_general | solution.py:229
  640.6 19.8 %add_convert_fusion = bf16[2048,2560]{1,0:T(8,128)(2,1)} fusion(f32[2048,2560]{1,0:T(8,128)} %fusion.119, bf16[2048,800]{0,1:T(8,128)(2,1)} %get-tuple-element.328, bf16[2560,800]{1,0:T(8,128)(2,1)} %bitcast.25), kind=kOutput, calls=%fused_computation | convolution fusion | flops 8399093760 | bytes 38830080 | tf_op jit(solution)/shard_map/dot_general | solution.py:229
  669.5 12.7 convolution_convert_fusion.6
  694.0 15.1 %collective-permute-done.32 = bf16[400,2560]{1,0:T(8,128)(2,1)S(1)} collective-permute-done((bf16[400,2560]{1,0:T(8,128)(2,1)S(1)}, bf16[400,2560]{1,0:T(8,128)(2,1)S(1)}, u32[]{:S(2)}, u32[]{:S(2)}) %collective-permute-start.32) | collective-permute-done | bytes 2048032 | tf_op jit(solution)/shard_map/ppermute | solution.py:66
  721.5 32.6 %collective-permute-done.33 = bf16[400,2560]{1,0:T(8,128)(2,1)S(1)} collective-permute-done((bf16[400,2560]{1,0:T(8,128)(2,1)S(1)}, bf16[400,2560]{1,0:T(8,128)(2,1)S(1)}, u32[]{:S(2)}, u32[]{:S(2)}) %collective-permute-start.33) | collective-permute-done | bytes 2048032 | tf_op jit(solution)/shard_map/ppermute | solution.py:66
  781.4 16.5 %convolution_convert_fusion.1 = bf16[2048,2560]{1,0:T(8,128)(2,1)} fusion(bf16[2048,800]{0,1:T(8,128)(2,1)} %get-tuple-element.326, bf16[400,2560]{1,0:T(8,128)(2,1)} %copy-done.84, bf16[400,2560]{1,0:T(8,128)(2,1)} %copy-done.82), kind=kOutput, calls=%fused_computation.4 | convolution fusion | flops 8402042880 | bytes 17858560 | tf_op jit(solution)/shard_map/dot_general | solution.py:532
  815.2 30.7 %collective-permute-done.36 = bf16[400,2560]{1,0:T(8,128)(2,1)S(1)} collective-permute-done((bf16[400,2560]{1,0:T(8,128)(2,1)S(1)}, bf16[400,2560]{1,0:T(8,128)(2,1)S(1)}, u32[]{:S(2)}, u32[]{:S(2)}) %collective-permute-start.36) | collective-permute-done | bytes 2048032 | tf_op jit(solution)/shard_map/ppermute | solution.py:66
  862.6 48.0 %shard_map.520 = (bf16[3840,256]{1,0:T(8,128)(2,1)S(1)}, bf16[1024,5120]{1,0:T(8,128)(2,1)}, f32[1024,128]{1,0:T(8,128)S(1)}) custom-call(bf16[3840,256]{1,0:T(8,128)(2,1)} %bitcast.332, bf16[1024,5120]{1,0:T(8,128)(2,1)} %convolution_convert_fusion.2.kv_ref, bf16[1024,128]{1,0:T(8,128)(2,1)S(1)} %copy-done.2, f32[1024,256]{1,0:T(8,128)S(1)} %compare_select_fusion.bias_ref, ...), custom_call_target="tpu_custom_call" | custom-call | tf_op jit(solution)/shard_map/pallas_call | solution.py:303
  960.9 20.6 %bitcast_select_fusion = (f32[800,2560]{1,0:T(8,128)}, f32[800,2560]{1,0:T(8,128)}, f32[800,2560]{1,0:T(8,128)}) fusion(f32[1,800,2560]{2,1,0:T(8,128)} %param.58, bf16[800,2560]{1,0:T(8,128)(2,1)} %pad_maximum_fusion.3, pred[]{:T(512)S(6)} %eq.32, f32[1,800,2560]{2,1,0:T(8,128)} %param.57, f32[1,800,2560]{2,1,0:T(8,128)} %param.56), kind=kLoop, calls=%fused_computation.8 | loop fusion | flops 36864000 | bytes 53248000 | tf_op jit(solution)/shard_map/jit(_where)/select_n | solution.py:339
  981.5 14.0 %collective-permute-done.42 = bf16[1280,800]{0,1:T(8,128)(2,1)} collective-permute-done((bf16[1280,800]{0,1:T(8,128)(2,1)}, bf16[1280,800]{0,1:T(8,128)(2,1)}, u32[]{:S(2)}, u32[]{:S(2)}) %collective-permute-start.42) | collective-permute-done | bytes 2048032 | tf_op jit(solution)/shard_map/ppermute | solution.py:66
  1015.2 30.5 %collective-permute-done.47 = bf16[320,2560]{1,0:T(8,128)(2,1)} collective-permute-done((bf16[320,2560]{1,0:T(8,128)(2,1)}, bf16[320,2560]{1,0:T(8,128)(2,1)}, u32[]{:S(2)}, u32[]{:S(2)}) %collective-permute-start.47) | collective-permute-done | bytes 1638432 | tf_op jit(solution)/shard_map/ppermute | solution.py:66
  1088.4 12.5 all-to-all-start.3
  1111.3 22.0 %collective-permute-done.50 = bf16[32,5120]{1,0:T(8,128)(2,1)S(1)} collective-permute-done((bf16[32,5120]{1,0:T(8,128)(2,1)S(1)}, bf16[32,5120]{1,0:T(8,128)(2,1)S(1)}, u32[]{:S(2)}, u32[]{:S(2)}) %collective-permute-start.50) | collective-permute-done | bytes 327712 | tf_op jit(solution)/shard_map/ppermute | solution.py:66
  1134.2 27.5 %all-to-all-done.3.blocks_ref = bf16[8,320,800]{2,1,0:T(8,128)(2,1)} async-done(((bf16[8,320,800]{2,1,0:T(8,128)(2,1)}), bf16[8,320,800]{2,1,0:T(8,128)(2,1)}, u32[]{:S(2)}, u32[]{:S(2)}) %all-to-all-start.3) | async-done | bytes 4096032 | tf_op jit(solution)/shard_map/all_to_all | solution.py:101
  1213.6 19.1 %shard_map.521 = (f32[320,6400]{1,0:T(8,128)}, f32[320,6400]{1,0:T(8,128)}, f32[320,6400]{1,0:T(8,128)}) custom-call(s32[1]{0:T(128)} %bitcast.62.owner_ref, bf16[8,320,800]{2,1,0:T(8,128)(2,1)} %all-to-all-done.3.blocks_ref, f32[320,6400]{1,0:T(8,128)} %bitcast.333, f32[320,6400]{1,0:T(8,128)} %bitcast.339, f32[320,6400]{1,0:T(8,128)} %bitcast.340), custom_call_target="tpu_custom_call" | custom-call | flops 40960000 | bytes 53248000 | tf_op jit(solution)/shard_map/pallas_call | solution.py:146
  1232.7 14.6 %all-to-all-done.4.blocks_ref = bf16[8,320,800]{2,1,0:T(8,128)(2,1)} async-done(((bf16[8,320,800]{2,1,0:T(8,128)(2,1)}), bf16[8,320,800]{2,1,0:T(8,128)(2,1)}, u32[]{:S(2)}, u32[]{:S(2)}) %all-to-all-start.4) | async-done | bytes 4096032 | tf_op jit(solution)/shard_map/all_to_all | solution.py:101
  1247.3 22.8 %shard_map.522 = (f32[320,6400]{1,0:T(8,128)}, f32[320,6400]{1,0:T(8,128)}, f32[320,6400]{1,0:T(8,128)}) custom-call(s32[1]{0:T(128)} %bitcast.68.owner_ref, bf16[8,320,800]{2,1,0:T(8,128)(2,1)} %all-to-all-done.4.blocks_ref, f32[320,6400]{1,0:T(8,128)} %bitcast.334, f32[320,6400]{1,0:T(8,128)} %bitcast.341, f32[320,6400]{1,0:T(8,128)} %bitcast.342), custom_call_target="tpu_custom_call" | custom-call | flops 40960000 | bytes 53248000 | tf_op jit(solution)/shard_map/pallas_call | solution.py:146
  (641 shorter events, 672.6 us)
Async XLA Ops:
  7.2 102.6 %all-gather.10.cloned.1.call-start = ((), (), s32[]{:S(2)}) async-start(), calls=%async_computation.12 | async-start | bytes 11796480 | tf_op jit(solution)/shard_map/all_gather | solution.py:173
  10.0 158.5 %all-gather.12.cloned.1.call-start = ((), (), s32[]{:S(2)}) async-start(), calls=%async_computation.13 | async-start | bytes 6635520 | tf_op jit(solution)/shard_map/all_gather | solution.py:173
  109.9 93.6 %all-gather.14.cloned.1.call-start = ((), (), s32[]{:S(2)}) async-start(), calls=%async_computation.14 | async-start | bytes 2949120 | tf_op jit(solution)/shard_map/all_gather | solution.py:173
  159.8 101.2 %all-gather.8.cloned.1.call-start = ((), (), s32[]{:S(2)}) async-start(), calls=%async_computation.11 | async-start | bytes 6635520 | tf_op jit(solution)/shard_map/all_gather | solution.py:173
  160.8 183.9 %all-gather.16.cloned.1.call-start = ((), (), s32[]{:S(2)}) async-start(), calls=%async_computation.15 | async-start | bytes 14745600 | tf_op jit(solution)/shard_map/all_gather | solution.py:173
  241.2 285.5 %all-gather.18.cloned.1.call-start = ((), (), s32[]{:S(2)}) async-start(), calls=%async_computation.16 | async-start | bytes 11796480 | tf_op jit(solution)/shard_map/all_gather | solution.py:173
  418.8 49.0 %collective-permute-start.24 = (bf16[160,6400]{1,0:T(8,128)(2,1)}, bf16[160,6400]{1,0:T(8,128)(2,1)}, u32[]{:S(2)}, u32[]{:S(2)}) collective-permute-start(bf16[160,6400]{1,0:T(8,128)(2,1)} %add.353), channel_id=1, source_target_pairs={{1,0},{2,3},{5,4},{6,7},{9,8},{10,11},{13,12},{14,15},{17,16},{18,... | collective-permute-start | bytes 6144008 | tf_op jit(solution)/shard_map/ppermute | solution.py:66
  420.1 47.7 %collective-permute-start.25 = (bf16[400,2560]{1,0:T(8,128)(2,1)}, bf16[400,2560]{1,0:T(8,128)(2,1)}, u32[]{:S(2)}, u32[]{:S(2)}) collective-permute-start(bf16[400,2560]{1,0:T(8,128)(2,1)} %add.354), channel_id=1, source_target_pairs={{1,2},{2,1},{5,6},{6,5},{9,10},{10,9},{13,14},{14,13},{17,18},{18,... | collective-permute-start | bytes 6144008 | tf_op jit(solution)/shard_map/ppermute | solution.py:66
  422.1 50.3 %collective-permute-start.26 = (bf16[400,2560]{1,0:T(8,128)(2,1)}, bf16[400,2560]{1,0:T(8,128)(2,1)}, u32[]{:S(2)}, u32[]{:S(2)}) collective-permute-start(bf16[400,2560]{1,0:T(8,128)(2,1)} %get-tuple-element.301), channel_id=1, source_target_pairs={{0,1},{3,2},{4,5},{7,6},{8,9},{11,10},{12,13},{15,14},{16,17},{19,... | collective-permute-start | bytes 6144008 | tf_op jit(solution)/shard_map/ppermute | solution.py:66
  447.5 58.2 %all-to-all-start = ((bf16[320,8,800]{2,0,1:T(8,128)(2,1)}), bf16[320,8,800]{2,0,1:T(8,128)(2,1)}, u32[]{:S(2)}, u32[]{:S(2)}) async-start(bf16[320,8,800]{2,0,1:T(8,128)(2,1)} %copy.117), calls=%async_computation | async-start | bytes 9175040 | tf_op jit(solution)/shard_map/all_to_all | solution.py:495
  479.0 47.7 %collective-permute-start.27 = (bf16[400,2560]{1,0:T(8,128)(2,1)S(1)}, bf16[400,2560]{1,0:T(8,128)(2,1)}, u32[]{:S(2)}, u32[]{:S(2)}) collective-permute-start(bf16[400,2560]{1,0:T(8,128)(2,1)S(1)} %add.355), channel_id=1, source_target_pairs={{1,0},{2,3},{5,4},{6,7},{9,8},{10,11},{13,12},{14,15},{17,16},{18,... | collective-permute-start | bytes 6144008 | tf_op jit(solution)/shard_map/ppermute | solution.py:66
  505.7 57.9 %all-to-all-start.1 = ((bf16[320,8,800]{2,0,1:T(8,128)(2,1)}), bf16[320,8,800]{2,0,1:T(8,128)(2,1)}, u32[]{:S(2)}, u32[]{:S(2)}) async-start(bf16[320,8,800]{2,0,1:T(8,128)(2,1)} %copy.118), calls=%async_computation.1 | async-start | bytes 9175040 | tf_op jit(solution)/shard_map/all_to_all | solution.py:498
  510.3 248.3 %reduce-scatter.7.cloned.1.call-start = ((), (), s32[]{:S(2)}) async-start(), calls=%async_computation.17 | async-start | bytes 11796480 | tf_op jit(solution)/shard_map/reduce_scatter | solution.py:177
  530.7 70.7 %collective-permute-start.29 = (bf16[400,2560]{1,0:T(8,128)(2,1)}, bf16[400,2560]{1,0:T(8,128)(2,1)}, u32[]{:S(2)}, u32[]{:S(2)}) collective-permute-start(bf16[400,2560]{1,0:T(8,128)(2,1)} %add.358), channel_id=1, source_target_pairs={{1,0},{2,3},{5,4},{6,7},{9,8},{10,11},{13,12},{14,15},{17,16},{18,... | collective-permute-start | bytes 6144008 | tf_op jit(solution)/shard_map/ppermute | solution.py:66
  660.5 258.8 %reduce-scatter.9.cloned.1.call-start = ((), (), s32[]{:S(2)}) async-start(), calls=%async_computation.18 | async-start | bytes 14745600 | tf_op jit(solution)/shard_map/reduce_scatter | solution.py:177
  781.4 232.8 %reduce-scatter.15.cloned.1.call-start = ((), (), s32[]{:S(2)}) async-start(), calls=%async_computation.21 | async-start | bytes 983040 | tf_op jit(solution)/shard_map/reduce_scatter | solution.py:591
  851.7 58.9 %collective-permute-start.39 = (bf16[1280,800]{0,1:T(8,128)(2,1)S(1)}, bf16[1280,800]{0,1:T(8,128)(2,1)S(1)}, u32[]{:S(2)}, u32[]{:S(2)}) collective-permute-start(bf16[1280,800]{0,1:T(8,128)(2,1)S(1)} %add.367), channel_id=1, source_target_pairs={{1,0},{2,3},{5,4},{6,7},{9,8},{10,11},{13,12},{14,15},{17,16},{18,... | collective-permute-start | bytes 6144008 | tf_op jit(solution)/shard_map/ppermute | solution.py:66
  853.1 57.5 %collective-permute-start.40 = (bf16[1280,800]{0,1:T(8,128)(2,1)S(1)}, bf16[1280,800]{0,1:T(8,128)(2,1)}, u32[]{:S(2)}, u32[]{:S(2)}) collective-permute-start(bf16[1280,800]{0,1:T(8,128)(2,1)S(1)} %add.368), channel_id=1, source_target_pairs={{1,2},{2,1},{5,6},{6,5},{9,10},{10,9},{13,14},{14,13},{17,18},{18,... | collective-permute-start | bytes 6144008 | tf_op jit(solution)/shard_map/ppermute | solution.py:66
  855.1 55.5 %collective-permute-start.41 = (bf16[1280,800]{0,1:T(8,128)(2,1)S(1)}, bf16[1280,800]{0,1:T(8,128)(2,1)}, u32[]{:S(2)}, u32[]{:S(2)}) collective-permute-start(bf16[1280,800]{0,1:T(8,128)(2,1)S(1)} %get-tuple-element.359), channel_id=1, source_target_pairs={{0,1},{3,2},{4,5},{7,6},{8,9},{11,10},{12,13},{15,14},{16,17},{19,... | collective-permute-start | bytes 6144008 | tf_op jit(solution)/shard_map/ppermute | solution.py:66
  919.3 154.3 %reduce-scatter.11.cloned.1.call-start = ((), (), s32[]{:S(2)}) async-start(), calls=%async_computation.19 | async-start | bytes 2949120 | tf_op jit(solution)/shard_map/reduce_scatter | solution.py:177
  928.0 145.6 %reduce-scatter.13.cloned.1.call-start = ((), (), s32[]{:S(2)}) async-start(), calls=%async_computation.20 | async-start | bytes 6635520 | tf_op jit(solution)/shard_map/reduce_scatter | solution.py:177
  935.8 198.4 %all-gather.20.cloned.1.call-start = ((), (), s32[]{:S(2)}) async-start(), calls=%async_computation.22 | async-start | bytes 4976640 | tf_op jit(solution)/shard_map/all_gather | solution.py:173
  947.6 47.8 %collective-permute-start.42 = (bf16[1280,800]{0,1:T(8,128)(2,1)}, bf16[1280,800]{0,1:T(8,128)(2,1)}, u32[]{:S(2)}, u32[]{:S(2)}) collective-permute-start(bf16[1280,800]{0,1:T(8,128)(2,1)} %add.369), channel_id=1, source_target_pairs={{1,0},{2,3},{5,4},{6,7},{9,8},{10,11},{13,12},{14,15},{17,16},{18,... | collective-permute-start | bytes 6144008 | tf_op jit(solution)/shard_map/ppermute | solution.py:66
  1073.6 60.5 %collective-permute-start.48 = (bf16[1280,800]{0,1:T(8,128)(2,1)}, bf16[1280,800]{0,1:T(8,128)(2,1)}, u32[]{:S(2)}, u32[]{:S(2)}) collective-permute-start(bf16[1280,800]{0,1:T(8,128)(2,1)} %add.378), channel_id=1, source_target_pairs={{1,0},{2,3},{5,4},{6,7},{9,8},{10,11},{13,12},{14,15},{17,16},{18,... | collective-permute-start | bytes 6144008 | tf_op jit(solution)/shard_map/ppermute | solution.py:66
  1076.8 57.3 %collective-permute-start.49 = (bf16[320,2560]{1,0:T(8,128)(2,1)}, bf16[320,2560]{1,0:T(8,128)(2,1)}, u32[]{:S(2)}, u32[]{:S(2)}) collective-permute-start(bf16[320,2560]{1,0:T(8,128)(2,1)} %add.379), channel_id=1, source_target_pairs={{1,2},{2,1},{5,6},{6,5},{9,10},{10,9},{13,14},{14,13},{17,18},{18,... | collective-permute-start | bytes 4915208 | tf_op jit(solution)/shard_map/ppermute | solution.py:66
  1088.4 73.3 %all-to-all-start.3 = ((bf16[8,320,800]{2,1,0:T(8,128)(2,1)}), bf16[8,320,800]{2,1,0:T(8,128)(2,1)}, u32[]{:S(2)}, u32[]{:S(2)}) async-start(bf16[8,320,800]{2,1,0:T(8,128)(2,1)} %bitcast.338), calls=%async_computation.9 | async-start | bytes 9175040 | tf_op jit(solution)/shard_map/all_to_all | solution.py:101
  1100.8 224.4 %reduce-scatter.17.cloned.1.call-start = ((), (), s32[]{:S(2)}) async-start(), calls=%async_computation.23 | async-start | bytes 11796480 | tf_op jit(solution)/shard_map/reduce_scatter | solution.py:177
  1173.9 73.4 %all-to-all-start.4 = ((bf16[8,320,800]{2,1,0:T(8,128)(2,1)}), bf16[8,320,800]{2,1,0:T(8,128)(2,1)}, u32[]{:S(2)}, u32[]{:S(2)}) async-start(bf16[8,320,800]{2,1,0:T(8,128)(2,1)} %bitcast.337), calls=%async_computation.10 | async-start | bytes 9175040 | tf_op jit(solution)/shard_map/all_to_all | solution.py:101
  1190.8 79.3 %collective-permute-start.52 = (bf16[320,2560]{1,0:T(8,128)(2,1)}, bf16[320,2560]{1,0:T(8,128)(2,1)}, u32[]{:S(2)}, u32[]{:S(2)}) collective-permute-start(bf16[320,2560]{1,0:T(8,128)(2,1)} %add.383), channel_id=1, source_target_pairs={{1,0},{2,3},{5,4},{6,7},{9,8},{10,11},{13,12},{14,15},{17,16},{18,... | collective-permute-start | bytes 4915208 | tf_op jit(solution)/shard_map/ppermute | solution.py:66
  1196.3 73.8 %collective-permute-start.53 = (bf16[32,5120]{1,0:T(8,128)(2,1)}, bf16[32,5120]{1,0:T(8,128)(2,1)}, u32[]{:S(2)}, u32[]{:S(2)}) collective-permute-start(bf16[32,5120]{1,0:T(8,128)(2,1)} %add.384), channel_id=1, source_target_pairs={{1,2},{2,1},{5,6},{6,5},{9,10},{10,9},{13,14},{14,13},{17,18},{18,... | collective-permute-start | bytes 983048 | tf_op jit(solution)/shard_map/ppermute | solution.py:66
  1197.7 72.4 %collective-permute-start.54 = (bf16[96,3840]{1,0:T(8,128)(2,1)S(1)}, bf16[96,3840]{1,0:T(8,128)(2,1)}, u32[]{:S(2)}, u32[]{:S(2)}) collective-permute-start(bf16[96,3840]{1,0:T(8,128)(2,1)S(1)} %add.385), channel_id=1, source_target_pairs={{1,2},{2,1},{5,6},{6,5},{9,10},{10,9},{13,14},{14,13},{17,18},{18,... | collective-permute-start | bytes 2211848 | tf_op jit(solution)/shard_map/ppermute | solution.py:66
  1199.2 70.9 %collective-permute-start.55 = (bf16[320,1059]{1,0:T(8,128)(2,1)}, bf16[320,1059]{1,0:T(8,128)(2,1)}, u32[]{:S(2)}, u32[]{:S(2)}) collective-permute-start(bf16[320,1059]{1,0:T(8,128)(2,1)} %pad_maximum_fusion.11), channel_id=1, source_target_pairs={{0,1},{3,2},{4,5},{7,6},{8,9},{11,10},{12,13},{15,14},{16,17},{19,... | collective-permute-start | bytes 2033288 | tf_op jit(solution)/shard_map/ppermute | solution.py:66
  (190 other events, 3995.7 us)
Sparse Core Ops, SparseCore 0:
  10.5 65.9 all-gather.9
  110.0 42.9 all-gather.11
  159.9 30.2 all-gather.13
  192.5 43.8 all-gather.7
  241.3 73.8 all-gather.15
  355.1 66.9 all-gather.17
  660.6 81.5 reduce-scatter.6
  781.5 103.3 reduce-scatter.8
  919.4 36.2 reduce-scatter.14
  959.4 41.3 reduce-scatter.10
  1004.9 59.6 reduce-scatter.12
  1066.9 54.6 all-gather.19
  1134.3 126.2 reduce-scatter.16
